TPU v7x, 32 devices: a whole 2x2x4 slice. The times are simulated.
32 devices in a mesh: seq: 8 (over z, y), wshard: 4 (over x, core).
Axes of the slice: x: 2, y: 2, z: 4, core: 2. Of those that a mesh axis runs over, the one named last changes fastest.
Arguments:
- block_in: bfloat16 [4, 8192, 1024], P('wshard', 'seq'), may hold values from -6 to 6
- norm_gain: float32 [1024], replicated, may hold values from 0.5 to 1.5
- in_weight: bfloat16 [1024, 4384], P('wshard'), may hold values from -0.1875 to 0.1875
- conv_x: float32 [4, 2048], P(None, 'seq'), may hold values from -3 to 3
- conv_x_bias: float32 [2048], P('seq'), may hold values from -3 to 3
- conv_bc: float32 [4, 256], replicated, may hold values from -3 to 3
- conv_bc_bias: float32 [256], replicated, may hold values from -3 to 3
- a_log: float32 [32], P('seq'), may hold values from -12 to 1
- skip: float32 [32], P('seq'), may hold values from -4 to 4
- dt_bias: float32 [32], P('seq'), may hold values from -5 to -2
- out_gain: float32 [2048], replicated, may hold values from 0.5 to 1.5
- out_weight: bfloat16 [2048, 1024], P('wshard'), may hold values from -0.125 to 0.125
- cotangent: bfloat16 [4, 8192, 1024], P('wshard', 'seq'), may hold values from -6 to 6
Outputs:
- output: bfloat16 [4, 8192, 1024], P('wshard', 'seq')
- input_grad: float32 [4, 8192, 1024], P('wshard', 'seq')
- norm_gain_grad: float32 [1024], replicated
- in_weight_grad: float32 [1024, 4384], P('wshard')
- conv_x_grad: float32 [4, 2048], P(None, 'seq')
- conv_x_bias_grad: float32 [2048], P('seq')
- conv_bc_grad: float32 [4, 256], replicated
- conv_bc_bias_grad: float32 [256], replicated
- a_log_grad: float32 [32], P('seq')
- skip_grad: float32 [32], P('seq')
- dt_bias_grad: float32 [32], P('seq')
- out_gain_grad: float32 [2048], replicated
- out_weight_grad: float32 [2048, 1024], P('wshard')
All inputs are finite; a program needn't handle non-finite values.
Results may differ from a plain program's by a relative error of at most 0.012.
The roundings to bfloat16 on the way count: a program that leaves them out, or rounds other values in their place, can miss the bound.
Values may be sent and summed in bfloat16 or wider, within the bound.
No kernel may reach another device: no remote copies, remote signals or barrier semaphores. Data moves between devices by JAX's collectives and lax.ppermute only.
A program may use at most 640 MiB of HBM per device.

v0:
```python
import jax
import jax.numpy as jnp
from jax import lax
from jax.sharding import PartitionSpec as P

STATE = 128
BLOCK = 256
INNER = 2048


epsilon = 1e-05
highest = lax.Precision.HIGHEST


def contract_rows(left, right):
    return lax.dot_general(
        left, right, (((0,), (0,)), ((), ())), preferred_element_type=jnp.float32
    )


def contract_cols(left, right):
    return lax.dot_general(
        left, right, (((1,), (1,)), ((), ())), preferred_element_type=jnp.float32
    )


def causal_conv(values, kernel, bias):
    taps = kernel.shape[0]
    length = values.shape[0]
    padded = jnp.concatenate([jnp.zeros((taps - 1, values.shape[1]), jnp.float32), values], axis=0)
    summed = jnp.zeros_like(values) + bias[None, :]
    for offset in range(taps):
        summed = summed + kernel[offset][None, :] * padded[offset : offset + length]
    return summed


def local_mixer(
    x_in, dt_in, bc_in, conv_x, conv_x_bias, conv_bc, conv_bc_bias, a_log, skip, dt_bias
):
    length = x_in.shape[0]
    head_count = dt_in.shape[1]
    head_dim = x_in.shape[1] // head_count
    blocks = length // BLOCK
    x_act = jax.nn.silu(causal_conv(x_in, conv_x, conv_x_bias))
    bc_act = jax.nn.silu(causal_conv(bc_in, conv_bc, conv_bc_bias))
    step_sizes = jax.nn.softplus(dt_in + dt_bias[None, :])
    log_decay = -jnp.exp(a_log)[None, :] * step_sizes
    x_blocks = x_act.reshape(blocks, BLOCK, head_count, head_dim)
    scaled = x_blocks * step_sizes.reshape(blocks, BLOCK, head_count, 1)
    cumulative = jnp.cumsum(log_decay.reshape(blocks, BLOCK, head_count), axis=1)
    b_blocks = bc_act[:, :STATE].reshape(blocks, BLOCK, STATE)
    c_blocks = bc_act[:, STATE:].reshape(blocks, BLOCK, STATE)
    positions = jnp.arange(BLOCK)
    lower_mask = positions[:, None] >= positions[None, :]
    differences = cumulative[:, :, None, :] - cumulative[:, None, :, :]
    weights = jnp.exp(jnp.where(lower_mask[None, :, :, None], differences, -jnp.inf))
    scores = jnp.einsum("ctn,csn->cts", c_blocks, b_blocks, precision=highest)
    within = jnp.einsum(
        "ctsh,cshp->cthp", scores[:, :, :, None] * weights, scaled, precision=highest
    )
    tail_decay = jnp.exp(cumulative[:, -1:, :] - cumulative)
    local_states = jnp.einsum(
        "csn,cshp->chpn", b_blocks, scaled * tail_decay[:, :, :, None], precision=highest
    )
    totals = cumulative[:, -1, :]
    running = jnp.cumsum(totals, axis=0)
    before = running - totals
    order = jnp.arange(blocks)
    earlier = order[:, None] > order[None, :]
    carry_weight = jnp.exp(
        jnp.where(earlier[:, :, None], before[:, None, :] - running[None, :, :], -jnp.inf)
    )
    entering = jnp.einsum("cdh,dhpn->chpn", carry_weight, local_states, precision=highest)
    carried = jnp.exp(cumulative)[:, :, :, None] * jnp.einsum(
        "ctn,chpn->cthp", c_blocks, entering, precision=highest
    )
    heads_view = (within + carried).reshape(length, head_count, head_dim)
    heads_view = heads_view + skip[None, :, None] * x_act.reshape(length, head_count, head_dim)
    return heads_view.reshape(length, head_count * head_dim)


def first_norm(values, gain):
    scale_first = lax.rsqrt(jnp.mean(values * values, axis=-1, keepdims=True) + epsilon)
    return values * scale_first * gain[None, :]


def gated_norm(values, gate_part, gain):
    gated = values * jax.nn.silu(gate_part)
    scale_second = lax.rsqrt(jnp.mean(gated * gated, axis=-1, keepdims=True) + epsilon)
    return gated * scale_second * gain[None, :]


def local(
    block_in,
    norm_gain,
    in_weight,
    conv_x,
    conv_x_bias,
    conv_bc,
    conv_bc_bias,
    a_log,
    skip,
    dt_bias,
    out_gain,
    out_weight,
    cotangent,
):
    tokens = block_in[0].astype(jnp.float32)
    full_in, full_out = (
        lax.all_gather(in_weight, "wshard", axis=0, tiled=True),
        lax.all_gather(out_weight, "wshard", axis=0, tiled=True),
    )
    normed_wide, norm_pull = jax.vjp(first_norm, tokens, norm_gain)
    normed = normed_wide.astype(jnp.bfloat16)
    projected = jnp.dot(normed, full_in, preferred_element_type=jnp.float32).astype(jnp.bfloat16)
    gate_part = projected[:, :INNER]
    x_raw = projected[:, INNER : 2 * INNER]
    bc_raw = projected[:, 2 * INNER : 2 * INNER + 2 * STATE]
    dt_raw = projected[:, 2 * INNER + 2 * STATE :]
    x_heads, dt_heads = (
        lax.all_to_all(x_raw, "seq", split_axis=1, concat_axis=0, tiled=True),
        lax.all_to_all(dt_raw, "seq", split_axis=1, concat_axis=0, tiled=True),
    )
    bc_whole = lax.all_gather(bc_raw, "seq", axis=0, tiled=True)
    mixed_wide, mixer_pull = jax.vjp(
        local_mixer,
        x_heads.astype(jnp.float32),
        dt_heads.astype(jnp.float32),
        bc_whole.astype(jnp.float32),
        conv_x,
        conv_x_bias,
        conv_bc,
        conv_bc_bias,
        a_log,
        skip,
        dt_bias,
    )
    mixed_heads = mixed_wide.astype(jnp.bfloat16)
    mixed_tokens = lax.all_to_all(mixed_heads, "seq", split_axis=0, concat_axis=1, tiled=True)
    normed_wide_out, out_pull = jax.vjp(
        gated_norm, mixed_tokens.astype(jnp.float32), gate_part.astype(jnp.float32), out_gain
    )
    normed_out = normed_wide_out.astype(jnp.bfloat16)
    branch = jnp.dot(normed_out, full_out, preferred_element_type=jnp.float32)
    output = (tokens + branch).astype(jnp.bfloat16)
    back_in, back_out = (full_in, full_out)
    grad_output = cotangent[0]
    out_weight_grad = contract_rows(normed_out, grad_output)
    grad_normed_out = contract_cols(grad_output, back_out)
    grad_mixed, grad_gate, out_gain_grad = out_pull(grad_normed_out)
    grad_heads = lax.all_to_all(
        grad_mixed.astype(jnp.bfloat16), "seq", split_axis=1, concat_axis=0, tiled=True
    )
    mixer_grads = mixer_pull(grad_heads.astype(jnp.float32))
    grad_x_tokens, grad_dt_tokens = (
        lax.all_to_all(
            mixer_grads[0].astype(jnp.bfloat16), "seq", split_axis=0, concat_axis=1, tiled=True
        ),
        lax.all_to_all(
            mixer_grads[1].astype(jnp.bfloat16), "seq", split_axis=0, concat_axis=1, tiled=True
        ),
    )
    grad_bc_tokens = lax.psum_scatter(
        mixer_grads[2], "seq", scatter_dimension=0, tiled=True
    ).astype(jnp.bfloat16)
    grad_projected = jnp.concatenate(
        [grad_gate.astype(jnp.bfloat16), grad_x_tokens, grad_bc_tokens, grad_dt_tokens], axis=1
    )
    in_weight_grad = contract_rows(normed, grad_projected)
    grad_normed = contract_cols(grad_projected, back_in)
    grad_tokens, norm_gain_grad = norm_pull(grad_normed)
    input_grad = grad_tokens + grad_output.astype(jnp.float32)
    in_total, out_total = lax.psum((in_weight_grad, out_weight_grad), "seq")
    in_owned, out_owned = (
        lax.psum_scatter(in_total, "wshard", scatter_dimension=0, tiled=True),
        lax.psum_scatter(out_total, "wshard", scatter_dimension=0, tiled=True),
    )
    conv_x_grad, conv_x_bias_grad, a_log_grad, skip_grad, dt_bias_grad = lax.psum(
        (mixer_grads[3], mixer_grads[4], mixer_grads[7], mixer_grads[8], mixer_grads[9]), "wshard"
    )
    norm_gain_sum, conv_bc_grad, conv_bc_bias_grad, out_gain_sum = lax.psum(
        (norm_gain_grad, mixer_grads[5], mixer_grads[6], out_gain_grad), ("seq", "wshard")
    )
    return (
        output[None],
        input_grad[None],
        norm_gain_sum,
        in_owned,
        conv_x_grad,
        conv_x_bias_grad,
        conv_bc_grad,
        conv_bc_bias_grad,
        a_log_grad,
        skip_grad,
        dt_bias_grad,
        out_gain_sum,
        out_owned,
    )


def solution(mesh):
    in_specs = (
        P("wshard", "seq", None),
        P(),
        P("wshard", None),
        P(None, "seq"),
        P("seq"),
        P(),
        P(),
        P("seq"),
        P("seq"),
        P("seq"),
        P(),
        P("wshard", None),
        P("wshard", "seq", None),
    )
    out_specs = (
        P("wshard", "seq", None),
        P("wshard", "seq", None),
        P(),
        P("wshard", None),
        P(None, "seq"),
        P("seq"),
        P(),
        P(),
        P("seq"),
        P("seq"),
        P("seq"),
        P(),
        P("wshard", None),
    )
    return jax.shard_map(local, mesh=mesh, in_specs=in_specs, out_specs=out_specs, check_vma=False)
```

profile of v0, /device:TPU:0, one launch (start us, length us, event | category | flops | bytes accessed | tf_op | source)
XLA Modules:
  0.0 1569.7 jit_solution(6266710726324763759)
XLA Ops:
  10.6 64.5 %all-gather.4.cloned.1.call-done = bf16[1024,4384]{0,1:T(8,128)(2,1)} async-done(((bf16[256,4384]{0,1:T(8,128)(2,1)}), bf16[1024,4384]{0,1:T(8,128)(2,1)}) %all-gather.4.cloned.1.call-update) | async-done | bytes 8978448 | tf_op jit(solution)/shard_map/all_gather | solution.py:110
  116.7 135.5 %all-to-all-done = bf16[1024,8,256]{0,2,1:T(8,128)(2,1)} async-done(((bf16[1024,8,256]{0,2,1:T(8,128)(2,1)}), bf16[1024,8,256]{0,2,1:T(8,128)(2,1)}, u32[]{:S(2)}, u32[]{:S(2)}) %all-to-all-start) | async-done | bytes 4194336 | tf_op jit(solution)/shard_map/all_to_all | solution.py:121
  266.1 21.9 %fusion.34 = (f32[8192,256]{0,1:T(8,128)}, f32[8192,256]{0,1:T(8,128)}) fusion(f32[8192,256]{0,1:T(8,128)} %convert_element_type.104, f32[256]{0:T(256)S(1)} %bitcast.317, f32[256]{0:T(256)S(1)} %bitcast.319, f32[256]{0:T(256)S(1)} %bitcast.315, f32[256]{0:T(256)S(1)} %bitcast.313, f32[256]{0:T(256)S(1)} %copy-done.68), kind=kLoop, calls=%fused_computation.81 | loop fusion | flops 25165824 | bytes 25170944 | tf_op jit(solution)/shard_map/jvp(jit(silu))/mul | solution.py:45
  320.5 22.3 %fusion.35 = (f32[8192,256]{0,1:T(8,128)}, f32[8192,256]{0,1:T(8,128)}) fusion(f32[8192,256]{0,1:T(8,128)} %bitcast.269, f32[256]{0:T(256)S(1)} %bitcast.309, f32[256]{0:T(256)S(1)} %bitcast.311, f32[256]{0:T(256)S(1)} %bitcast.307, f32[256]{0:T(256)S(1)} %bitcast.305, f32[256]{0:T(256)S(1)} %copy-done.69), kind=kLoop, calls=%fused_computation.84 | loop fusion | flops 25165824 | bytes 25170944 | tf_op jit(solution)/shard_map/jvp(jit(silu))/mul | solution.py:44
  393.6 44.4 %bitcast_add_fusion.1 = f32[32,256,4,64]{1,3,2,0:T(8,128)} fusion(f32[32,256,4,64]{1,3,2,0:T(8,128)} %fusion.68, f32[32,256,4]{1,2,0:T(4,128)S(1)} %copy.310, f32[32,256,4]{1,2,0:T(4,128)S(1)} %copy.308, f32[32,256,256]{2,1,0:T(8,128)} %fusion.158, pred[256,256]{1,0:T(8,128)(4,1)S(1)} %iota_compare_fusion, f32[32,256,4,64]{1,0,3,2:T(8,128)S(1)} %bitcast.263, ...), kind=kOutput, calls=%fused_computation.55 | convolution fusion | flops 6473908224 | bytes 34013184 | tf_op jit(solution)/shard_map/jvp(ctsh,cshp->cthp)/dot_general | solution.py:58
  471.6 91.6 %all-to-all-done.2 = bf16[8,1024,256]{1,2,0:T(8,128)(2,1)} async-done(((bf16[8,1024,256]{1,2,0:T(8,128)(2,1)}), bf16[8,1024,256]{1,2,0:T(8,128)(2,1)}, u32[]{:S(2)}, u32[]{:S(2)}) %all-to-all-start.2) | async-done | bytes 4194336 | tf_op jit(solution)/shard_map/all_to_all | solution.py:139
  570.5 14.9 multiply_reduce_fusion
  596.4 97.1 %all_to_all.93 = bf16[1024,8,256]{0,2,1:T(8,128)(2,1)S(1)} all-to-all(bf16[1024,8,256]{0,2,1:T(8,128)(2,1)S(1)} %bitcast.297), channel_id=1, replica_groups=mesh['seq'=8,'wshard'=4] {'seq'}, dimensions={1} | all-to-all | bytes 8388608 | tf_op jit(solution)/shard_map/all_to_all | solution.py:151
  707.5 15.5 fusion.85
  723.0 21.8 %fusion.20 = f32[32,256,128,1]{2,1,3,0:T(8,128)} fusion(f32[32,256,4]{1,2,0:T(4,128)S(1)} %copy.310, f32[32,4,64,128]{3,0,2,1:T(8,128)S(1)} %copy-done.4, bf16[32,256,4,64]{1,0,3,2:T(8,128)(2,1)S(1)} %copy-done.1), kind=kOutput, calls=%fused_computation.30 | convolution fusion | flops 3225419776 | bytes 12713984 | tf_op jit(solution)/shard_map/transpose(jvp(ctn,chpn->cthp))/dot_general | solution.py:74
  744.8 40.7 %fusion.9 = (f32[32,256,4]{1,2,0:T(4,128)S(1)}, f32[32,256,4]{1,2,0:T(4,128)S(1)}, f32[32,256,256]{2,1,0:T(8,128)}) fusion(f32[32,256,4]{1,2,0:T(4,128)S(1)} %copy.308, f32[32,256,256]{2,1,0:T(8,128)} %fusion.158, pred[256,256]{1,0:T(8,128)(4,1)S(1)} %iota_compare_fusion, f32[32,256,4,64]{1,0,3,2:T(8,128)S(1)} %bitcast.267, ...), kind=kOutput, calls=%fused_computation.10 | convolution fusion | flops 6517882880 | bytes 29949952 | tf_op jit(solution)/shard_map/transpose(jvp(ctsh,cshp->cthp))/dot_general | solution.py:58
  794.1 21.9 %fusion.36 = f32[32,256,128,1]{2,1,3,0:T(8,128)} fusion(f32[32,256,4,64]{1,0,3,2:T(8,128)S(1)} %bitcast.268, f32[32,256,4]{1,2,0:T(4,128)S(1)} %copy.311, f32[32,256,4]{1,2,0:T(4,128)S(1)} %get-tuple-element.52, f32[32,4,64,128]{3,0,2,1:T(8,128)S(1)} %fusion.82), kind=kOutput, calls=%fused_computation.87 | convolution fusion | flops 3225419776 | bytes 17039360 | tf_op jit(solution)/shard_map/transpose(jvp(csn,cshp->chpn))/dot_general | solution.py:62
  816.1 18.1 %bitcast_add_fusion.2 = f32[32,256,128]{2,1,0:T(8,128)} fusion(f32[32,256,128,1]{2,1,3,0:T(8,128)} %fusion.36, f32[32,256,256]{2,1,0:T(8,128)} %get-tuple-element.15, f32[32,256,128]{2,1,0:T(8,128)S(1)} %copy-done.9), kind=kOutput, calls=%fused_computation.108 | convolution fusion | flops 3222274048 | bytes 20971520 | tf_op jit(solution)/shard_map/transpose(jvp(ctn,csn->cts))/dot_general | solution.py:57
  854.6 21.0 %multiply_reduce_fusion.4 = (f32[256]{0:T(256)}, f32[256]{0:T(256)}, f32[256]{0:T(256)}, f32[256]{0:T(256)}, f32[256]{0:T(256)}, /*index=5*/f32[8192,256]{0,1:T(8,128)}) fusion(f32[8192,256]{0,1:T(8,128)} %convert_element_type.104, bf16[8192,256]{0,1:T(8,128)(2,1)} %all-gather.6.cloned.1.call-done, f32[8192,256]{0,1:T(8,128)} %get-tuple-element.56, ...), kind=kLoop, calls=%fused_computation.67 | loop fusion | flops 41941760 | bytes 37753856 | tf_op jit(solution)/shard_map/transpose(jvp())/reduce_sum | solution.py:33
  930.2 25.0 %fusion.4 = f32[32,4,64,256]{3,2,1,0:T(8,128)} fusion(f32[32,256,4]{1,2,0:T(4,128)S(1)} %copy.308, f32[32,256,256]{2,1,0:T(8,128)} %fusion.158, pred[256,256]{1,0:T(8,128)(4,1)S(1)} %iota_compare_fusion, bf16[32,256,4,64]{1,0,3,2:T(8,128)(2,1)S(1)} %copy-done.2), kind=kOutput, calls=%fused_computation.7 | convolution fusion | flops 6467616768 | bytes 21168128 | tf_op jit(solution)/shard_map/transpose(jvp(ctsh,cshp->cthp))/dot_general | solution.py:58
  955.8 24.7 %multiply_reduce_fusion.10 = (f32[32,256,4]{1,2,0:T(4,128)S(1)}, f32[32,256,4]{1,2,0:T(4,128)S(1)}, f32[32,256,4,64]{1,3,2,0:T(8,128)}) fusion(f32[32,256,4,64]{1,0,3,2:T(8,128)} %bitcast.264, f32[32,256,4]{1,2,0:T(4,128)S(1)} %get-tuple-element.52, f32[32,4,64,256]{3,2,1,0:T(8,128)} %fusion.4, f32[32,256,4]{1,2,0:T(4,128)S(1)} %copy.311, ...), kind=kOutput, calls=%fused_computation.73 | convolution fusion | flops 3237937152 | bytes 34078720 | tf_op jit(solution)/shard_map/transpose(jvp(csn,cshp->chpn))/dot_general | solution.py:62
  1031.1 14.4 multiply_reduce_fusion.9
  1056.9 15.2 fusion.33
  1082.3 91.6 %all-to-all-done.4 = bf16[8,1024,256]{1,2,0:T(8,128)(2,1)} async-done(((bf16[8,1024,256]{1,2,0:T(8,128)(2,1)}), bf16[8,1024,256]{1,2,0:T(8,128)(2,1)}, u32[]{:S(2)}, u32[]{:S(2)}) %all-to-all-start.4) | async-done | bytes 4194336 | tf_op jit(solution)/shard_map/all_to_all | solution.py:156
  1173.9 23.6 %fusion.91 = f32[1024,4384]{0,1:T(8,128)} fusion(bf16[1024,32]{0,1:T(8,128)(2,1)S(1)} %all_to_all.86, bf16[1024,256]{0,1:T(8,128)(2,1)S(1)} %convert_element_type.117, bf16[1024,2048]{0,1:T(8,128)(2,1)} %bitcast.38, bf16[1024,2048]{0,1:T(8,128)(2,1)} %get-tuple-element.57, bf16[1,1024,1024]{2,1,0:T(8,128)(2,1)S(1)} %copy-done.20, f32[1024]{0:T(1024)S(1)} %copy-done.60, ...), kind=kOutput, calls=%fused_computation.154 | convolution fusion | flops 9234022400 | bytes 29040640 | tf_op jit(solution)/shard_map/dot_general | solution.py:16
  1197.8 131.5 %reduce-scatter.6.cloned.1.call-done = f32[256,4384]{0,1:T(8,128)} async-done(((f32[1024,4384]{0,1:T(8,128)}), f32[256,4384]{0,1:T(8,128)}) %reduce-scatter.6.cloned.1.call-update) | async-done | bytes 4489232 | tf_op jit(solution)/shard_map/reduce_scatter | solution.py:175
  1347.6 16.7 %fusion.44 = (f32[1024]{0:T(1024)S(1)}, f32[1024]{0:T(1024)S(1)}, f32[1024,1024]{1,0:T(8,128)}) fusion(bf16[1,1024,1024]{2,1,0:T(8,128)(2,1)S(1)} %copy-done.20, f32[1024]{0:T(1024)S(1)} %copy-done.35, f32[1024]{0:T(1024)S(1)} %copy-done.60, bf16[1024,4384]{0,1:T(8,128)(2,1)} %all-gather.4.cloned.1.call-done, bf16[1024,32]{0,1:T(8,128)(2,1)S(1)} %all_to_all.86, ...), kind=kOutput, calls=%fused_computation.100 | convolution fusion | flops 9237166080 | bytes 24264704 | tf_op jit(solution)/shard_map/dot_general | solution.py:22
  1364.3 44.2 %all-reduce.22 = (f32[1024]{0:T(1024)}, f32[4,256]{1,0:T(4,128)}, f32[256]{0:T(256)}, f32[2048]{0:T(1024)}) all-reduce(f32[1024]{0:T(1024)S(1)} %get-tuple-element.30, f32[4,256]{1,0:T(4,128)S(1)} %pad_add_fusion.6, f32[256]{0:T(256)S(1)} %copy-done.61, f32[2048]{0:T(1024)S(1)} %copy-done.54), channel_id=1, replica_groups=mesh['seq'=8,'wshard'=4] {'seq','wshard'}, use_global_device_ids=true, to_apply=%region_21.22 | all-reduce | flops 4352 | bytes 34816 | tf_op jit(solution)/shard_map/psum | solution.py:181
  1413.4 142.8 %all-reduce.27.cloned.1.call-done = (f32[256,4384]{0,1:T(8,128)}, f32[512,1024]{1,0:T(8,128)}) async-done(((f32[256,4384]{0,1:T(8,128)}, f32[512,1024]{1,0:T(8,128)}), (f32[256,4384]{0,1:T(8,128)}, f32[512,1024]{1,0:T(8,128)})) %all-reduce.27.cloned.1.call-update) | async-done | bytes 6586384 | tf_op jit(solution)/shard_map/psum | solution.py:173
  (296 shorter events, 392.9 us)
Async XLA Ops:
  7.2 67.9 %all-gather.4.cloned.1.call-start = ((), (), s32[]{:S(2)}) async-start(), calls=%async_computation.9 | async-start | bytes 11223040 | tf_op jit(solution)/shard_map/all_gather | solution.py:110
  92.1 12.4 all-to-all-start.1
  104.5 147.7 %all-to-all-start = ((bf16[1024,8,256]{0,2,1:T(8,128)(2,1)}), bf16[1024,8,256]{0,2,1:T(8,128)(2,1)}, u32[]{:S(2)}, u32[]{:S(2)}) async-start(bf16[1024,8,256]{0,2,1:T(8,128)(2,1)} %bitcast.291), calls=%async_computation | async-start | bytes 8388608 | tf_op jit(solution)/shard_map/all_to_all | solution.py:121
  109.1 150.5 %all-gather.6.cloned.1.call-start = ((), (), s32[]{:S(2)}) async-start(), calls=%async_computation.10 | async-start | bytes 4718592 | tf_op jit(solution)/shard_map/all_gather | solution.py:124
  111.2 349.8 %copy-start.36 = (f32[256]{0:T(256)}, f32[256]{0:T(256)S(1)}, u32[]{:S(2)}) copy-start(f32[256]{0:T(256)S(1)} %mul.504) | copy-start | bytes 3076
  111.3 148.3 %copy-start.58 = (f32[4]{0:T(128)}, f32[4]{0:T(128)S(1)}, u32[]{:S(2)}) copy-start(f32[4]{0:T(128)S(1)} %exponential_negate_fusion) | copy-start | bytes 52
  111.3 209.1 %copy-start.38 = (f32[1,256]{1,0:T(1,128)}, f32[1,256]{1,0:T(1,128)S(1)}, u32[]{:S(2)}) copy-start(f32[1,256]{1,0:T(1,128)S(1)} %get-tuple-element.73) | copy-start | bytes 3076
  111.3 209.1 %copy-start.40 = (f32[1,256]{1,0:T(1,128)}, f32[1,256]{1,0:T(1,128)S(1)}, u32[]{:S(2)}) copy-start(f32[1,256]{1,0:T(1,128)S(1)} %get-tuple-element.74) | copy-start | bytes 3076
  111.3 209.1 %copy-start.42 = (f32[1,256]{1,0:T(1,128)}, f32[1,256]{1,0:T(1,128)S(1)}, u32[]{:S(2)}) copy-start(f32[1,256]{1,0:T(1,128)S(1)} %get-tuple-element.75) | copy-start | bytes 3076
  111.4 209.1 %copy-start.44 = (f32[1,256]{1,0:T(1,128)}, f32[1,256]{1,0:T(1,128)S(1)}, u32[]{:S(2)}) copy-start(f32[1,256]{1,0:T(1,128)S(1)} %get-tuple-element.76) | copy-start | bytes 3076
  111.4 154.7 %copy-start.46 = (f32[1,256]{1,0:T(1,128)}, f32[1,256]{1,0:T(1,128)S(1)}, u32[]{:S(2)}) copy-start(f32[1,256]{1,0:T(1,128)S(1)} %get-tuple-element.77) | copy-start | bytes 3076
  111.4 154.7 %copy-start.48 = (f32[1,256]{1,0:T(1,128)}, f32[1,256]{1,0:T(1,128)S(1)}, u32[]{:S(2)}) copy-start(f32[1,256]{1,0:T(1,128)S(1)} %get-tuple-element.78) | copy-start | bytes 3076
  111.4 154.7 %copy-start.50 = (f32[1,256]{1,0:T(1,128)}, f32[1,256]{1,0:T(1,128)S(1)}, u32[]{:S(2)}) copy-start(f32[1,256]{1,0:T(1,128)S(1)} %get-tuple-element.79) | copy-start | bytes 3076
  111.4 154.7 %copy-start.52 = (f32[1,256]{1,0:T(1,128)}, f32[1,256]{1,0:T(1,128)S(1)}, u32[]{:S(2)}) copy-start(f32[1,256]{1,0:T(1,128)S(1)} %get-tuple-element.80) | copy-start | bytes 3076
  115.0 144.6 %copy-start.21 = (f32[32,4,2,128]{3,0,1,2:T(8,128)}, f32[32,4,2,128]{3,0,1,2:T(8,128)S(1)}, u32[]{:S(2)}) copy-start(f32[32,4,2,128]{3,0,1,2:T(8,128)S(1)} %reduce-window.14) | copy-start | bytes 393220
  466.3 96.9 %all-to-all-start.2 = ((bf16[8,1024,256]{1,2,0:T(8,128)(2,1)}), bf16[8,1024,256]{1,2,0:T(8,128)(2,1)}, u32[]{:S(2)}, u32[]{:S(2)}) async-start(bf16[8,1024,256]{1,2,0:T(8,128)(2,1)} %bitcast.293), calls=%async_computation.2 | async-start | bytes 8388608 | tf_op jit(solution)/shard_map/all_to_all | solution.py:139
  470.8 99.6 %all-gather.8.cloned.1.call-start = ((), (), s32[]{:S(2)}) async-start(), calls=%async_computation.11 | async-start | bytes 5242880 | tf_op jit(solution)/shard_map/all_gather | solution.py:111
  471.6 609.4 %reduce-scatter.4.cloned.1.call-start = ((), (), s32[]{:S(2)}) async-start(), calls=%async_computation.12 | async-start | bytes 9437184 | tf_op jit(solution)/shard_map/reduce_scatter | solution.py:163
  900.5 297.3 %reduce-scatter.8.cloned.1.call-start = ((), (), s32[]{:S(2)}) async-start(), calls=%async_computation.14 | async-start | bytes 10485760 | tf_op jit(solution)/shard_map/reduce_scatter | solution.py:176
  1012.2 62.6 %all-to-all-start.5 = ((bf16[8,1024,4]{1,2,0:T(4,128)(2,1)}), bf16[8,1024,4]{1,2,0:T(4,128)(2,1)S(1)}, u32[]{:S(2)}, u32[]{:S(2)}) async-start(bf16[8,1024,4]{1,2,0:T(4,128)(2,1)} %fusion.113), calls=%async_computation.6 | async-start | bytes 131072 | tf_op jit(solution)/shard_map/all_to_all | solution.py:159
  1072.1 101.8 %copy-start.35 = (f32[1024]{0:T(1024)S(1)}, f32[1024]{0:T(1024)}, u32[]{:S(2)}) copy-start(f32[1024]{0:T(1024)} %copy-done.34) | copy-start | bytes 12292
  1074.7 99.1 %all-to-all-start.4 = ((bf16[8,1024,256]{1,2,0:T(8,128)(2,1)}), bf16[8,1024,256]{1,2,0:T(8,128)(2,1)}, u32[]{:S(2)}, u32[]{:S(2)}) async-start(bf16[8,1024,256]{1,2,0:T(8,128)(2,1)} %bitcast.292), calls=%async_computation.4 | async-start | bytes 8388608 | tf_op jit(solution)/shard_map/all_to_all | solution.py:156
  1080.9 248.4 %reduce-scatter.6.cloned.1.call-start = ((), (), s32[]{:S(2)}) async-start(), calls=%async_computation.13 | async-start | bytes 22446080 | tf_op jit(solution)/shard_map/reduce_scatter | solution.py:175
  1197.5 358.8 %all-reduce.27.cloned.1.call-start = ((), (), s32[]{:S(2)}) async-start(), calls=%async_computation.15 | async-start | bytes 13172736 | tf_op jit(solution)/shard_map/psum | solution.py:173
  (69 other events, 1329.4 us)
Sparse Core Ops, SparseCore 0:
  9.6 65.5 all-gather.3
  112.7 135.4 all-gather.5
  473.2 34.8 all-gather.7
  900.6 148.9 reduce-scatter.3
  1052.2 70.6 reduce-scatter.7
  1197.6 131.6 reduce-scatter.5
  1333.9 222.2 all-reduce.26
where the time goes:
time: 1580 us; the launch traced here: 1570 us
  waiting for transfers between devices  661 us (42%)
  matrix products  372 us (24%)
  other arithmetic  200 us (13%)
  local copies, waits for them, and re-layouts  148 us (9%)
  blocking collectives  148 us (9%)
  starting transfers between devices  25.4 us (2%)
    psum x1, waiting for transfers between devices, local(): in_total, out_total = lax.psum((in_weight_grad, out_weight_grad), 'seq')  143 us
    all_to_all x1, waiting for transfers between devices, local(): lax.all_to_all(x_raw, 'seq', split_axis=1, concat_axis=0, tiled=True)  136 us
    reduce_scatter x1, waiting for transfers between devices, local(): lax.psum_scatter(in_total, 'wshard', scatter_dimension=0, tiled=True)  132 us
    dot_general x3, matrix products, local_mixer(): jnp.einsum('ctsh,cshp->cthp', scores[:, :, :, None] * weights, scaled, pr...  110 us
    all_to_all x1, blocking collectives, local(): lax.all_to_all(grad_mixed.astype(jnp.bfloat16), 'seq', split_axis=1, conc...  97.1 us
    all_to_all x1, waiting for transfers between devices, local(): lax.all_to_all(mixer_grads[0].astype(jnp.bfloat16), 'seq', split_axis=0,...  91.6 us
    all_to_all x1, waiting for transfers between devices, local(): lax.all_to_all(mixed_heads, 'seq', split_axis=0, concat_axis=1, tiled=True)  91.6 us
    all_gather x1, waiting for transfers between devices, local(): lax.all_gather(in_weight, 'wshard', axis=0, tiled=True)  64.5 us
  transfers between devices with their start and end apart: 12, of which 7 were waited for; matrix products, arithmetic and copies ran while one was open for 16% of the time, Pallas kernels for 0%

commit v1 on v0

v1 whole, which is shorter than its diff:
```python
import functools

import jax
import jax.numpy as jnp
from jax import lax
from jax.experimental import pallas as pl
from jax.experimental.pallas import tpu as pltpu
from jax.sharding import PartitionSpec as P

INNER = 2048
STATE = 128
HEADS = 32
TAPS = 4
BC = 2 * STATE
CH = INNER + BC
XCOLS = 2432
XUSED = 2336
Q = 256
TILE = 256
TILES = INNER // TILE
PAIRS = HEADS // 2
EDGE = 16
EPS = 1e-05

f32 = jnp.float32
bf16 = jnp.bfloat16
highest = lax.Precision.HIGHEST


def cparams(megabytes=56):
    return pltpu.CompilerParams(
        dimension_semantics=("arbitrary",), vmem_limit_bytes=megabytes * 2**20
    )


def dot(a, b):
    return lax.dot_general(a, b, (((1,), (0,)), ((), ())), preferred_element_type=f32)


def dot_lanes(a, b):
    return lax.dot_general(a, b, (((1,), (1,)), ((), ())), preferred_element_type=f32)


def dot_rows(a, b):
    return lax.dot_general(a, b, (((0,), (0,)), ((), ())), preferred_element_type=f32)


def sigmoid(v):
    return 0.5 * jnp.tanh(0.5 * v) + 0.5


def lane_iota(rows, lanes):
    return lax.broadcasted_iota(jnp.int32, (rows, lanes), 1)


def row_iota(rows, lanes):
    return lax.broadcasted_iota(jnp.int32, (rows, lanes), 0)


def pair_of(cols, first):
    rows = cols.shape[0]
    low = lane_iota(rows, 128) < 64
    return jnp.where(low, cols[:, first : first + 1], cols[:, first + 1 : first + 2])


def four_of(cols, first):
    return jnp.concatenate([pair_of(cols, first), pair_of(cols, first + 2)], axis=1)


def split_dot(value, select):
    high = value.astype(bf16)
    low = (value - high.astype(f32)).astype(bf16)
    return dot(high, select) + dot(low, select)


def halves(value):
    high = value.astype(bf16)
    return high, (value - high.astype(f32)).astype(bf16)


def fine(product, a, b):
    a_high, a_low = halves(a)
    b_high, b_low = halves(b)
    return product(a_high, b_high) + (product(a_high, b_low) + product(a_low, b_high))


def head_select(tile):
    lanes = row_iota(TILE, 128) >> 6
    return jnp.where(lanes + tile * (TILE // 64) == lane_iota(TILE, 128), 1.0, 0.0).astype(bf16)


def shifted(current, before):
    joined = jnp.concatenate([before[EDGE - 8 :], current], axis=0)
    rows = current.shape[0]
    return [joined[5 + k : 5 + k + rows] for k in range(TAPS - 1)] + [current]


def conv_of(parts, taps, bias):
    total = bias + taps[0:1] * parts[0]
    for k in range(1, TAPS):
        total = total + taps[k : k + 1] * parts[k]
    return total


def conv_back(grad, after, taps):
    joined = jnp.concatenate([grad, after], axis=0)
    rows = grad.shape[0]
    total = taps[TAPS - 1 : TAPS] * grad
    for k in range(TAPS - 1):
        total = total + taps[k : k + 1] * joined[TAPS - 1 - k : TAPS - 1 - k + rows]
    return total


def tile_at(j, width=TILE):
    return pl.ds(pl.multiple_of(j * width, width), width)


def project_kernel(order, tokens, edge, gain, w0, w1, w2, w3, normed, out, out_edge, full):
    rows = w0.shape[0]

    def norm(values):
        wide = values.astype(f32)
        scale = lax.rsqrt(jnp.mean(wide * wide, axis=1, keepdims=True) + EPS)
        return (wide * scale * gain[...]).astype(bf16)

    @pl.when(pl.program_id(0) == 0)
    def _():
        for k, piece in enumerate((w0, w1, w2, w3)):
            full[pl.ds(pl.multiple_of(order[k] * rows, rows), rows), :] = piece[...]
        early = norm(edge[...])
        out_edge[...] = dot(early, full[...]).astype(bf16)

    now = norm(tokens[...])
    normed[...] = now
    for start in range(0, XCOLS, TILE):
        stop = min(start + TILE, XCOLS)
        out[:, start:stop] = dot(now, full[:, start:stop]).astype(bf16)


def project(order, tokens, edge, gain, pieces):
    length, width = tokens.shape
    rows = pieces[0].shape[0]
    whole = lambda shape: pl.BlockSpec(shape, lambda i, o: (0,) * len(shape), pipeline_mode=pl.Buffered(1))
    return pl.pallas_call(
        project_kernel,
        grid_spec=pltpu.PrefetchScalarGridSpec(
            num_scalar_prefetch=1,
            grid=(length // Q,),
            in_specs=[
                pl.BlockSpec((Q, width), lambda i, o: (i, 0)),
                whole((EDGE, width)),
                whole((1, width)),
            ]
            + [whole((rows, XCOLS))] * 4,
            out_specs=[
                pl.BlockSpec((Q, width), lambda i, o: (i, 0)),
                pl.BlockSpec((Q, XCOLS), lambda i, o: (i, 0)),
                pl.BlockSpec((EDGE, XCOLS), lambda i, o: (0, 0)),
            ],
            scratch_shapes=[pltpu.VMEM((4 * rows, XCOLS), bf16)],
        ),
        out_shape=[
            jax.ShapeDtypeStruct((length, width), bf16),
            jax.ShapeDtypeStruct((length, XCOLS), bf16),
            jax.ShapeDtypeStruct((EDGE, XCOLS), bf16),
        ],
        compiler_params=cparams(),
        cost_estimate=pl.CostEstimate(flops=2 * length * width * XCOLS, bytes_accessed=14 * 2**20, transcendentals=0),
        name="project",
    )(order, tokens, edge, gain, *pieces)


def gate_kernel(order, normed, w0, w1, w2, w3, out, full):
    rows = w0.shape[0]

    @pl.when(pl.program_id(0) == 0)
    def _():
        for k, piece in enumerate((w0, w1, w2, w3)):
            full[pl.ds(pl.multiple_of(order[k] * rows, rows), rows), :] = piece[...]

    for j in range(TILES):
        cols = slice(j * TILE, (j + 1) * TILE)
        out[:, cols] = dot(normed[...], full[:, cols]).astype(bf16)


def gate_project(order, normed, pieces):
    length, width = normed.shape
    rows = pieces[0].shape[0]
    return pl.pallas_call(
        gate_kernel,
        grid_spec=pltpu.PrefetchScalarGridSpec(
            num_scalar_prefetch=1,
            grid=(length // Q,),
            in_specs=[pl.BlockSpec((Q, width), lambda i, o: (i, 0))]
            + [pl.BlockSpec((rows, INNER), lambda i, o: (0, 0), pipeline_mode=pl.Buffered(1))] * 4,
            out_specs=pl.BlockSpec((Q, INNER), lambda i, o: (i, 0)),
            scratch_shapes=[pltpu.VMEM((4 * rows, INNER), bf16)],
        ),
        out_shape=jax.ShapeDtypeStruct((length, INNER), bf16),
        compiler_params=cparams(),
        cost_estimate=pl.CostEstimate(flops=2 * length * width * INNER, bytes_accessed=10 * 2**20, transcendentals=0),
        name="gate_project",
    )(order, normed, *pieces)


def states_kernel(
    now, prior, edge, taps, bias, taps_bc, bias_bc, heads,
    x_act, bc_act, aux_out, cum_t, local, payload,
    run, total, b_rows,
):
    c = pl.program_id(0)
    first = c == 0

    @pl.when(first)
    def _():
        run[...] = jnp.zeros_like(run)
        total[...] = jnp.zeros_like(total)

    def before(cols):
        return jnp.where(first, edge[:, cols], prior[:, cols]).astype(f32)

    band = slice(INNER, CH)
    parts = shifted(now[:, band].astype(f32), before(band))
    pre = conv_of(parts, taps_bc[...], bias_bc[...])
    act = pre * sigmoid(pre)
    bc_act[...] = act
    b_rows[...] = act[:, :STATE].T

    raw = now[:, CH : CH + HEADS].astype(f32) + heads[2:3, :HEADS]
    step = jnp.maximum(raw, 0.0) + jnp.log1p(jnp.exp(-jnp.abs(raw)))
    decay = -jnp.exp(heads[0:1, :HEADS]) * step
    lower = jnp.where(row_iota(Q, Q) >= lane_iota(Q, Q), 1.0, 0.0)
    cumulative = jnp.dot(lower, decay, precision=highest, preferred_element_type=f32)
    last = cumulative[Q - 1 : Q]
    aux = jnp.concatenate([cumulative, step, jnp.exp(last - cumulative), jnp.exp(cumulative)], axis=1)
    aux_out[...] = aux
    cum_t[...] = aux.T[:HEADS]

    def body(j, carry):
        cols = tile_at(j)
        x_parts = shifted(now[:, cols].astype(f32), before(cols))
        pre_x = conv_of(x_parts, taps[:, cols], bias[:, cols])
        x = pre_x * sigmoid(pre_x)
        x_act[:, cols] = x
        turned = pltpu.roll(aux, lax.rem(128 - 4 * j, 128), 1)
        state = fine(dot, b_rows[...], x * (four_of(turned, 32) * four_of(turned, 64)))
        local[0, j] = state
        end = turned[Q - 1 : Q]
        run[j] = four_of(end, 96) * run[j] + state
        total[:, cols] += four_of(end, 0)
        return carry

    lax.fori_loop(0, TILES, body, 0)

    @pl.when(c == pl.num_programs(0) - 1)
    def _():
        for j in range(TILES):
            payload[j, :STATE, :] = run[j]
            payload[j, STATE:, :] = jnp.broadcast_to(total[:, j * TILE : (j + 1) * TILE], (8, TILE))


def whole_spec(shape):
    return pl.BlockSpec(shape, lambda i: (0,) * len(shape), pipeline_mode=pl.Buffered(1))


def states(proj, proj_edge, taps, bias, taps_bc, bias_bc, heads):
    length = proj.shape[0]
    chunks = length // Q
    per = Q // EDGE
    return pl.pallas_call(
        states_kernel,
        grid=(chunks,),
        in_specs=[
            pl.BlockSpec((Q, XCOLS), lambda i: (i, 0)),
            pl.BlockSpec((EDGE, XCOLS), lambda i: (jnp.maximum(i * per - 1, 0), 0)),
            whole_spec((EDGE, XCOLS)),
            whole_spec((TAPS, INNER)),
            whole_spec((1, INNER)),
            whole_spec((TAPS, BC)),
            whole_spec((1, BC)),
            whole_spec((8, 128)),
        ],
        out_specs=[
            pl.BlockSpec((Q, INNER), lambda i: (i, 0)),
            pl.BlockSpec((Q, BC), lambda i: (i, 0)),
            pl.BlockSpec((Q, 128), lambda i: (i, 0)),
            pl.BlockSpec((HEADS, Q), lambda i: (0, i)),
            pl.BlockSpec((1, TILES, STATE, TILE), lambda i: (i, 0, 0, 0)),
            pl.BlockSpec((TILES, STATE + 8, TILE), lambda i: (0, 0, 0)),
        ],
        out_shape=[
            jax.ShapeDtypeStruct((length, INNER), f32),
            jax.ShapeDtypeStruct((length, BC), f32),
            jax.ShapeDtypeStruct((length, 128), f32),
            jax.ShapeDtypeStruct((HEADS, length), f32),
            jax.ShapeDtypeStruct((chunks, TILES, STATE, TILE), f32),
            jax.ShapeDtypeStruct((TILES, STATE + 8, TILE), f32),
        ],
        scratch_shapes=[
            pltpu.VMEM((TILES, STATE, TILE), f32),
            pltpu.VMEM((1, INNER), f32),
            pltpu.VMEM((STATE, Q), f32),
        ],
        compiler_params=cparams(),
        cost_estimate=pl.CostEstimate(flops=2 * 10**10, bytes_accessed=20 * 2**20, transcendentals=0),
        name="states",
    )(proj, proj, proj_edge, taps, bias, taps_bc, bias_bc, heads)


def chain_kernel(forward, values, totals, out):
    count = out.shape[0]
    order = range(count) if forward else range(count - 1, -1, -1)
    state = jnp.zeros(out.shape[1:], f32)
    for i in order:
        out[i] = state
        state = jnp.exp(totals[i, 0:1, :]) * state + values[i, :STATE, :]


def chain(forward, values, totals):
    count, _, width = values.shape
    return pl.pallas_call(
        functools.partial(chain_kernel, forward),
        out_shape=jax.ShapeDtypeStruct((count, STATE, width), f32),
        compiler_params=pltpu.CompilerParams(vmem_limit_bytes=56 * 2**20),
        name="chain",
    )(values, totals)


def within_kernel(x_act, bc_act, aux, cum_t, skip, out, scores):
    lower = row_iota(Q, Q) >= lane_iota(Q, Q)
    scores[...] = jnp.where(lower, fine(dot_lanes, bc_act[:, STATE:], bc_act[:, :STATE]), 0.0)
    low = lane_iota(Q, 128) < 64

    def body(p, carry):
        cols = tile_at(p, 128)
        turned = pltpu.roll(aux[...], lax.rem(128 - 2 * p, 128), 1)
        x = x_act[:, cols]
        u = x * pair_of(turned, 32)
        results = []
        for i in range(2):
            difference = turned[:, i : i + 1] - cum_t[pl.ds(2 * p + i, 1), :]
            weights = jnp.exp(jnp.minimum(difference, 0.0))
            results.append(fine(dot, weights * scores[...], u))
        out[:, cols] = jnp.where(low, results[0], results[1]) + skip[:, cols] * x
        return carry

    lax.fori_loop(0, PAIRS, body, 0)


def within(x_act, bc_act, aux, cum_t, skip):
    length = x_act.shape[0]
    return pl.pallas_call(
        within_kernel,
        grid=(length // Q,),
        in_specs=[
            pl.BlockSpec((Q, INNER), lambda i: (i, 0)),
            pl.BlockSpec((Q, BC), lambda i: (i, 0)),
            pl.BlockSpec((Q, 128), lambda i: (i, 0)),
            pl.BlockSpec((HEADS, Q), lambda i: (0, i)),
            whole_spec((1, INNER)),
        ],
        out_specs=pl.BlockSpec((Q, INNER), lambda i: (i, 0)),
        out_shape=jax.ShapeDtypeStruct((length, INNER), f32),
        scratch_shapes=[pltpu.VMEM((Q, Q), f32)],
        compiler_params=cparams(),
        cost_estimate=pl.CostEstimate(flops=2 * 10**10, bytes_accessed=20 * 2**20, transcendentals=0),
        name="within",
    )(x_act, bc_act, aux, cum_t, skip)


def within_back_kernel(x_act, bc_act, aux, cum_t, dy, out, out_bc, scores, grad_scores):
    act = bc_act[...].astype(bf16)
    upper = row_iota(Q, Q) <= lane_iota(Q, Q)
    scores[...] = jnp.where(upper, dot_lanes(act[:, :STATE], act[:, STATE:]), 0.0)
    grad_scores[...] = jnp.zeros_like(grad_scores)
    low = lane_iota(Q, 128) < 64

    def body(p, carry):
        cols = tile_at(p, 128)
        turned = pltpu.roll(aux[...], lax.rem(128 - 2 * p, 128), 1)
        u = x_act[:, cols] * pair_of(turned, 32)
        grad = dy[:, cols]
        results = []
        for i in range(2):
            difference = cum_t[pl.ds(2 * p + i, 1), :] - turned[:, i : i + 1]
            weights = jnp.exp(jnp.minimum(difference, 0.0))
            mine = jnp.where(low if i == 0 else ~low, u, 0.0).astype(bf16)
            grad_scores[...] += weights * dot_lanes(mine, grad)
            results.append(dot((weights * scores[...]).astype(bf16), grad))
        out[:, cols] = jnp.where(low, results[0], results[1])
        return carry

    lax.fori_loop(0, PAIRS, body, 0)
    masked = jnp.where(upper, grad_scores[...], 0.0).astype(bf16)
    out_bc[:, :STATE] = dot(masked, act[:, STATE:])
    out_bc[:, STATE:] = dot_rows(masked, act[:, :STATE])


def within_back(x_act, bc_act, aux, cum_t, dy):
    length = x_act.shape[0]
    return pl.pallas_call(
        within_back_kernel,
        grid=(length // Q,),
        in_specs=[
            pl.BlockSpec((Q, INNER), lambda i: (i, 0)),
            pl.BlockSpec((Q, BC), lambda i: (i, 0)),
            pl.BlockSpec((Q, 128), lambda i: (i, 0)),
            pl.BlockSpec((HEADS, Q), lambda i: (0, i)),
            pl.BlockSpec((Q, INNER), lambda i: (i, 0)),
        ],
        out_specs=[
            pl.BlockSpec((Q, INNER), lambda i: (i, 0)),
            pl.BlockSpec((Q, BC), lambda i: (i, 0)),
        ],
        out_shape=[
            jax.ShapeDtypeStruct((length, INNER), f32),
            jax.ShapeDtypeStruct((length, BC), f32),
        ],
        scratch_shapes=[pltpu.VMEM((Q, Q), f32), pltpu.VMEM((Q, Q), f32)],
        compiler_params=cparams(),
        cost_estimate=pl.CostEstimate(flops=3 * 10**10, bytes_accessed=24 * 2**20, transcendentals=0),
        name="within_back",
    )(x_act, bc_act, aux, cum_t, dy)


def middle_kernel(
    order, y_in, bc_act, aux, local, entering, gate, tokens, cot, gain, w0, w1, w2, w3,
    normed_out, output, dy_out, grad_gate, ends, back_states, payload, y_dot, gain_grad,
    full, state, back, before, y_keep, gated_keep, grad_keep,
):
    c = pl.program_id(0)
    rows = w0.shape[0]

    @pl.when(c == 0)
    def _():
        for k, piece in enumerate((w0, w1, w2, w3)):
            full[pl.ds(pl.multiple_of(order[k] * rows, rows), rows), :] = piece[...]
        state[...] = entering[...]
        back[...] = jnp.zeros_like(back)
        before[...] = jnp.zeros_like(before)
        gain_grad[...] = jnp.zeros_like(gain_grad)

    keep = aux[...]
    c_cols = bc_act[:, STATE:]
    c_rows = bc_act[:, STATE:].T

    def turn(j):
        return pltpu.roll(keep, lax.rem(128 - 4 * j, 128), 1)

    def mix(j, squares):
        cols = tile_at(j)
        turned = turn(j)
        carried = fine(dot, c_cols, state[j])
        y = y_in[:, cols] + four_of(turned, 96) * carried
        y_keep[:, cols] = y
        raw = gate[:, cols].astype(f32)
        gated = y.astype(bf16).astype(f32) * (raw * sigmoid(raw))
        gated_keep[:, cols] = gated
        moved = four_of(turned[Q - 1 : Q], 96) * state[j] + local[0, j]
        state[j] = moved
        ends[0, j] = moved
        both = gated * gated
        return squares + (both[:, :128] + both[:, 128:])

    squares = lax.fori_loop(0, TILES, mix, jnp.zeros((Q, 128), f32))
    scale = lax.rsqrt(jnp.sum(squares, axis=1, keepdims=True) / INNER + EPS)

    def back_out(j, products):
        cols = tile_at(j)
        gated = gated_keep[:, cols]
        gains = gain[:, cols]
        normed_out[:, cols] = (gated * scale * gains).astype(bf16)
        grad = dot_lanes(cot[...], full[cols, :])
        grad_keep[:, cols] = grad
        gain_grad[:, cols] += jnp.sum(grad * gated * scale, axis=0, keepdims=True)
        both = grad * gains * gated
        return products + (both[:, :128] + both[:, 128:])

    products = lax.fori_loop(0, TILES, back_out, jnp.zeros((Q, 128), f32))
    shared = jnp.sum(products, axis=1, keepdims=True) / INNER * (scale * scale * scale)
    for start in range(0, output.shape[1], TILE):
        cols = slice(start, start + TILE)
        branch = dot(normed_out[...], full[:, cols])
        output[:, cols] = (tokens[:, cols].astype(f32) + branch).astype(bf16)

    def finish(j, y_sum):
        cols = tile_at(j)
        turned = turn(j)
        raw = gate[:, cols].astype(f32)
        sig = sigmoid(raw)
        grad_gated = scale * (grad_keep[:, cols] * gain[:, cols]) - gated_keep[:, cols] * shared
        y = y_keep[:, cols]
        dy = (grad_gated * (raw * sig)).astype(bf16)
        dy_out[:, cols] = dy
        mixed = y.astype(bf16).astype(f32)
        grad_gate[:, cols] = (grad_gated * mixed * (sig * (1.0 + raw * (1.0 - sig)))).astype(bf16)
        wide = dy.astype(f32)
        piece = fine(dot, c_rows, wide * four_of(turned, 96))
        back_states[0, j] = piece
        back[j] += jnp.exp(before[:, cols]) * piece
        before[:, cols] += four_of(turned[Q - 1 : Q], 0)
        return y_sum + split_dot(wide * y, head_select(j))

    y_dot[...] = lax.fori_loop(0, TILES, finish, jnp.zeros((Q, 128), f32))

    @pl.when(c == pl.num_programs(0) - 1)
    def _():
        payload[...] = back[...]


def middle(order, y_in, bc_act, aux, local, entering, gate, tokens, cot, gain, pieces):
    length, width = tokens.shape
    rows = pieces[0].shape[0]
    chunks = length // Q
    block = lambda cols: pl.BlockSpec((Q, cols), lambda i, o: (i, 0))
    whole = lambda shape: pl.BlockSpec(shape, lambda i, o: (0,) * len(shape), pipeline_mode=pl.Buffered(1))
    per_chunk = pl.BlockSpec((1, TILES, STATE, TILE), lambda i, o: (i, 0, 0, 0))
    return pl.pallas_call(
        middle_kernel,
        grid_spec=pltpu.PrefetchScalarGridSpec(
            num_scalar_prefetch=1,
            grid=(chunks,),
            in_specs=[
                block(INNER),
                block(BC),
                block(128),
                per_chunk,
                whole((TILES, STATE, TILE)),
                block(INNER),
                block(width),
                block(width),
                whole((1, INNER)),
            ]
            + [whole((rows, width))] * 4,
            out_specs=[
                block(INNER),
                block(width),
                block(INNER),
                block(INNER),
                per_chunk,
                per_chunk,
                pl.BlockSpec((TILES, STATE, TILE), lambda i, o: (0, 0, 0)),
                block(128),
                pl.BlockSpec((1, INNER), lambda i, o: (0, 0)),
            ],
            scratch_shapes=[
                pltpu.VMEM((4 * rows, width), bf16),
                pltpu.VMEM((TILES, STATE, TILE), f32),
                pltpu.VMEM((TILES, STATE, TILE), f32),
                pltpu.VMEM((1, INNER), f32),
                pltpu.VMEM((Q, INNER), f32),
                pltpu.VMEM((Q, INNER), f32),
                pltpu.VMEM((Q, INNER), f32),
            ],
        ),
        out_shape=[
            jax.ShapeDtypeStruct((length, INNER), bf16),
            jax.ShapeDtypeStruct((length, width), bf16),
            jax.ShapeDtypeStruct((length, INNER), bf16),
            jax.ShapeDtypeStruct((length, INNER), bf16),
            jax.ShapeDtypeStruct((chunks, TILES, STATE, TILE), f32),
            jax.ShapeDtypeStruct((chunks, TILES, STATE, TILE), f32),
            jax.ShapeDtypeStruct((TILES, STATE, TILE), f32),
            jax.ShapeDtypeStruct((length, 128), f32),
            jax.ShapeDtypeStruct((1, INNER), f32),
        ],
        compiler_params=cparams(),
        cost_estimate=pl.CostEstimate(flops=4 * 10**10, bytes_accessed=40 * 2**20, transcendentals=0),
        name="middle",
    )(order, y_in, bc_act, aux, local, entering, gate, tokens, cot, gain, *pieces)


def back_kernel(
    now, prior, edge, taps, bias, taps_bc, bias_bc, heads, skip,
    dy, du_in, bc_act, bc_in, aux, y_dot, ends_before, ends_now, entering, back_states, leaving,
    grad, grad_taps, grad_taps_bc, grad_heads, tail, start,
    later, after, x_dot, k_dot, edge_dot, b_sum, c_sum,
):
    step_id = pl.program_id(0)
    c = pl.num_programs(0) - 1 - step_id
    first = c == 0

    @pl.when(step_id == 0)
    def _():
        later[...] = leaving[...]
        after[...] = jnp.zeros_like(after)
        grad_taps[...] = jnp.zeros_like(grad_taps)
        grad_taps_bc[...] = jnp.zeros_like(grad_taps_bc)
        grad_heads[...] = jnp.zeros_like(grad_heads)

    def before(cols):
        return jnp.where(first, edge[:, cols], prior[:, cols]).astype(f32)

    keep = aux[...]
    act = bc_act[...].astype(bf16)
    x_dot[...] = jnp.zeros_like(x_dot)
    k_dot[...] = jnp.zeros_like(k_dot)
    edge_dot[...] = jnp.zeros_like(edge_dot)
    b_sum[...] = bc_in[:, :STATE]
    c_sum[...] = bc_in[:, STATE:]

    def through(cols, dv, parts, tap_values):
        sums = [jnp.sum(dv * part, axis=0, keepdims=True) for part in parts]
        sums.append(jnp.sum(dv, axis=0, keepdims=True))
        result = conv_back(dv, after[:, cols], tap_values)
        after[:, cols] = dv[:8]
        grad[:, cols] = result.astype(bf16)

        @pl.when(step_id == 0)
        def _():
            tail[:, cols] = result[Q - EDGE :]

        return jnp.concatenate(sums + [jnp.zeros((3, sums[0].shape[1]), f32)], axis=0)

    def body(j, carry):
        cols = tile_at(j)
        turned = pltpu.roll(keep, lax.rem(128 - 4 * j, 128), 1)
        step = four_of(turned, 32)
        tail_decay = four_of(turned, 64)
        parts = shifted(now[:, cols].astype(f32), before(cols))
        tap_values = taps[:, cols]
        pre = conv_of(parts, tap_values, bias[:, cols])
        sig = sigmoid(pre)
        x = pre * sig
        wide = dy[:, cols].astype(f32)
        later_state = later[j]
        later_low = later_state.astype(bf16)
        du = du_in[:, cols] + tail_decay * dot(act[:, :STATE], later_low)
        select = head_select(j)
        x_dot[...] += split_dot(x * du, select)
        k_dot[...] += split_dot(x * wide, select)
        enter = jnp.where(first, entering[j], ends_before[0, j])
        b_sum[...] += fine(dot_lanes, x * step * tail_decay, later_state)
        c_sum[...] += fine(dot_lanes, wide * four_of(turned, 96), enter)
        meet = jnp.sum(ends_now[0, j] * later_state, axis=0, keepdims=True)
        edge_dot[...] += split_dot(jnp.broadcast_to(meet, (8, TILE)), select)
        later[j] = four_of(turned[Q - 1 : Q], 96) * later_state + back_states[0, j]
        dx = step * du + skip[:, cols] * wide
        dv = dx * (sig * (1.0 + pre * (1.0 - sig)))
        grad_taps[:, cols] += through(cols, dv, parts, tap_values)
        return carry

    lax.fori_loop(0, TILES, body, 0)

    band = slice(INNER, CH)
    parts = shifted(now[:, band].astype(f32), before(band))
    pre = conv_of(parts, taps_bc[...], bias_bc[...])
    sig = sigmoid(pre)
    grad_act = jnp.concatenate([b_sum[...], c_sum[...]], axis=1)
    dv = grad_act * (sig * (1.0 + pre * (1.0 - sig)))
    grad_taps_bc[...] += through(band, dv, parts, taps_bc[...])

    step = keep[:, HEADS : 2 * HEADS]
    by_step = x_dot[:, :HEADS]
    by_skip = k_dot[:, :HEADS]
    rate = -jnp.exp(heads[0:1, :HEADS])
    by_sum = y_dot[:, :HEADS] - heads[1:2, :HEADS] * by_skip - step * by_step
    upper = jnp.where(row_iota(Q, Q) <= lane_iota(Q, Q), 1.0, 0.0)
    by_decay = jnp.dot(upper, by_sum, precision=highest, preferred_element_type=f32) + edge_dot[0:1, :HEADS]
    raw = now[:, CH : CH + HEADS].astype(f32) + heads[2:3, :HEADS]
    grad_dt = (by_step + by_decay * rate) * sigmoid(raw)
    full_dt = jnp.concatenate([grad_dt, jnp.zeros((Q, 128 - HEADS), f32)], axis=1)
    grad[:, CH:] = full_dt.astype(bf16)
    sums = [
        jnp.sum(by_decay * (rate * step), axis=0, keepdims=True),
        jnp.sum(by_skip, axis=0, keepdims=True),
        jnp.sum(grad_dt, axis=0, keepdims=True),
        jnp.zeros((5, HEADS), f32),
    ]
    grad_heads[:, :HEADS] += jnp.concatenate(sums, axis=0)

    @pl.when(first)
    def _():
        start[...] = after[...]


def backward(
    proj, proj_edge, taps, bias, taps_bc, bias_bc, heads, skip,
    dy, du, bc_act, grad_bc, aux, y_dot, ends, entering, back_states, leaving,
):
    length = proj.shape[0]
    chunks = length // Q
    per = Q // EDGE
    at = lambda i: chunks - 1 - i
    block = lambda cols: pl.BlockSpec((Q, cols), lambda i: (at(i), 0))
    per_chunk = pl.BlockSpec((1, TILES, STATE, TILE), lambda i: (at(i), 0, 0, 0))
    return pl.pallas_call(
        back_kernel,
        grid=(chunks,),
        in_specs=[
            block(XCOLS),
            pl.BlockSpec((EDGE, XCOLS), lambda i: (jnp.maximum(at(i) * per - 1, 0), 0)),
            whole_spec((EDGE, XCOLS)),
            whole_spec((TAPS, INNER)),
            whole_spec((1, INNER)),
            whole_spec((TAPS, BC)),
            whole_spec((1, BC)),
            whole_spec((8, 128)),
            whole_spec((1, INNER)),
            block(INNER),
            block(INNER),
            block(BC),
            block(BC),
            block(128),
            block(128),
            pl.BlockSpec((1, TILES, STATE, TILE), lambda i: (jnp.maximum(at(i) - 1, 0), 0, 0, 0)),
            per_chunk,
            whole_spec((TILES, STATE, TILE)),
            per_chunk,
            whole_spec((TILES, STATE, TILE)),
        ],
        out_specs=[
            block(XCOLS),
            pl.BlockSpec((8, INNER), lambda i: (0, 0)),
            pl.BlockSpec((8, BC), lambda i: (0, 0)),
            pl.BlockSpec((8, 128), lambda i: (0, 0)),
            pl.BlockSpec((EDGE, CH), lambda i: (0, 0)),
            pl.BlockSpec((8, CH), lambda i: (0, 0)),
        ],
        out_shape=[
            jax.ShapeDtypeStruct((length, XCOLS), bf16),
            jax.ShapeDtypeStruct((8, INNER), f32),
            jax.ShapeDtypeStruct((8, BC), f32),
            jax.ShapeDtypeStruct((8, 128), f32),
            jax.ShapeDtypeStruct((EDGE, CH), f32),
            jax.ShapeDtypeStruct((8, CH), f32),
        ],
        scratch_shapes=[
            pltpu.VMEM((TILES, STATE, TILE), f32),
            pltpu.VMEM((8, CH), f32),
            pltpu.VMEM((Q, 128), f32),
            pltpu.VMEM((Q, 128), f32),
            pltpu.VMEM((8, 128), f32),
            pltpu.VMEM((Q, STATE), f32),
            pltpu.VMEM((Q, STATE), f32),
        ],
        compiler_params=cparams(),
        cost_estimate=pl.CostEstimate(flops=4 * 10**10, bytes_accessed=40 * 2**20, transcendentals=0),
        name="backward",
    )(
        proj, proj, proj_edge, taps, bias, taps_bc, bias_bc, heads, skip,
        dy, du, bc_act, grad_bc, aux, y_dot, ends, ends, entering, back_states, leaving,
    )


def input_kernel(order, grad_gate, grad_x, tokens, cot, gain, g0, g1, g2, g3, x0, x1, x2, x3, out, gain_grad):
    rows = g0.shape[0]

    @pl.when(pl.program_id(0) == 0)
    def _():
        gain_grad[...] = jnp.zeros_like(gain_grad)

    for k, (gate_w, x_w) in enumerate(((g0, x0), (g1, x1), (g2, x2), (g3, x3))):
        cols = pl.ds(pl.multiple_of(order[k] * rows, rows), rows)
        out[:, cols] = dot_lanes(grad_gate[...], gate_w[...]) + dot_lanes(grad_x[...], x_w[...])
    grad = out[...]
    wide = tokens[...].astype(f32)
    width = wide.shape[1]
    scale = lax.rsqrt(jnp.mean(wide * wide, axis=1, keepdims=True) + EPS)
    gain_grad[...] += jnp.sum(grad * wide * scale, axis=0, keepdims=True)
    scaled = grad * gain[...]
    shared = jnp.sum(scaled * wide, axis=1, keepdims=True) / width
    out[...] = cot[...].astype(f32) + (scale * scaled - wide * (scale * scale * scale * shared))


def input_back(order, grad_gate, grad_x, tokens, cot, gain, gate_pieces, x_pieces):
    length, width = tokens.shape
    rows = gate_pieces[0].shape[0]
    block = lambda cols: pl.BlockSpec((Q, cols), lambda i, o: (i, 0))
    whole = lambda shape: pl.BlockSpec(shape, lambda i, o: (0,) * len(shape), pipeline_mode=pl.Buffered(1))
    return pl.pallas_call(
        input_kernel,
        grid_spec=pltpu.PrefetchScalarGridSpec(
            num_scalar_prefetch=1,
            grid=(length // Q,),
            in_specs=[block(INNER), block(XCOLS), block(width), block(width), whole((1, width))]
            + [whole((rows, INNER))] * 4
            + [whole((rows, XCOLS))] * 4,
            out_specs=[block(width), pl.BlockSpec((1, width), lambda i, o: (0, 0))],
        ),
        out_shape=[
            jax.ShapeDtypeStruct((length, width), f32),
            jax.ShapeDtypeStruct((1, width), f32),
        ],
        compiler_params=cparams(),
        cost_estimate=pl.CostEstimate(flops=2 * length * width * (INNER + XCOLS), bytes_accessed=20 * 2**20, transcendentals=0),
        name="input_back",
    )(order, grad_gate, grad_x, tokens, cot, gain, *gate_pieces, *x_pieces)


def swap(value, axis, bit):
    count = lax.axis_size(axis)
    return lax.ppermute(value, axis, [(i, i ^ bit) for i in range(count)])


def gather_pieces(piece):
    across = swap(piece, "wshard", 2)
    beside = swap(piece, "wshard", 1)
    return piece, beside, across, swap(across, "wshard", 1)


def exchange(value, axis):
    return lax.all_to_all(value, axis, split_axis=0, concat_axis=0, tiled=True)


def to_owners(value, count):
    if count == TILES:
        return value
    rows = value.shape[1]
    width = INNER // count
    lanes = value.reshape(TILES, rows, TILE // width, width)
    return lanes.transpose(0, 2, 1, 3).reshape(count, rows, width)


def from_owners(value):
    count, rows, width = value.shape
    if count == TILES:
        return value
    lanes = value.reshape(TILES, TILE // width, rows, width)
    return lanes.transpose(0, 2, 1, 3).reshape(TILES, rows, TILE)


def sum_to_rows(partial):
    rows = partial.shape[0] // 4
    cols = partial.shape[1]
    me = lax.axis_index("wshard")
    blocks = [
        lax.dynamic_slice_in_dim(partial, (me ^ k) * rows, rows, axis=0) for k in range(4)
    ]
    sent = jnp.stack([blocks[1], blocks[3]]).astype(bf16)
    got = swap(sent, "wshard", 1).astype(f32)
    mine = blocks[0] + got[0]
    other = (blocks[2] + got[1]).astype(bf16)
    mine = mine + swap(other, "wshard", 2).astype(f32)
    count = lax.axis_size("seq")
    place = lax.axis_index("seq")
    half = rows // 2
    group = count // 2
    bit = place & 1
    theirs = lax.dynamic_slice_in_dim(mine, (1 - bit) * half, half, axis=0).astype(bf16)
    kept = lax.dynamic_slice_in_dim(mine, bit * half, half, axis=0)
    kept = kept + swap(theirs, "seq", 1).astype(f32)
    groups = [[2 * i + b for i in range(group)] for b in range(2)]
    spread = lambda v: lax.all_to_all(
        v, "seq", split_axis=0, concat_axis=0, tiled=True, axis_index_groups=groups
    )
    parts = spread(kept.astype(bf16).reshape(group, half // group, cols))
    owned = jnp.sum(parts.astype(f32), axis=0).astype(bf16)
    full_half = spread(jnp.broadcast_to(owned[None], (group,) + owned.shape)).reshape(half, cols)
    other_half = swap(full_half, "seq", 1)
    first = jnp.where(bit == 0, full_half, other_half)
    second = jnp.where(bit == 0, other_half, full_half)
    return jnp.concatenate([first, second], axis=0).astype(f32)


def local(
    block_in, norm_gain, in_weight, conv_x, conv_x_bias, conv_bc, conv_bc_bias,
    a_log, skip, dt_bias, out_gain, out_weight, cotangent,
):
    tokens = block_in[0]
    cot = cotangent[0]
    length, width = tokens.shape
    seq = lax.axis_size("seq")
    shards = lax.axis_size("wshard")
    own_heads = HEADS // seq
    own_ch = INNER // seq
    me = lax.axis_index("wshard")
    order = jnp.stack([me ^ k for k in range(4)]).astype(jnp.int32)

    x_piece = jnp.pad(in_weight[:, INNER:], ((0, 0), (0, XCOLS - XUSED)))
    edge = lax.ppermute(tokens[length - EDGE :], "seq", [(i, i + 1) for i in range(seq - 1)])
    small = jnp.concatenate(
        [
            conv_x,
            conv_x_bias[None],
            jnp.pad(jnp.stack([a_log, skip, dt_bias]), ((0, 0), (0, own_ch - own_heads))),
        ],
        axis=0,
    )
    small_all = exchange(jnp.broadcast_to(small[None], (seq,) + small.shape), "seq")
    x_pieces = gather_pieces(x_piece)
    x_params = small_all[:, :5].transpose(1, 0, 2).reshape(5, INNER)
    head_params = small_all[:, 5:, :own_heads].transpose(1, 0, 2).reshape(3, HEADS)
    taps, bias = x_params[:4], x_params[4:5]
    heads = jnp.pad(head_params, ((0, 5), (0, 128 - HEADS)))
    skip_row = jnp.repeat(head_params[1], INNER // HEADS)[None]

    normed, proj, proj_edge = project(order, tokens, edge, norm_gain[None], x_pieces)
    gate_pieces = gather_pieces(in_weight[:, :INNER])
    out_pieces = gather_pieces(out_weight)
    x_act, bc_act, aux, cum_t, chunk_states, payload = states(
        proj, proj_edge, taps, bias, conv_bc, conv_bc_bias[None], heads
    )
    arrived = exchange(to_owners(payload, seq), "seq")
    gate = gate_project(order, normed, gate_pieces)
    y_within = within(x_act, bc_act, aux, cum_t, skip_row)
    totals = arrived[:, STATE:, :]
    entering = from_owners(exchange(chain(True, arrived, totals), "seq"))
    normed_out, output, dy, grad_gate, ends, back_states, back_payload, y_dot, out_gain_grad = middle(
        order, y_within, bc_act, aux, chunk_states, entering, gate, tokens, cot, out_gain[None], out_pieces
    )
    back_arrived = exchange(to_owners(back_payload, seq), "seq")
    du, grad_bc = within_back(x_act, bc_act, aux, cum_t, dy)
    out_weight_grad = dot_rows(normed_out, cot)
    gate_weight_grad = dot_rows(normed, grad_gate)
    leaving = from_owners(exchange(chain(False, back_arrived, totals), "seq"))
    grad_x, grad_taps, grad_taps_bc, grad_heads, tail, start = backward(
        proj, proj_edge, taps, bias, conv_bc, conv_bc_bias[None], heads, skip_row,
        dy, du, bc_act, grad_bc, aux, y_dot, ends, entering, back_states, leaving,
    )
    out_owned = sum_to_rows(out_weight_grad)
    gate_owned = sum_to_rows(gate_weight_grad)
    after = lax.ppermute(start, "seq", [(i, i - 1) for i in range(1, seq)])
    all_taps = jnp.concatenate([taps, conv_bc], axis=1)
    fixes = [
        tail[EDGE - 3 + a] + sum(all_taps[k] * after[a - k] for k in range(a + 1)) for a in range(3)
    ]
    fixed = jnp.concatenate([tail[: EDGE - 3], jnp.stack(fixes)], axis=0).astype(bf16)
    grad_x = lax.dynamic_update_slice(grad_x, fixed, (length - EDGE, 0))
    x_weight_grad = dot_rows(normed, grad_x)
    x_owned = sum_to_rows(x_weight_grad)
    input_grad, norm_gain_grad = input_back(
        order, grad_gate, grad_x, tokens, cot, norm_gain[None], gate_pieces, x_pieces
    )

    shared = jnp.concatenate(
        [norm_gain_grad[0], out_gain_grad[0], grad_taps_bc[:5].reshape(-1)]
    )
    mine = jnp.concatenate(
        [
            grad_taps[:5].reshape(5, seq, own_ch).transpose(1, 0, 2).reshape(seq, 5 * own_ch),
            grad_heads[:3, :HEADS].reshape(3, seq, own_heads).transpose(1, 0, 2).reshape(seq, 3 * own_heads),
        ],
        axis=1,
    )
    shared_size, mine_size = shared.shape[0], mine.shape[1]
    pad = -(shared_size + mine_size) % 1024
    small_out = jnp.concatenate(
        [jnp.broadcast_to(shared[None], (seq, shared_size)), mine, jnp.zeros((seq, pad), f32)], axis=1
    )
    small_out = jnp.broadcast_to(small_out[:, None], (seq, shards, small_out.shape[1]))
    small_sum = jnp.sum(
        exchange(small_out.reshape(seq * shards, 8, -1), ("seq", "wshard")), axis=0
    ).reshape(-1)
    in_owned = jnp.concatenate([gate_owned, x_owned[:, :XUSED]], axis=1)
    pos = [0]

    def take(shape):
        size = 1
        for extent in shape:
            size *= extent
        out = small_sum[pos[0] : pos[0] + size].reshape(shape)
        pos[0] += size
        return out

    norm_gain_sum = take((width,))
    out_gain_sum = take((INNER,))
    bc_sum = take((5, BC))
    x_sum = take((5, own_ch))
    head_sum = take((3, own_heads))
    return (
        output[None],
        input_grad[None],
        norm_gain_sum,
        in_owned,
        x_sum[:4],
        x_sum[4],
        bc_sum[:4],
        bc_sum[4],
        head_sum[0],
        head_sum[1],
        head_sum[2],
        out_gain_sum,
        out_owned,
    )


def solution(mesh):
    in_specs = (
        P("wshard", "seq", None),
        P(),
        P("wshard", None),
        P(None, "seq"),
        P("seq"),
        P(),
        P(),
        P("seq"),
        P("seq"),
        P("seq"),
        P(),
        P("wshard", None),
        P("wshard", "seq", None),
    )
    out_specs = (
        P("wshard", "seq", None),
        P("wshard", "seq", None),
        P(),
        P("wshard", None),
        P(None, "seq"),
        P("seq"),
        P(),
        P(),
        P("seq"),
        P("seq"),
        P("seq"),
        P(),
        P("wshard", None),
    )
    return jax.shard_map(local, mesh=mesh, in_specs=in_specs, out_specs=out_specs, check_vma=False)
```

time: 1580 us -> 648 us (0.41)
  waiting for transfers between devices: 661 us -> 182 us
  matrix products: 372 us -> 20.8 us
  Pallas kernels: 0 us -> 277 us
  other arithmetic: 200 us -> 42.5 us
  blocking collectives: 148 us -> 0 us
  local copies, waits for them, and re-layouts: 148 us -> 39.3 us
  starting transfers between devices: 25.4 us -> 78 us
    dot_general x21 -> x3, matrix products: 372 us -> 20.8 us  [dot_rows(): lax.dot_general(a, b, (((0,), (0,)), ((), ())), preferred_element_type=f32)]
    pallas_call x0 -> x10, Pallas kernels: none -> 277 us  [the longest x1 61.6 us: backward(): pl.pallas_call(back_kernel, grid=(chunks,), in_specs=[block(XCOLS), pl.Bl...]
    all_to_all x5 -> x12, waiting for transfers between devices: 321 us -> 61.3 us  [the longest x6 48.2 us: sum_to_rows(): lax.all_to_all(v, 'seq', split_axis=0, concat_axis=0, tiled=True, axis_in...]
    psum x1 -> x0, waiting for transfers between devices: 143 us -> none  [local(): in_total, out_total = lax.psum((in_weight_grad, out_weight_grad), 'seq')]
    reduce_scatter x3 -> x0, waiting for transfers between devices: 132 us -> none  [the longest x1 132 us: local(): lax.psum_scatter(in_total, 'wshard', scatter_dimension=0, tiled=True)]
    ppermute x0 -> x23, waiting for transfers between devices: none -> 120 us  [the longest x21 118 us: swap(): return lax.ppermute(value, axis, [(i, i ^ bit) for i in range(count)])]
    all_to_all x1 -> x0, blocking collectives: 97.1 us -> none  [local(): lax.all_to_all(grad_mixed.astype(jnp.bfloat16), 'seq', split_axis=1, conc...]
    mul x5 -> x0, other arithmetic: 66.9 us -> none  [the longest x2 22.7 us: causal_conv(): summed = summed + kernel[offset][None, :] * padded[offset:offset + length]]
  transfers between devices with their start and end apart: 12 -> 35, of which waited for: 7 -> 16; matrix products, arithmetic and copies ran while one was open for 16% -> 11% of each run, Pallas kernels for 0% -> 27%
where the time goes in v1:
time: 648 us; the launch traced here: 641 us
  Pallas kernels  277 us (43%)
  waiting for transfers between devices  182 us (28%)
  starting transfers between devices  78 us (12%)
  other arithmetic  42.5 us (7%)
  local copies, waits for them, and re-layouts  39.3 us (6%)
  matrix products  20.8 us (3%)
    ppermute x21, waiting for transfers between devices, swap(): return lax.ppermute(value, axis, [(i, i ^ bit) for i in range(count)])  118 us
    pallas_call x1, Pallas kernels, backward(): pl.pallas_call(back_kernel, grid=(chunks,), in_specs=[block(XCOLS), pl.Bl...  61.6 us
    pallas_call x1, Pallas kernels, middle(): pl.pallas_call(middle_kernel, grid_spec=pltpu.PrefetchScalarGridSpec(num_...  58.5 us
    all_to_all x6, waiting for transfers between devices, sum_to_rows(): lax.all_to_all(v, 'seq', split_axis=0, concat_axis=0, tiled=True, axis_in...  48.2 us
    pallas_call x1, Pallas kernels, within(): pl.pallas_call(within_kernel, grid=(length // Q,), in_specs=[pl.BlockSpec...  43.9 us
    pallas_call x1, Pallas kernels, within_back(): pl.pallas_call(within_back_kernel, grid=(length // Q,), in_specs=[pl.Bloc...  36.5 us
    pallas_call x1, Pallas kernels, states(): pl.pallas_call(states_kernel, grid=(chunks,), in_specs=[pl.BlockSpec((Q,...  31.4 us
    all_to_all x6, starting transfers between devices, exchange(): return lax.all_to_all(value, axis, split_axis=0, concat_axis=0, tiled=True)  28.8 us
  transfers between devices with their start and end apart: 35, of which 16 were waited for; matrix products, arithmetic and copies ran while one was open for 11% of the time, Pallas kernels for 27%

profile of v1, /device:TPU:0, one launch (start us, length us, event | category | flops | bytes accessed | tf_op | source)
XLA Modules:
  0.0 641.2 jit_solution(4754286269973296900)
XLA Ops:
  5.9 27.5 %collective-permute-done.2.w2.x2 = bf16[256,2432]{1,0:T(8,128)(2,1)} collective-permute-done((bf16[256,2432]{1,0:T(8,128)(2,1)S(1)}, bf16[256,2432]{1,0:T(8,128)(2,1)}, u32[]{:S(2)}, u32[]{:S(2)}) %collective-permute-start.2) | collective-permute-done | bytes 1245216 | tf_op jit(solution)/shard_map/ppermute | solution.py:793
  34.1 6.1 all-to-all-start
  49.6 12.1 %project.1 = (bf16[1024,1024]{1,0:T(8,128)(2,1)}, bf16[1024,2432]{1,0:T(8,128)(2,1)}, bf16[16,2432]{1,0:T(8,128)(2,1)}) custom-call(s32[4]{0:T(128)} %pad_add_fusion.order, bf16[1024,1024]{1,0:T(8,128)(2,1)} %bitcast.119, bf16[16,1024]{1,0:T(8,128)(2,1)} %copy-done.30, f32[1,1024]{1,0:T(1,128)} %bitcast.128, bf16[256,2432]{1,0:T(8,128)(2,1)} %copy-done.11, ...), custom_call_target="tpu_custom_call" | custom-call | flops 5100273664 | bytes 14680064 | tf_op jit(solution)/shard_map/project/pallas_call | solution.py:144
  61.8 31.4 %states.1 = (f32[1024,2048]{1,0:T(8,128)}, f32[1024,256]{1,0:T(8,128)}, f32[1024,128]{1,0:T(8,128)}, f32[32,1024]{1,0:T(8,128)}, f32[4,8,128,256]{3,2,1,0:T(8,128)}, /*index=5*/f32[8,136,256]{2,1,0:T(8,128)}) custom-call(bf16[1024,2432]{1,0:T(8,128)(2,1)} %get-tuple-element.41.now.prior, bf16[1024,2432]{1,0:T(8,128)(2,1)} %get-tuple-element.41.now.prior, ...), custom_call_target="tpu_custom_call" | custom-call | flops 20000000000 | bytes 20971520 | tf_op jit(solution)/shard_map/states/pallas_call | solution.py:270
  101.1 22.8 %collective-permute-done.5.w2.g2 = bf16[256,2048]{1,0:T(8,128)(2,1)} collective-permute-done((bf16[256,2048]{1,0:T(8,128)(2,1)S(1)}, bf16[256,2048]{1,0:T(8,128)(2,1)}, u32[]{:S(2)}, u32[]{:S(2)}) %collective-permute-start.5) | collective-permute-done | bytes 1048608 | tf_op jit(solution)/shard_map/ppermute | solution.py:793
  123.9 20.4 %collective-permute-done.8.w2 = bf16[512,1024]{1,0:T(8,128)(2,1)} collective-permute-done((bf16[512,1024]{1,0:T(8,128)(2,1)}, bf16[512,1024]{1,0:T(8,128)(2,1)}, u32[]{:S(2)}, u32[]{:S(2)}) %collective-permute-start.8) | collective-permute-done | bytes 1048608 | tf_op jit(solution)/shard_map/ppermute | solution.py:793
  147.6 6.2 all-to-all-start.2
  153.8 43.9 %within.1.y_in = f32[1024,2048]{1,0:T(8,128)} custom-call(f32[1024,2048]{1,0:T(8,128)} %get-tuple-element.43.x_act, f32[1024,256]{1,0:T(8,128)} %get-tuple-element.44.bc_act, f32[1024,128]{1,0:T(8,128)} %get-tuple-element.45.aux, f32[32,1024]{1,0:T(8,128)} %get-tuple-element.46.cum_t, f32[1,2048]{1,0:T(1,128)} %broadcast_in_dim_reshape.3.skip), custom_call_target="tpu_custom_call" | custom-call | flops 20000000000 | bytes 20971520 | tf_op jit(solution)/shard_map/within/pallas_call | solution.py:352
  197.7 9.5 %gate_project.1.gate = bf16[1024,2048]{1,0:T(8,128)(2,1)} custom-call(s32[4]{0:T(128)} %pad_add_fusion.order, bf16[1024,1024]{1,0:T(8,128)(2,1)} %get-tuple-element.49.normed, bf16[256,2048]{1,0:T(8,128)(2,1)} %copy-done.12, bf16[256,2048]{1,0:T(8,128)(2,1)} %collective-permute-done.4.w1.g1, bf16[256,2048]{1,0:T(8,128)(2,1)} %collective-permute-done.5.w2.g2, ...), custom_call_target="tpu_custom_call" | custom-call | flops 4294967296 | bytes 10485760 | tf_op jit(solution)/shard_map/gate_project/pallas_call | solution.py:189
  208.3 58.5 %middle.1 = (bf16[1024,2048]{1,0:T(8,128)(2,1)}, bf16[1024,1024]{1,0:T(8,128)(2,1)}, bf16[1024,2048]{1,0:T(8,128)(2,1)}, bf16[1024,2048]{1,0:T(8,128)(2,1)}, f32...) custom-call(s32[4]{0:T(128)} %pad_add_fusion.order, ...), custom_call_target="tpu_custom_call" | custom-call | flops 40000000000 | bytes 41943040 | tf_op jit(solution)/shard_map/middle/pallas_call | solution.py:518
  266.8 9.0 %fusion.23 = f32[2048,1024]{1,0:T(8,128)} fusion(bf16[1024,2048]{1,0:T(8,128)(2,1)} %get-tuple-element.68, bf16[1,1024,1024]{2,1,0:T(8,128)(2,1)S(1)} %copy-done.29), kind=kOutput, calls=%fused_computation.72 | convolution fusion | flops 4294967296 | bytes 14680064 | tf_op jit(solution)/shard_map/dot_general | solution.py:45
  275.8 6.2 all-to-all-start.3
  296.3 11.5 %all-to-all-done.3.values = f32[8,128,256]{2,1,0:T(8,128)S(1)} async-done(((f32[8,128,256]{2,1,0:T(8,128)}), f32[8,128,256]{2,1,0:T(8,128)S(1)}, u32[]{:S(2)}, u32[]{:S(2)}) %all-to-all-start.3) | async-done | bytes 1048608 | tf_op jit(solution)/shard_map/all_to_all | solution.py:803
  314.8 36.5 %within_back.1 = (f32[1024,2048]{1,0:T(8,128)}, f32[1024,256]{1,0:T(8,128)}) custom-call(f32[1024,2048]{1,0:T(8,128)} %get-tuple-element.43.x_act, f32[1024,256]{1,0:T(8,128)} %get-tuple-element.44.bc_act, f32[1024,128]{1,0:T(8,128)} %get-tuple-element.45.aux, f32[32,1024]{1,0:T(8,128)} %get-tuple-element.46.cum_t, bf16[1024,2048]{1,0:T(8,128)(2,1)} %get-tuple-element.52.dy), custom_call_target="tpu_custom_call" | custom-call | flops 30000001024 | bytes 25165824 | tf_op jit(solution)/shard_map/within_back/pallas_call | solution.py:401
  361.9 61.6 %backward.1 = (bf16[1024,2432]{1,0:T(8,128)(2,1)}, f32[8,2048]{1,0:T(8,128)}, f32[8,256]{1,0:T(8,128)}, f32[8,128]{1,0:T(8,128)}, f32[16,2304]{1,0:T(8,128)}, /*index=5*/f32[8,2304]{1,0:T(8,128)}) custom-call(bf16[1024,2432]{1,0:T(8,128)(2,1)} %get-tuple-element.41.now.prior, bf16[1024,2432]{1,0:T(8,128)(2,1)} %get-tuple-element.41.now.prior, ...), custom_call_target="tpu_custom_call" | custom-call | flops 40000000000 | bytes 41943040 | tf_op jit(solution)/shard_map/backward/pallas_call | solution.py:687
  432.7 7.2 %fusion.29 = f32[1024,2432]{1,0:T(8,128)S(1)} fusion(bf16[1024,1024]{1,0:T(8,128)(2,1)} %get-tuple-element.49.normed, bf16[1024,2432]{1,0:T(8,128)(2,1)S(1)} %maximum_dynamic-update-slice_fusion.grad_x), kind=kOutput, calls=%fused_computation.78 | convolution fusion | flops 5100273664 | bytes 17039360 | tf_op jit(solution)/shard_map/dot_general | solution.py:45
  457.5 7.0 %collective-permute-done.21 = bf16[256,1024]{1,0:T(8,128)(2,1)S(1)} collective-permute-done((bf16[256,1024]{1,0:T(8,128)(2,1)S(1)}, bf16[256,1024]{1,0:T(8,128)(2,1)S(1)}, u32[]{:S(2)}, u32[]{:S(2)}) %collective-permute-start.21) | collective-permute-done | bytes 524320 | tf_op jit(solution)/shard_map/ppermute | solution.py:793
  492.3 8.7 %all-to-all-done.6 = bf16[4,32,2048]{2,1,0:T(8,128)(2,1)S(1)} async-done(((bf16[4,32,2048]{2,1,0:T(8,128)(2,1)}), bf16[4,32,2048]{2,1,0:T(8,128)(2,1)S(1)}, u32[]{:S(2)}, u32[]{:S(2)}) %all-to-all-start.6) | async-done | bytes 524320 | tf_op jit(solution)/shard_map/all_to_all | solution.py:844
  505.6 19.2 %input_back.1 = (f32[1024,1024]{1,0:T(8,128)}, f32[1,1024]{1,0:T(1,128)}) custom-call(s32[4]{0:T(128)} %pad_add_fusion.order, bf16[1024,2048]{1,0:T(8,128)(2,1)} %get-tuple-element.51.grad_gate, bf16[1024,2432]{1,0:T(8,128)(2,1)} %copy-done.28, bf16[1024,1024]{1,0:T(8,128)(2,1)} %bitcast.121, bf16[1024,1024]{1,0:T(8,128)(2,1)} %bitcast.126, ...), custom_call_target="tpu_custom_call" | custom-call | flops 9395240960 | bytes 20971520 | tf_op jit(solution)/shard_map/input_back/pallas_call | solution.py:771
  536.3 10.3 %all-to-all-done.7 = bf16[4,32,2048]{2,1,0:T(8,128)(2,1)S(1)} async-done(((bf16[4,32,2048]{2,1,0:T(8,128)(2,1)}), bf16[4,32,2048]{2,1,0:T(8,128)(2,1)S(1)}, u32[]{:S(2)}, u32[]{:S(2)}) %all-to-all-start.7) | async-done | bytes 524320 | tf_op jit(solution)/shard_map/all_to_all | solution.py:844
  552.1 22.7 %collective-permute-done.17 = bf16[128,2432]{1,0:T(8,128)(2,1)S(1)} collective-permute-done((bf16[128,2432]{1,0:T(8,128)(2,1)S(1)}, bf16[128,2432]{1,0:T(8,128)(2,1)S(1)}, u32[]{:S(2)}, u32[]{:S(2)}) %collective-permute-start.17) | collective-permute-done | bytes 622624 | tf_op jit(solution)/shard_map/ppermute | solution.py:793
  582.6 14.4 %all-to-all-done.8 = bf16[4,32,2432]{2,1,0:T(8,128)(2,1)S(1)} async-done(((bf16[4,32,2432]{2,1,0:T(8,128)(2,1)}), bf16[4,32,2432]{2,1,0:T(8,128)(2,1)S(1)}, u32[]{:S(2)}, u32[]{:S(2)}) %all-to-all-start.8) | async-done | bytes 622624 | tf_op jit(solution)/shard_map/all_to_all | solution.py:844
  605.6 11.9 %all-to-all-done.9 = bf16[4,32,2432]{2,1,0:T(8,128)(2,1)S(1)} async-done(((bf16[4,32,2432]{2,1,0:T(8,128)(2,1)}), bf16[4,32,2432]{2,1,0:T(8,128)(2,1)S(1)}, u32[]{:S(2)}, u32[]{:S(2)}) %all-to-all-start.9) | async-done | bytes 622624 | tf_op jit(solution)/shard_map/all_to_all | solution.py:844
  621.1 11.4 %collective-permute-done.18 = bf16[128,2432]{1,0:T(8,128)(2,1)S(1)} collective-permute-done((bf16[128,2432]{1,0:T(8,128)(2,1)S(1)}, bf16[128,2432]{1,0:T(8,128)(2,1)S(1)}, u32[]{:S(2)}, u32[]{:S(2)}) %collective-permute-start.18) | collective-permute-done | bytes 622624 | tf_op jit(solution)/shard_map/ppermute | solution.py:793
  (206 shorter events, 163.7 us)
Async XLA Ops:
  2.9 30.5 %collective-permute-start.2 = (bf16[256,2432]{1,0:T(8,128)(2,1)S(1)}, bf16[256,2432]{1,0:T(8,128)(2,1)}, u32[]{:S(2)}, u32[]{:S(2)}) collective-permute-start(bf16[256,2432]{1,0:T(8,128)(2,1)S(1)} %pad.12.w0.x0), channel_id=1, source_target_pairs={{0,2},{1,3},{2,0},{3,1},{4,6},{5,7},{6,4},{7,5},{8,10},{9,11},{10,... | collective-permute-start | bytes 3735560 | tf_op jit(solution)/shard_map/ppermute | solution.py:793
  5.9 43.1 %collective-permute-start.1 = (bf16[256,2432]{1,0:T(8,128)(2,1)S(1)}, bf16[256,2432]{1,0:T(8,128)(2,1)}, u32[]{:S(2)}, u32[]{:S(2)}) collective-permute-start(bf16[256,2432]{1,0:T(8,128)(2,1)S(1)} %pad.12.w0.x0), channel_id=1, source_target_pairs={{0,1},{1,0},{2,3},{3,2},{4,5},{5,4},{6,7},{7,6},{8,9},{9,8},{10,11... | collective-permute-start | bytes 3735560 | tf_op jit(solution)/shard_map/ppermute | solution.py:793
  93.2 51.2 %all-to-all-start.1 = ((f32[8,136,256]{2,1,0:T(8,128)}), f32[8,136,256]{2,1,0:T(8,128)S(1)}, u32[]{:S(2)}, u32[]{:S(2)}) async-start(f32[8,136,256]{2,1,0:T(8,128)} %get-tuple-element.48), calls=%async_computation.1 | async-start | bytes 2228224 | tf_op jit(solution)/shard_map/all_to_all | solution.py:803
  97.7 26.3 %collective-permute-start.5 = (bf16[256,2048]{1,0:T(8,128)(2,1)S(1)}, bf16[256,2048]{1,0:T(8,128)(2,1)}, u32[]{:S(2)}, u32[]{:S(2)}) collective-permute-start(bf16[256,2048]{1,0:T(8,128)(2,1)S(1)} %copy.50.w0.g0), channel_id=1, source_target_pairs={{0,2},{1,3},{2,0},{3,1},{4,6},{5,7},{6,4},{7,5},{8,10},{9,11},{10,... | collective-permute-start | bytes 3145736 | tf_op jit(solution)/shard_map/ppermute | solution.py:793
  99.2 45.1 %collective-permute-start.8 = (bf16[512,1024]{1,0:T(8,128)(2,1)}, bf16[512,1024]{1,0:T(8,128)(2,1)}, u32[]{:S(2)}, u32[]{:S(2)}) collective-permute-start(bf16[512,1024]{1,0:T(8,128)(2,1)} %w0.1), channel_id=1, source_target_pairs={{0,2},{1,3},{2,0},{3,1},{4,6},{5,7},{6,4},{7,5},{8,10},{9,11},{10,... | collective-permute-start | bytes 3145736 | tf_op jit(solution)/shard_map/ppermute | solution.py:793
  99.8 98.0 %collective-permute-start.4 = (bf16[256,2048]{1,0:T(8,128)(2,1)S(1)}, bf16[256,2048]{1,0:T(8,128)(2,1)}, u32[]{:S(2)}, u32[]{:S(2)}) collective-permute-start(bf16[256,2048]{1,0:T(8,128)(2,1)S(1)} %copy.50.w0.g0), channel_id=1, source_target_pairs={{0,1},{1,0},{2,3},{3,2},{4,5},{5,4},{6,7},{7,6},{8,9},{9,8},{10,11... | collective-permute-start | bytes 3145736 | tf_op jit(solution)/shard_map/ppermute | solution.py:793
  99.8 107.5 %collective-permute-start.7 = (bf16[512,1024]{1,0:T(8,128)(2,1)}, bf16[512,1024]{1,0:T(8,128)(2,1)}, u32[]{:S(2)}, u32[]{:S(2)}) collective-permute-start(bf16[512,1024]{1,0:T(8,128)(2,1)} %w0.1), channel_id=1, source_target_pairs={{0,1},{1,0},{2,3},{3,2},{4,5},{5,4},{6,7},{7,6},{8,9},{9,8},{10,11... | collective-permute-start | bytes 3145736 | tf_op jit(solution)/shard_map/ppermute | solution.py:793
  123.9 73.8 %collective-permute-start.6 = (bf16[256,2048]{1,0:T(8,128)(2,1)}, bf16[256,2048]{1,0:T(8,128)(2,1)}, u32[]{:S(2)}, u32[]{:S(2)}) collective-permute-start(bf16[256,2048]{1,0:T(8,128)(2,1)} %collective-permute-done.5.w2.g2), channel_id=1, source_target_pairs={{0,1},{1,0},{2,3},{3,2},{4,5},{5,4},{6,7},{7,6},{8,9},{9,8},{10,11... | collective-permute-start | bytes 3145736 | tf_op jit(solution)/shard_map/ppermute | solution.py:793
  144.3 63.0 %collective-permute-start.9 = (bf16[512,1024]{1,0:T(8,128)(2,1)}, bf16[512,1024]{1,0:T(8,128)(2,1)}, u32[]{:S(2)}, u32[]{:S(2)}) collective-permute-start(bf16[512,1024]{1,0:T(8,128)(2,1)} %collective-permute-done.8.w2), channel_id=1, source_target_pairs={{0,1},{1,0},{2,3},{3,2},{4,5},{5,4},{6,7},{7,6},{8,9},{9,8},{10,11... | collective-permute-start | bytes 3145736 | tf_op jit(solution)/shard_map/ppermute | solution.py:793
  147.6 59.6 %all-to-all-start.2 = ((f32[8,128,256]{2,1,0:T(8,128)}), f32[8,128,256]{2,1,0:T(8,128)S(1)}, u32[]{:S(2)}, u32[]{:S(2)}) async-start(f32[8,128,256]{2,1,0:T(8,128)} %chain.2), calls=%async_computation.2 | async-start | bytes 2097152 | tf_op jit(solution)/shard_map/all_to_all | solution.py:803
  275.8 32.0 %all-to-all-start.3 = ((f32[8,128,256]{2,1,0:T(8,128)}), f32[8,128,256]{2,1,0:T(8,128)S(1)}, u32[]{:S(2)}, u32[]{:S(2)}) async-start(f32[8,128,256]{2,1,0:T(8,128)} %get-tuple-element.58), calls=%async_computation.3 | async-start | bytes 2097152 | tf_op jit(solution)/shard_map/all_to_all | solution.py:803
  286.3 65.0 %collective-permute-start.19 = (bf16[2,512,1024]{2,1,0:T(8,128)(2,1)}, bf16[2,512,1024]{2,1,0:T(8,128)(2,1)S(1)}, u32[]{:S(2)}, u32[]{:S(2)}) collective-permute-start(bf16[2,512,1024]{2,1,0:T(8,128)(2,1)} %pad_maximum_fusion.3), channel_id=1, source_target_pairs={{0,1},{1,0},{2,3},{3,2},{4,5},{5,4},{6,7},{7,6},{8,9},{9,8},{10,11... | collective-permute-start | bytes 6291464 | tf_op jit(solution)/shard_map/ppermute | solution.py:793
  296.3 60.4 %collective-permute-start.11 = (bf16[2,256,2048]{2,1,0:T(8,128)(2,1)}, bf16[2,256,2048]{2,1,0:T(8,128)(2,1)}, u32[]{:S(2)}, u32[]{:S(2)}) collective-permute-start(bf16[2,256,2048]{2,1,0:T(8,128)(2,1)} %pad_maximum_fusion.2), channel_id=1, source_target_pairs={{0,1},{1,0},{2,3},{3,2},{4,5},{5,4},{6,7},{7,6},{8,9},{9,8},{10,11... | collective-permute-start | bytes 6291464 | tf_op jit(solution)/shard_map/ppermute | solution.py:793
  311.2 49.7 %all-to-all-start.4 = ((f32[8,128,256]{2,1,0:T(8,128)}), f32[8,128,256]{2,1,0:T(8,128)S(1)}, u32[]{:S(2)}, u32[]{:S(2)}) async-start(f32[8,128,256]{2,1,0:T(8,128)} %chain.3), calls=%async_computation.4 | async-start | bytes 2097152 | tf_op jit(solution)/shard_map/all_to_all | solution.py:803
  355.2 90.5 %collective-permute-start.20 = (bf16[512,1024]{1,0:T(8,128)(2,1)S(1)}, bf16[512,1024]{1,0:T(8,128)(2,1)S(1)}, u32[]{:S(2)}, u32[]{:S(2)}) collective-permute-start(bf16[512,1024]{1,0:T(8,128)(2,1)S(1)} %fusion.7), channel_id=1, source_target_pairs={{0,2},{1,3},{2,0},{3,1},{4,6},{5,7},{6,4},{7,5},{8,10},{9,11},{10,... | collective-permute-start | bytes 3145736 | tf_op jit(solution)/shard_map/ppermute | solution.py:793
  427.2 24.7 %collective-permute-start.12 = (bf16[256,2048]{1,0:T(8,128)(2,1)S(1)}, bf16[256,2048]{1,0:T(8,128)(2,1)}, u32[]{:S(2)}, u32[]{:S(2)}) collective-permute-start(bf16[256,2048]{1,0:T(8,128)(2,1)S(1)} %fusion.11), channel_id=1, source_target_pairs={{0,2},{1,3},{2,0},{3,1},{4,6},{5,7},{6,4},{7,5},{8,10},{9,11},{10,... | collective-permute-start | bytes 3145736 | tf_op jit(solution)/shard_map/ppermute | solution.py:793
  445.7 30.8 %collective-permute-start.15 = (bf16[2,256,2432]{2,1,0:T(8,128)(2,1)}, bf16[2,256,2432]{2,1,0:T(8,128)(2,1)}, u32[]{:S(2)}, u32[]{:S(2)}) collective-permute-start(bf16[2,256,2432]{2,1,0:T(8,128)(2,1)} %pad_maximum_fusion), channel_id=1, source_target_pairs={{0,1},{1,0},{2,3},{3,2},{4,5},{5,4},{6,7},{7,6},{8,9},{9,8},{10,11... | collective-permute-start | bytes 7471112 | tf_op jit(solution)/shard_map/ppermute | solution.py:793
  490.8 42.3 %collective-permute-start.16 = (bf16[256,2432]{1,0:T(8,128)(2,1)}, bf16[256,2432]{1,0:T(8,128)(2,1)}, u32[]{:S(2)}, u32[]{:S(2)}) collective-permute-start(bf16[256,2432]{1,0:T(8,128)(2,1)} %fusion.1), channel_id=1, source_target_pairs={{0,2},{1,3},{2,0},{3,1},{4,6},{5,7},{6,4},{7,5},{8,10},{9,11},{10,... | collective-permute-start | bytes 3735560 | tf_op jit(solution)/shard_map/ppermute | solution.py:793
  501.9 25.3 %all-to-all-start.11 = ((bf16[4,64,1024]{2,1,0:T(8,128)(2,1)}), bf16[4,64,1024]{2,1,0:T(8,128)(2,1)S(1)}, u32[]{:S(2)}, u32[]{:S(2)}) async-start(bf16[4,64,1024]{2,1,0:T(8,128)(2,1)} %broadcast_in_dim.75), calls=%async_computation.11 | async-start | bytes 1048576 | tf_op jit(solution)/shard_map/all_to_all | solution.py:844
  547.4 28.4 %all-to-all-start.5 = ((f32[32,8,768]{2,1,0:T(8,128)}), f32[32,8,768]{2,1,0:T(8,128)S(1)}, u32[]{:S(2)}, u32[]{:S(2)}) async-start(f32[32,8,768]{2,1,0:T(8,128)} %reshape.107), calls=%async_computation.5 | async-start | bytes 1572864 | tf_op jit(solution)/shard_map/all_to_all | solution.py:803
  550.3 24.5 %collective-permute-start.17 = (bf16[128,2432]{1,0:T(8,128)(2,1)S(1)}, bf16[128,2432]{1,0:T(8,128)(2,1)S(1)}, u32[]{:S(2)}, u32[]{:S(2)}) collective-permute-start(bf16[128,2432]{1,0:T(8,128)(2,1)S(1)} %dynamic-slice_convert_fusion.6), channel_id=1, source_target_pairs={{0,4},{4,0},{8,12},{12,8},{16,20},{20,16},{24,28},{28,24},{1,5},{5... | collective-permute-start | bytes 1867784 | tf_op jit(solution)/shard_map/ppermute | solution.py:793
  575.8 21.2 %all-to-all-start.8 = ((bf16[4,32,2432]{2,1,0:T(8,128)(2,1)}), bf16[4,32,2432]{2,1,0:T(8,128)(2,1)S(1)}, u32[]{:S(2)}, u32[]{:S(2)}) async-start(bf16[4,32,2432]{2,1,0:T(8,128)(2,1)} %bitcast.103), calls=%async_computation.8 | async-start | bytes 1245184 | tf_op jit(solution)/shard_map/all_to_all | solution.py:844
  580.5 23.9 %collective-permute-start.22 = (bf16[256,1024]{1,0:T(8,128)(2,1)}, bf16[256,1024]{1,0:T(8,128)(2,1)}, u32[]{:S(2)}, u32[]{:S(2)}) collective-permute-start(bf16[256,1024]{1,0:T(8,128)(2,1)} %bitcast.104), channel_id=1, source_target_pairs={{0,4},{4,0},{8,12},{12,8},{16,20},{20,16},{24,28},{28,24},{1,5},{5... | collective-permute-start | bytes 1572872 | tf_op jit(solution)/shard_map/ppermute | solution.py:793
  581.1 38.9 %collective-permute-start.14 = (bf16[128,2048]{1,0:T(8,128)(2,1)}, bf16[128,2048]{1,0:T(8,128)(2,1)}, u32[]{:S(2)}, u32[]{:S(2)}) collective-permute-start(bf16[128,2048]{1,0:T(8,128)(2,1)} %bitcast.105), channel_id=1, source_target_pairs={{0,4},{4,0},{8,12},{12,8},{16,20},{20,16},{24,28},{28,24},{1,5},{5... | collective-permute-start | bytes 1572872 | tf_op jit(solution)/shard_map/ppermute | solution.py:793
  (46 other events, 739.9 us)

commit v2 on v1

v2 whole, which is shorter than its diff:
```python
import functools

import jax
import jax.numpy as jnp
from jax import lax
from jax.experimental import pallas as pl
from jax.experimental.pallas import tpu as pltpu
from jax.sharding import PartitionSpec as P

INNER = 2048
STATE = 128
HEADS = 32
TAPS = 4
BC = 2 * STATE
CH = INNER + BC
XCOLS = 2432
XUSED = 2336
Q = 256
HALF = Q // 2
TILE = 256
TILES = INNER // TILE
GROUPS = 2
GT = TILES // GROUPS
GW = INNER // GROUPS
REST = XCOLS - INNER
PIECES = 2 * GT
EDGE = 16
EPS = 1e-05

f32 = jnp.float32
bf16 = jnp.bfloat16
highest = lax.Precision.HIGHEST


def cparams(megabytes=56):
    return pltpu.CompilerParams(
        dimension_semantics=("arbitrary",), vmem_limit_bytes=megabytes * 2**20
    )


def dot(a, b):
    return lax.dot_general(a, b, (((1,), (0,)), ((), ())), preferred_element_type=f32)


def dot_lanes(a, b):
    return lax.dot_general(a, b, (((1,), (1,)), ((), ())), preferred_element_type=f32)


def dot_rows(a, b):
    return lax.dot_general(a, b, (((0,), (0,)), ((), ())), preferred_element_type=f32)


def sigmoid(v):
    return 0.5 * jnp.tanh(0.5 * v) + 0.5


def lane_iota(rows, lanes):
    return lax.broadcasted_iota(jnp.int32, (rows, lanes), 1)


def row_iota(rows, lanes):
    return lax.broadcasted_iota(jnp.int32, (rows, lanes), 0)


def spread(terms, width, first, shift):
    rows = row_iota(terms * HEADS, width) & (HEADS - 1)
    return jnp.where(rows == first + (lane_iota(terms * HEADS, width) >> shift), 1.0, 0.0).astype(bf16)


def halves(value):
    high = value.astype(bf16)
    return high, (value - high.astype(f32)).astype(bf16)


def terms2(value):
    return jnp.concatenate(halves(value), axis=1)


def terms4(value):
    high = value.astype(bf16)
    rest = value - high.astype(f32)
    middle, low = halves(rest)
    return jnp.concatenate([high, middle, low, jnp.zeros_like(high)], axis=1)


def split_dot(value, select):
    high = value.astype(bf16)
    low = (value - high.astype(f32)).astype(bf16)
    return dot(high, select) + dot(low, select)


def fine(product, a, b):
    a_high, a_low = halves(a)
    b_high, b_low = halves(b)
    return product(a_high, b_high) + (product(a_high, b_low) + product(a_low, b_high))


def head_select(tile):
    lanes = row_iota(TILE, 128) >> 6
    return jnp.where(lanes + tile * (TILE // 64) == lane_iota(TILE, 128), 1.0, 0.0).astype(bf16)


def shifted(current, before):
    joined = jnp.concatenate([before[EDGE - 8 :], current], axis=0)
    rows = current.shape[0]
    return [joined[5 + k : 5 + k + rows] for k in range(TAPS - 1)] + [current]


def conv_of(parts, taps, bias):
    total = bias + taps[0:1] * parts[0]
    for k in range(1, TAPS):
        total = total + taps[k : k + 1] * parts[k]
    return total


def later_rows(grad, after):
    joined = jnp.concatenate([grad, after], axis=0)
    rows = grad.shape[0]
    return [joined[TAPS - 1 - k : TAPS - 1 - k + rows] for k in range(TAPS - 1)] + [grad]


def tap_sums(parts, raw, grad, early):
    first = grad[:8]
    sums = []
    for k in range(TAPS):
        total = jnp.sum(parts[k] * raw, axis=0, keepdims=True)
        if k < TAPS - 1:
            total = total + jnp.sum(first[: TAPS - 1 - k] * early[8 - TAPS + 1 + k :], axis=0, keepdims=True)
        sums.append(total)
    sums.append(jnp.sum(grad, axis=0, keepdims=True))
    sums.append(jnp.zeros((3, grad.shape[1]), f32))
    return jnp.concatenate(sums, axis=0)


def tile_at(j, width=TILE):
    return pl.ds(pl.multiple_of(j * width, width), width)


def assemble(order, pieces, full):
    rows = pieces[0].shape[0]
    for k, piece in enumerate(pieces):
        full[pl.ds(pl.multiple_of(order[k] * rows, rows), rows), :] = piece[...]


def norm_rows(values, gain):
    wide = values.astype(f32)
    scale = lax.rsqrt(jnp.mean(wide * wide, axis=1, keepdims=True) + EPS)
    return (wide * scale * gain).astype(bf16)


def project_kernel(order, tokens, edge, gain, w0, w1, w2, w3, normed, out, out_rest, out_edge, out_edge_rest, full):
    @pl.when(pl.program_id(0) == 0)
    def _():
        assemble(order, (w0, w1, w2, w3), full)
        early = dot(norm_rows(edge[...], gain[...]), full[...]).astype(bf16)
        out_edge[...] = early[:, :GW]
        out_edge_rest[...] = early[:, GW:]

    now = norm_rows(tokens[...], gain[...])
    normed[...] = now
    for start in range(0, GW, TILE):
        out[:, start : start + TILE] = dot(now, full[:, start : start + TILE]).astype(bf16)
    out_rest[...] = dot(now, full[:, GW:]).astype(bf16)


def project_more_kernel(order, normed, edge, gain, w0, w1, w2, w3, out, out_edge, full):
    @pl.when(pl.program_id(0) == 0)
    def _():
        assemble(order, (w0, w1, w2, w3), full)
        out_edge[...] = dot(norm_rows(edge[...], gain[...]), full[...]).astype(bf16)

    for start in range(0, GW, TILE):
        out[:, start : start + TILE] = dot(normed[...], full[:, start : start + TILE]).astype(bf16)


def fixed(shape):
    return pl.BlockSpec(shape, lambda i, *o: (0,) * len(shape), pipeline_mode=pl.Buffered(1))


def kept(shape):
    return pl.BlockSpec(shape, lambda i, *o: (0,) * len(shape))


def rows_of(cols, group=0):
    return pl.BlockSpec((Q, cols), lambda i, *o: (i, group))


def shape_of(shape, dtype=f32):
    return jax.ShapeDtypeStruct(shape, dtype)


def cost(flops, megabytes):
    return pl.CostEstimate(flops=int(flops) // 50, bytes_accessed=int(megabytes * 2**20) // 50, transcendentals=0)


def project(order, tokens, edge, gain, pieces):
    length, width = tokens.shape
    rows = pieces[0].shape[0]
    return pl.pallas_call(
        project_kernel,
        grid_spec=pltpu.PrefetchScalarGridSpec(
            num_scalar_prefetch=1,
            grid=(length // Q,),
            in_specs=[rows_of(width), fixed((EDGE, width)), fixed((1, width))] + [fixed((rows, GW + REST))] * 4,
            out_specs=[rows_of(width), rows_of(GW), rows_of(REST), kept((EDGE, GW)), kept((EDGE, REST))],
            scratch_shapes=[pltpu.VMEM((4 * rows, GW + REST), bf16)],
        ),
        out_shape=[
            shape_of((length, width), bf16),
            shape_of((length, GW), bf16),
            shape_of((length, REST), bf16),
            shape_of((EDGE, GW), bf16),
            shape_of((EDGE, REST), bf16),
        ],
        compiler_params=cparams(),
        cost_estimate=cost(2 * length * width * (GW + REST), 9),
        name="project",
    )(order, tokens, edge, gain, *pieces)


def project_more(order, normed, edge, gain, pieces):
    length, width = normed.shape
    rows = pieces[0].shape[0]
    return pl.pallas_call(
        project_more_kernel,
        grid_spec=pltpu.PrefetchScalarGridSpec(
            num_scalar_prefetch=1,
            grid=(length // Q,),
            in_specs=[rows_of(width), fixed((EDGE, width)), fixed((1, width))] + [fixed((rows, GW))] * 4,
            out_specs=[rows_of(GW), kept((EDGE, GW))],
            scratch_shapes=[pltpu.VMEM((4 * rows, GW), bf16)],
        ),
        out_shape=[shape_of((length, GW), bf16), shape_of((EDGE, GW), bf16)],
        compiler_params=cparams(),
        cost_estimate=cost(2 * length * width * GW, 6),
        name="project_more",
    )(order, normed, edge, gain, *pieces)


def gate_kernel(order, normed, w0, w1, w2, w3, out, full):
    @pl.when(pl.program_id(0) == 0)
    def _():
        assemble(order, (w0, w1, w2, w3), full)

    for j in range(TILES):
        cols = slice(j * TILE, (j + 1) * TILE)
        out[:, cols] = dot(normed[...], full[:, cols]).astype(bf16)


def gate_project(order, normed, pieces):
    length, width = normed.shape
    rows = pieces[0].shape[0]
    return pl.pallas_call(
        gate_kernel,
        grid_spec=pltpu.PrefetchScalarGridSpec(
            num_scalar_prefetch=1,
            grid=(length // Q,),
            in_specs=[rows_of(width)] + [fixed((rows, INNER))] * 4,
            out_specs=rows_of(INNER),
            scratch_shapes=[pltpu.VMEM((4 * rows, INNER), bf16)],
        ),
        out_shape=shape_of((length, INNER), bf16),
        compiler_params=cparams(),
        cost_estimate=cost(2 * length * width * INNER, 10),
        name="gate_project",
    )(order, normed, *pieces)


def factors_kernel(now, prior, edge, taps_bc, bias_bc, heads, bc_act, aux_out, cum_t):
    first = pl.program_id(0) == 0
    early = jnp.where(first, edge[:, :BC], prior[:, :BC]).astype(f32)
    pre = conv_of(shifted(now[:, :BC].astype(f32), early), taps_bc[...], bias_bc[...])
    bc_act[...] = pre * sigmoid(pre)
    raw = now[:, BC : BC + HEADS].astype(f32) + heads[2:3, :HEADS]
    step = jnp.maximum(raw, 0.0) + jnp.log1p(jnp.exp(-jnp.abs(raw)))
    decay = -jnp.exp(heads[0:1, :HEADS]) * step
    lower = jnp.where(row_iota(Q, Q) >= lane_iota(Q, Q), 1.0, 0.0)
    cumulative = jnp.dot(lower, decay, precision=highest, preferred_element_type=f32)
    last = cumulative[Q - 1 : Q]
    aux = jnp.concatenate([cumulative, step, jnp.exp(last - cumulative), jnp.exp(cumulative)], axis=1)
    aux_out[...] = aux
    cum_t[...] = aux.T[:HEADS]


def states_kernel(
    group, now, prior, edge, taps, bias, bc_act, aux, x_act, local, payload, run, total, b_rows
):
    c = pl.program_id(0)
    first = c == 0

    @pl.when(first)
    def _():
        run[...] = jnp.zeros_like(run)
        total[...] = jnp.zeros_like(total)

    b_rows[...] = bc_act[:, :STATE].T
    weight2 = terms2(aux[:, HEADS : 2 * HEADS] * aux[:, 2 * HEADS : 3 * HEADS])
    ends4 = terms4(jnp.concatenate([aux[Q - 8 :, 3 * HEADS :], aux[Q - 8 :, :HEADS]], axis=0))

    def body(j, carry):
        cols = tile_at(j)
        early = jnp.where(first, edge[:, cols], prior[:, cols]).astype(f32)
        pre = conv_of(shifted(now[:, cols].astype(f32), early), taps[:, cols], bias[:, cols])
        x = pre * sigmoid(pre)
        x_act[:, cols] = x
        lead = 4 * (j + group * GT)
        state = fine(dot, b_rows[...], x * dot(weight2, spread(2, TILE, lead, 6)))
        local[0, j] = state
        end = dot(ends4, spread(4, TILE, lead, 6))
        run[j] = end[7:8] * run[j] + state
        total[:, cols] += end[15:16]
        return carry

    lax.fori_loop(0, GT, body, 0, unroll=GT)

    @pl.when(c == pl.num_programs(0) - 1)
    def _():
        for j in range(2 * GT):
            lanes = slice(128 * (j % 2), 128 * (j % 2) + 128)
            payload[j, :STATE, :] = run[j // 2, :, lanes]
            payload[j, STATE:, :] = jnp.broadcast_to(total[:, j * 128 : (j + 1) * 128], (8, 128))


def prior_rows(cols, group=0):
    per = Q // EDGE
    return pl.BlockSpec((EDGE, cols), lambda i, *o: (jnp.maximum(i * per - 1, 0), group))


def at_group(rows, group):
    return pl.BlockSpec((rows, GW), lambda i, *o: (0, group), pipeline_mode=pl.Buffered(1))


def factors(rest, rest_edge, taps_bc, bias_bc, heads):
    length = rest.shape[0]
    return pl.pallas_call(
        factors_kernel,
        grid=(length // Q,),
        in_specs=[
            rows_of(REST), prior_rows(REST), fixed((EDGE, REST)),
            fixed((TAPS, BC)), fixed((1, BC)), fixed((8, 128)),
        ],
        out_specs=[rows_of(BC), rows_of(128), pl.BlockSpec((HEADS, Q), lambda i: (0, i))],
        out_shape=[shape_of((length, BC)), shape_of((length, 128)), shape_of((HEADS, length))],
        compiler_params=cparams(),
        cost_estimate=cost(10**9, 4),
        name="factors",
    )(rest, rest, rest_edge, taps_bc, bias_bc, heads)


def states(group, proj, proj_edge, taps, bias, bc_act, aux):
    length = proj.shape[0]
    chunks = length // Q
    return pl.pallas_call(
        functools.partial(states_kernel, group),
        grid=(chunks,),
        in_specs=[
            rows_of(GW), prior_rows(GW), fixed((EDGE, GW)),
            at_group(TAPS, group), at_group(1, group), rows_of(BC), rows_of(128),
        ],
        out_specs=[
            rows_of(GW),
            pl.BlockSpec((1, GT, STATE, TILE), lambda i: (i, 0, 0, 0)),
            kept((2 * GT, STATE + 8, 128)),
        ],
        out_shape=[
            shape_of((length, GW)),
            shape_of((chunks, GT, STATE, TILE)),
            shape_of((2 * GT, STATE + 8, 128)),
        ],
        scratch_shapes=[
            pltpu.VMEM((GT, STATE, TILE), f32),
            pltpu.VMEM((1, GW), f32),
            pltpu.VMEM((STATE, Q), f32),
        ],
        compiler_params=cparams(),
        cost_estimate=cost(10**10, 10),
        name="states",
    )(proj, proj, proj_edge, taps, bias, bc_act, aux)


def chain_kernel(forward, values, totals, out):
    count = out.shape[0]
    order = range(count) if forward else range(count - 1, -1, -1)
    state = jnp.zeros(out.shape[1:], f32)
    for i in order:
        out[i] = state
        state = jnp.exp(totals[i, 0:1, :]) * state + values[i, :STATE, :]


def chain(forward, values, totals):
    count, _, width = values.shape
    return pl.pallas_call(
        functools.partial(chain_kernel, forward),
        out_shape=jax.ShapeDtypeStruct((count, STATE, width), f32),
        compiler_params=pltpu.CompilerParams(vmem_limit_bytes=56 * 2**20),
        cost_estimate=cost(10**8, 3),
        name="chain",
    )(values, totals)


def within_kernel(group, x_act, bc_act, aux, cum_t, skip, out, scores, columns):
    lower = row_iota(HALF, HALF) >= lane_iota(HALF, HALF)
    for b in range(2):
        rows = slice(b * HALF, (b + 1) * HALF)
        scores[rows, :] = jnp.where(lower, fine(dot_lanes, bc_act[rows, STATE:], bc_act[rows, :STATE]), 0.0)
    cross_high, cross_low = halves(fine(dot_lanes, bc_act[HALF:, STATE:], bc_act[:HALF, :STATE]))
    cross2 = jnp.concatenate([cross_high, cross_low], axis=1)
    cumulative = aux[:, :HEADS]
    middle_row = cumulative[HALF - 1 : HALF]
    step2 = terms2(aux[:, HEADS : 2 * HEADS])
    bridge2 = terms2(jnp.exp(jnp.concatenate([middle_row - cumulative[:HALF], cumulative[HALF:] - middle_row], axis=0)))
    cumulative4 = terms4(cumulative)
    for j in range(GT):
        columns[:, j * 512 : (j + 1) * 512] = dot(cumulative4, spread(4, 512, 4 * (j + group * GT), 7))
    low = lane_iota(HALF, HALF) < 64

    def body(j, carry):
        cols = tile_at(j)
        x = x_act[:, cols]
        select = spread(2, TILE, 4 * (j + group * GT), 6)
        u = x * dot(step2, select)
        bridge = dot(bridge2, select)
        u_high, u_low = halves(u)
        v_high, v_low = halves(u[:HALF] * bridge[:HALF])
        across = dot(cross2, jnp.concatenate([v_high, v_high], axis=0)) + dot(cross_high, v_low)
        across = across * bridge[HALF:]
        direct = skip[:, cols] * x
        for pair in range(2):
            lanes = slice(pair * 128, (pair + 1) * 128)
            place = pl.ds(pl.multiple_of(j * TILE + pair * 128, 128), 128)
            for b in range(2):
                rows = slice(b * HALF, (b + 1) * HALF)
                weights = []
                for i in range(2):
                    head = 4 * j + 2 * pair + i
                    column = columns[rows, pl.ds(pl.multiple_of(head * 128, 128), 128)]
                    row = cum_t[pl.ds(head + 4 * GT * group, 1), :][:, rows]
                    weights.append(jnp.exp(jnp.minimum(column - row, 0.0)) * scores[rows, :])
                w_high, w_low = halves(jnp.concatenate(weights, axis=1))
                top = both_heads(low, u_high[rows, lanes])
                bottom = both_heads(low, u_low[rows, lanes])
                twice = dot(w_high, jnp.concatenate([top, bottom], axis=1))
                y = twice[:, :128] + twice[:, 128:] + dot(w_low, top) + direct[rows, lanes]
                if b == 1:
                    y = y + across[:, lanes]
                out[rows, place] = y
        return carry

    lax.fori_loop(0, GT, body, 0, unroll=GT)


def both_heads(low, value):
    zero = jnp.zeros_like(value)
    return jnp.concatenate([jnp.where(low, value, zero), jnp.where(low, zero, value)], axis=0)


def within(group, x_act, bc_act, aux, cum_t, skip):
    length = x_act.shape[0]
    return pl.pallas_call(
        functools.partial(within_kernel, group),
        grid=(length // Q,),
        in_specs=[
            rows_of(GW), rows_of(BC), rows_of(128),
            pl.BlockSpec((HEADS, Q), lambda i: (0, i)), at_group(1, group),
        ],
        out_specs=rows_of(GW),
        out_shape=shape_of((length, GW)),
        scratch_shapes=[pltpu.VMEM((Q, HALF), f32), pltpu.VMEM((Q, GT * 512), f32)],
        compiler_params=cparams(),
        cost_estimate=cost(10**10, 10),
        name="within",
    )(x_act, bc_act, aux, cum_t, skip)


def within_back_kernel(
    group, x_act, bc_act, aux, cum_t, dy, now, prior, edge, taps, bias, ends, entering,
    out, slope, out_bc, k_dot, scores, grad_scores, grad_cross, columns,
):
    first = pl.program_id(0) == 0
    k_dot[...] = jnp.zeros_like(k_dot)
    out_bc[:, STATE:] = jnp.zeros((Q, STATE), f32)
    upper = row_iota(HALF, HALF) <= lane_iota(HALF, HALF)
    act = bc_act[...].astype(bf16)
    b_act, c_act = act[:, :STATE], act[:, STATE:]
    for b in range(2):
        rows = slice(b * HALF, (b + 1) * HALF)
        scores[rows, :] = jnp.where(upper, dot_lanes(b_act[rows], c_act[rows]), 0.0)
    grad_scores[...] = jnp.zeros_like(grad_scores)
    grad_cross[...] = jnp.zeros_like(grad_cross)
    cross = dot_lanes(b_act[:HALF], c_act[HALF:]).astype(bf16)
    cumulative = aux[:, :HEADS]
    middle_row = cumulative[HALF - 1 : HALF]
    step2 = terms2(aux[:, HEADS : 2 * HEADS])
    decayed2 = terms2(aux[:, 3 * HEADS :])
    bridge2 = terms2(jnp.exp(jnp.concatenate([middle_row - cumulative[:HALF], cumulative[HALF:] - middle_row], axis=0)))
    cumulative4 = terms4(cumulative)
    for j in range(GT):
        columns[:, j * 512 : (j + 1) * 512] = dot(cumulative4, spread(4, 512, 4 * (j + group * GT), 7))
    low = lane_iota(HALF, HALF) < 64

    def body(j, carry):
        cols = tile_at(j)
        lead = 4 * (j + group * GT)
        select = spread(2, TILE, lead, 6)
        x = x_act[:, cols]
        u = x * dot(step2, select)
        bridge = dot(bridge2, select)
        u_low = u.astype(bf16)
        grad = dy[:, cols]
        wide = grad.astype(f32)
        early_raw = jnp.where(first, edge[:, cols], prior[:, cols]).astype(f32)
        pre = conv_of(shifted(now[:, cols].astype(f32), early_raw), taps[:, cols], bias[:, cols])
        sig = sigmoid(pre)
        slope[:, cols] = (sig + x * (1.0 - sig)).astype(bf16)
        k_dot[...] += split_dot(x * wide, head_select(j + group * GT))
        enter = jnp.where(first, entering[j], ends[0, j])
        out_bc[:, STATE:] += fine(dot_lanes, wide * dot(decayed2, select), enter)
        early = (u[:HALF] * bridge[:HALF]).astype(bf16)
        late = (grad[HALF:].astype(f32) * bridge[HALF:]).astype(bf16)
        grad_cross[...] += dot_lanes(early, late)
        across = dot(cross, late) * bridge[:HALF]
        totals = [None, None]
        for pair in range(2):
            lanes = slice(pair * 128, (pair + 1) * 128)
            place = pl.ds(pl.multiple_of(j * TILE + pair * 128, 128), 128)
            for b in range(2):
                rows = slice(b * HALF, (b + 1) * HALF)
                spaced = both_heads(low, grad[rows, lanes])
                products = dot_lanes(u_low[rows, lanes], spaced)
                weights = []
                for i in range(2):
                    head = 4 * j + 2 * pair + i
                    column = columns[rows, pl.ds(pl.multiple_of(head * 128, 128), 128)]
                    row = cum_t[pl.ds(head + 4 * GT * group, 1), :][:, rows]
                    weight = jnp.exp(jnp.minimum(row - column, 0.0))
                    part = weight * products[:, i * 128 : (i + 1) * 128]
                    totals[b] = part if totals[b] is None else totals[b] + part
                    weights.append((weight * scores[rows, :]).astype(bf16))
                du = dot(jnp.concatenate(weights, axis=1), spaced)
                if b == 0:
                    du = du + across[:, lanes]
                out[rows, place] = du.astype(bf16)
        for b in range(2):
            grad_scores[b * HALF : (b + 1) * HALF, :] += totals[b]
        return carry

    lax.fori_loop(0, GT, body, 0, unroll=GT)
    far = grad_cross[...].astype(bf16)
    near0 = jnp.where(upper, grad_scores[:HALF, :], 0.0).astype(bf16)
    near1 = jnp.where(upper, grad_scores[HALF:, :], 0.0).astype(bf16)
    out_bc[:HALF, :STATE] = dot(near0, c_act[:HALF]) + dot(far, c_act[HALF:])
    out_bc[HALF:, :STATE] = dot(near1, c_act[HALF:])
    out_bc[:HALF, STATE:] += dot_rows(near0, b_act[:HALF])
    out_bc[HALF:, STATE:] += dot_rows(near1, b_act[HALF:]) + dot_rows(far, b_act[:HALF])


def within_back(group, x_act, bc_act, aux, cum_t, dy, proj, proj_edge, taps, bias, ends, entering):
    length = x_act.shape[0]
    return pl.pallas_call(
        functools.partial(within_back_kernel, group),
        grid=(length // Q,),
        in_specs=[
            rows_of(GW), rows_of(BC), rows_of(128),
            pl.BlockSpec((HEADS, Q), lambda i: (0, i)), rows_of(GW, group),
            rows_of(GW), prior_rows(GW), fixed((EDGE, GW)),
            at_group(TAPS, group), at_group(1, group),
            pl.BlockSpec((1, GT, STATE, TILE), lambda i: (jnp.maximum(i - 1, 0), group, 0, 0)),
            pl.BlockSpec((GT, STATE, TILE), lambda i: (group, 0, 0), pipeline_mode=pl.Buffered(1)),
        ],
        out_specs=[rows_of(GW), rows_of(GW), rows_of(BC), rows_of(128)],
        out_shape=[
            shape_of((length, GW), bf16), shape_of((length, GW), bf16),
            shape_of((length, BC)), shape_of((length, 128)),
        ],
        scratch_shapes=[
            pltpu.VMEM((Q, HALF), f32),
            pltpu.VMEM((Q, HALF), f32),
            pltpu.VMEM((HALF, HALF), f32),
            pltpu.VMEM((Q, GT * 512), f32),
        ],
        compiler_params=cparams(),
        cost_estimate=cost(2 * 10**10, 14),
        name="within_back",
    )(x_act, bc_act, aux, cum_t, dy, proj, proj, proj_edge, taps, bias, ends, entering)


def middle_kernel(
    order, y_in0, y_in1, bc_act, aux, local0, local1, entering0, entering1, gate, tokens, cot, gain, w0, w1, w2, w3,
    normed_out, output, dy_out, grad_gate, ends, back_states, begin, payload, y_dot, gain_grad,
    full, state, back, before, y_keep, gated_keep, grad_keep,
):
    c = pl.program_id(0)

    @pl.when(c == 0)
    def _():
        assemble(order, (w0, w1, w2, w3), full)
        for g, entering in enumerate((entering0, entering1)):
            for j in range(GT):
                state[g * GT + j, :, :128] = entering[2 * j]
                state[g * GT + j, :, 128:] = entering[2 * j + 1]
        begin[...] = state[...]
        back[...] = jnp.zeros_like(back)
        before[...] = jnp.zeros_like(before)
        gain_grad[...] = jnp.zeros_like(gain_grad)

    keep = aux[...]
    c_cols = bc_act[:, STATE:]
    c_rows = bc_act[:, STATE:].T

    decayed2 = terms2(keep[:, 3 * HEADS :])
    ends4 = terms4(jnp.concatenate([keep[Q - 8 :, 3 * HEADS :], keep[Q - 8 :, :HEADS]], axis=0))

    def mix(y_in, local, shift, place, squares):
        j = place + shift
        cols = tile_at(j)
        carried = fine(dot, c_cols, state[j])
        y = y_in[:, tile_at(place)] + dot(decayed2, spread(2, TILE, 4 * j, 6)) * carried
        y_keep[:, cols] = y
        raw = gate[:, cols].astype(f32)
        gated = y.astype(bf16).astype(f32) * (raw * sigmoid(raw))
        gated_keep[:, cols] = gated
        moved = dot(ends4, spread(4, TILE, 4 * j, 6))[7:8] * state[j] + local[0, place]
        state[j] = moved
        ends[0, j] = moved
        both = gated * gated
        return squares + (both[:, :128] + both[:, 128:])

    squares = jnp.zeros((Q, 128), f32)
    for g, (y_in, local) in enumerate(((y_in0, local0), (y_in1, local1))):
        squares = lax.fori_loop(0, GT, functools.partial(mix, y_in, local, g * GT), squares, unroll=GT)
    scale = lax.rsqrt(jnp.sum(squares, axis=1, keepdims=True) / INNER + EPS)

    def back_out(j, products):
        cols = tile_at(j)
        gated = gated_keep[:, cols]
        gains = gain[:, cols]
        normed_out[:, cols] = (gated * scale * gains).astype(bf16)
        grad = dot_lanes(cot[...], full[cols, :])
        grad_keep[:, cols] = grad
        gain_grad[:, cols] += jnp.sum(grad * gated * scale, axis=0, keepdims=True)
        both = grad * gains * gated
        return products + (both[:, :128] + both[:, 128:])

    products = lax.fori_loop(0, TILES, back_out, jnp.zeros((Q, 128), f32), unroll=4)
    shared = jnp.sum(products, axis=1, keepdims=True) / INNER * (scale * scale * scale)
    for start in range(0, output.shape[1], TILE):
        cols = slice(start, start + TILE)
        branch = dot(normed_out[...], full[:, cols])
        output[:, cols] = (tokens[:, cols].astype(f32) + branch).astype(bf16)

    def finish(j, y_sum):
        cols = tile_at(j)
        raw = gate[:, cols].astype(f32)
        sig = sigmoid(raw)
        grad_gated = scale * (grad_keep[:, cols] * gain[:, cols]) - gated_keep[:, cols] * shared
        y = y_keep[:, cols]
        dy = (grad_gated * (raw * sig)).astype(bf16)
        dy_out[:, cols] = dy
        mixed = y.astype(bf16).astype(f32)
        grad_gate[:, cols] = (grad_gated * mixed * (sig * (1.0 + raw * (1.0 - sig)))).astype(bf16)
        wide = dy.astype(f32)
        piece = fine(dot, c_rows, wide * dot(decayed2, spread(2, TILE, 4 * j, 6)))
        back_states[0, j] = piece
        back[j] += jnp.exp(before[:, cols]) * piece
        before[:, cols] += dot(ends4, spread(4, TILE, 4 * j, 6))[15:16]
        return y_sum + split_dot(wide * y, head_select(j))

    y_dot[...] = lax.fori_loop(0, TILES, finish, jnp.zeros((Q, 128), f32), unroll=4)

    @pl.when(c == pl.num_programs(0) - 1)
    def _():
        for g in range(GROUPS):
            for j in range(GT):
                payload[2 * j, :, g * 128 : (g + 1) * 128] = back[g * GT + j, :, :128]
                payload[2 * j + 1, :, g * 128 : (g + 1) * 128] = back[g * GT + j, :, 128:]


def middle(order, y_in, bc_act, aux, local, entering, gate, tokens, cot, gain, pieces):
    length, width = tokens.shape
    rows = pieces[0].shape[0]
    chunks = length // Q
    per_group = pl.BlockSpec((1, GT, STATE, TILE), lambda i, o: (i, 0, 0, 0))
    per_chunk = pl.BlockSpec((1, TILES, STATE, TILE), lambda i, o: (i, 0, 0, 0))
    return pl.pallas_call(
        middle_kernel,
        grid_spec=pltpu.PrefetchScalarGridSpec(
            num_scalar_prefetch=1,
            grid=(chunks,),
            in_specs=[rows_of(GW)] * 2
            + [rows_of(BC), rows_of(128)]
            + [per_group] * 2
            + [fixed((2 * GT, STATE, 128))] * 2
            + [rows_of(INNER), rows_of(width), rows_of(width), fixed((1, INNER))]
            + [fixed((rows, width))] * 4,
            out_specs=[
                rows_of(INNER), rows_of(width), rows_of(INNER), rows_of(INNER), per_chunk, per_chunk,
                kept((TILES, STATE, TILE)), kept((PIECES, STATE, TILE)), rows_of(128), kept((1, INNER)),
            ],
            scratch_shapes=[
                pltpu.VMEM((4 * rows, width), bf16),
                pltpu.VMEM((TILES, STATE, TILE), f32),
                pltpu.VMEM((TILES, STATE, TILE), f32),
                pltpu.VMEM((1, INNER), f32),
                pltpu.VMEM((Q, INNER), f32),
                pltpu.VMEM((Q, INNER), f32),
                pltpu.VMEM((Q, INNER), f32),
            ],
        ),
        out_shape=[
            shape_of((length, INNER), bf16),
            shape_of((length, width), bf16),
            shape_of((length, INNER), bf16),
            shape_of((length, INNER), bf16),
            shape_of((chunks, TILES, STATE, TILE)),
            shape_of((chunks, TILES, STATE, TILE)),
            shape_of((TILES, STATE, TILE)),
            shape_of((PIECES, STATE, TILE)),
            shape_of((length, 128)),
            shape_of((1, INNER)),
        ],
        compiler_params=cparams(),
        cost_estimate=cost(4 * 10**10, 40),
        name="middle",
    )(order, *y_in, bc_act, aux, *local, *entering, gate, tokens, cot, gain, *pieces)


def back_kernel(
    group, now, edge, taps, skip, dy, du_in, slope, x_act, bc_act, aux, ends, back_states, leaving, *others
):
    last_group = group == GROUPS - 1
    if last_group:
        (rest, rest_prior, rest_edge, taps_bc, bias_bc, heads, y_dot,
         k_dot0, k_dot1, x_before, edge_before, b_before, bc_in0, bc_in1,
         grad, grad_taps, tail, start, grad_taps_bc, grad_heads,
         later, after, x_dot, edge_dot, b_sum) = others
    else:
        (grad, grad_taps, tail, start, x_dot, edge_dot, b_sum, later, after) = others
    step_id = pl.program_id(0)
    first = step_id == pl.num_programs(0) - 1

    @pl.when(step_id == 0)
    def _():
        for j in range(GT):
            later[j, :, :128] = leaving[2 * j, :, group * 128 : (group + 1) * 128]
            later[j, :, 128:] = leaving[2 * j + 1, :, group * 128 : (group + 1) * 128]
        after[...] = jnp.zeros_like(after)
        grad_taps[...] = jnp.zeros_like(grad_taps)
        if last_group:
            grad_taps_bc[...] = jnp.zeros_like(grad_taps_bc)
            grad_heads[...] = jnp.zeros_like(grad_heads)

    keep = aux[...]
    b_act = bc_act[:, :STATE].astype(bf16)
    factors2 = terms2(
        jnp.concatenate([keep[:, HEADS * k : HEADS * (k + 1)] for k in range(1, 3)], axis=0)
    )
    ends4 = terms4(keep[Q - 8 :, 3 * HEADS :])
    x_dot[...] = jnp.zeros_like(x_dot)
    edge_dot[...] = jnp.zeros_like(edge_dot)
    b_sum[...] = jnp.zeros_like(b_sum)

    def through(cols, dv, raw, early, tap_values):
        parts = later_rows(dv, after[:, cols])
        result = conv_of(parts, tap_values, 0.0)
        after[:, cols] = dv[:8]
        grad[:, cols] = result.astype(bf16)

        @pl.when(step_id == 0)
        def _():
            tail[:, cols] = result[Q - EDGE :]

        early = jnp.where(first, early[EDGE - 8 :].astype(f32), 0.0)
        return tap_sums(parts, raw, dv, early)

    def body(j, carry):
        cols = tile_at(j)
        select = spread(2, TILE, 4 * (j + group * GT), 6)
        heads_of = head_select(j + group * GT)
        factors = dot(factors2, select)
        step, tail_decay = factors[:Q], factors[Q:]
        x = x_act[:, cols]
        later_state = later[j]
        du = du_in[:, cols].astype(f32) + tail_decay * dot(b_act, later_state.astype(bf16))
        x_dot[...] += split_dot(x * du, heads_of)
        b_sum[...] += fine(dot_lanes, x * step * tail_decay, later_state)
        meet = jnp.sum(ends[0, j] * later_state, axis=0, keepdims=True)
        edge_dot[...] += split_dot(jnp.broadcast_to(meet, (8, TILE)), heads_of)
        later[j] = dot(ends4, spread(4, TILE, 4 * (j + group * GT), 6))[7:8] * later_state + back_states[0, j]
        dv = (step * du + skip[:, cols] * dy[:, cols].astype(f32)) * slope[:, cols].astype(f32)
        grad_taps[:, cols] += through(cols, dv, now[:, cols].astype(f32), edge[:, cols], taps[:, cols])
        return carry

    lax.fori_loop(0, GT, body, 0, unroll=2)

    if last_group:
        band = slice(GW, GW + BC)
        current = rest[:, :BC].astype(f32)
        early = jnp.where(first, rest_edge[:, :BC], rest_prior[:, :BC])
        pre = conv_of(shifted(current, early.astype(f32)), taps_bc[...], bias_bc[...])
        sig = sigmoid(pre)
        grad_act = bc_in0[...] + bc_in1[...]
        grad_act = grad_act + jnp.concatenate([b_sum[...] + b_before[...], jnp.zeros((Q, STATE), f32)], axis=1)
        dv = grad_act * (sig * (1.0 + pre * (1.0 - sig)))
        grad_taps_bc[...] += through(band, dv, current, rest_edge[:, :BC], taps_bc[...])

        step = keep[:, HEADS : 2 * HEADS]
        by_step = x_dot[:, :HEADS] + x_before[:, :HEADS]
        by_skip = k_dot0[:, :HEADS] + k_dot1[:, :HEADS]
        rate = -jnp.exp(heads[0:1, :HEADS])
        by_sum = y_dot[:, :HEADS] - heads[1:2, :HEADS] * by_skip - step * by_step
        upper = jnp.where(row_iota(Q, Q) <= lane_iota(Q, Q), 1.0, 0.0)
        by_decay = jnp.dot(upper, by_sum, precision=highest, preferred_element_type=f32)
        by_decay = by_decay + (edge_dot[0:1, :HEADS] + edge_before[0:1, :HEADS])
        raw = rest[:, BC : BC + HEADS].astype(f32) + heads[2:3, :HEADS]
        grad_dt = (by_step + by_decay * rate) * sigmoid(raw)
        full_dt = jnp.concatenate([grad_dt, jnp.zeros((Q, 128 - HEADS), f32)], axis=1)
        grad[:, GW + BC :] = full_dt.astype(bf16)
        sums = [
            jnp.sum(by_decay * (rate * step), axis=0, keepdims=True),
            jnp.sum(by_skip, axis=0, keepdims=True),
            jnp.sum(grad_dt, axis=0, keepdims=True),
            jnp.zeros((5, HEADS), f32),
        ]
        grad_heads[:, :HEADS] += jnp.concatenate(sums, axis=0)

    @pl.when(first)
    def _():
        start[...] = after[...]


def backward(group, proj, proj_edge, taps, skip, dy, du, slope, x_act, bc_act, aux, ends, back_states, leaving, others=()):
    length = proj.shape[0]
    chunks = length // Q
    per = Q // EDGE
    last_group = group == GROUPS - 1
    at = lambda i: chunks - 1 - i
    block = lambda cols, g=0: pl.BlockSpec((Q, cols), lambda i: (at(i), g))
    per_chunk = pl.BlockSpec((1, GT, STATE, TILE), lambda i: (at(i), group, 0, 0))
    dots = pl.BlockSpec((8, 128), lambda i: (at(i), 0))
    in_specs = [
        block(GW), fixed((EDGE, GW)), at_group(TAPS, group), at_group(1, group),
        block(GW, group), block(GW), block(GW), block(GW), block(BC), block(128),
        per_chunk, per_chunk, fixed((PIECES, STATE, TILE)),
    ]
    width = GW + BC if last_group else GW
    cols = GW + REST if last_group else GW
    out_specs = [block(cols), kept((8, GW)), kept((EDGE, width)), kept((8, width))]
    out_shape = [
        shape_of((length, cols), bf16), shape_of((8, GW)), shape_of((EDGE, width)), shape_of((8, width)),
    ]
    scratch = [pltpu.VMEM((GT, STATE, TILE), f32), pltpu.VMEM((8, width), f32)]
    if last_group:
        in_specs += [
            block(REST),
            pl.BlockSpec((EDGE, REST), lambda i: (jnp.maximum(at(i) * per - 1, 0), 0)),
            fixed((EDGE, REST)), fixed((TAPS, BC)), fixed((1, BC)), fixed((8, 128)),
            block(128), block(128), block(128), block(128), dots, block(STATE), block(BC), block(BC),
        ]
        out_specs += [kept((8, BC)), kept((8, 128))]
        out_shape += [shape_of((8, BC)), shape_of((8, 128))]
        scratch += [pltpu.VMEM((Q, 128), f32), pltpu.VMEM((8, 128), f32), pltpu.VMEM((Q, STATE), f32)]
    else:
        out_specs += [block(128), dots, block(STATE)]
        out_shape += [shape_of((length, 128)), shape_of((8 * chunks, 128)), shape_of((length, STATE))]
    return pl.pallas_call(
        functools.partial(back_kernel, group),
        grid=(chunks,),
        in_specs=in_specs,
        out_specs=out_specs,
        out_shape=out_shape,
        scratch_shapes=scratch,
        compiler_params=cparams(),
        cost_estimate=cost(2 * 10**10, 20),
        name="backward",
    )(proj, proj_edge, taps, skip, dy, du, slope, x_act, bc_act, aux, ends, back_states, leaving, *others)


def quarters(left, order):
    rows = left.shape[1] // 4
    block = [lax.dynamic_slice_in_dim(left, order[k] * rows, rows, axis=1) for k in range(4)]
    return jnp.concatenate([block[1], block[3]], axis=1), jnp.concatenate([block[0], block[2]], axis=1)


def weight_grad(parts, right):
    sent, held = parts
    return dot_rows(right, sent).astype(bf16), dot_rows(right, held)


def out_weight_sums(parts, right):
    sent, held = parts
    return dot_rows(sent, right).astype(bf16), dot_rows(held, right)


def input_kernel(
    order, grad_gate, grad_x0, grad_x1, tokens, cot, gain,
    g0, g1, g2, g3, a0, a1, a2, a3, b0, b1, b2, b3, out, gain_grad,
):
    rows = g0.shape[0]

    @pl.when(pl.program_id(0) == 0)
    def _():
        gain_grad[...] = jnp.zeros_like(gain_grad)

    for k, (gate_w, a_w, b_w) in enumerate(((g0, a0, b0), (g1, a1, b1), (g2, a2, b2), (g3, a3, b3))):
        cols = pl.ds(pl.multiple_of(order[k] * rows, rows), rows)
        total = dot_lanes(grad_gate[...], gate_w[...]) + dot_lanes(grad_x0[...], a_w[:, :GW])
        total = total + dot_lanes(grad_x1[:, :GW], b_w[...])
        out[:, cols] = total + dot_lanes(grad_x1[:, GW:], a_w[:, GW:])
    grad = out[...]
    wide = tokens[...].astype(f32)
    width = wide.shape[1]
    scale = lax.rsqrt(jnp.mean(wide * wide, axis=1, keepdims=True) + EPS)
    gain_grad[...] += jnp.sum(grad * wide * scale, axis=0, keepdims=True)
    scaled = grad * gain[...]
    shared = jnp.sum(scaled * wide, axis=1, keepdims=True) / width
    out[...] = cot[...].astype(f32) + (scale * scaled - wide * (scale * scale * scale * shared))


def input_back(order, grad_gate, grad_x0, grad_x1, tokens, cot, gain, gate_pieces, a_pieces, b_pieces):
    length, width = tokens.shape
    rows = width // 4
    return pl.pallas_call(
        input_kernel,
        grid_spec=pltpu.PrefetchScalarGridSpec(
            num_scalar_prefetch=1,
            grid=(length // Q,),
            in_specs=[rows_of(INNER), rows_of(GW), rows_of(GW + REST), rows_of(width), rows_of(width), fixed((1, width))]
            + [fixed((rows, INNER))] * 4
            + [fixed((rows, GW + REST))] * 4
            + [fixed((rows, GW))] * 4,
            out_specs=[rows_of(width), kept((1, width))],
        ),
        out_shape=[shape_of((length, width)), shape_of((1, width))],
        compiler_params=cparams(),
        cost_estimate=cost(2 * length * width * (INNER + XCOLS), 26),
        name="input_back",
    )(order, grad_gate, grad_x0, grad_x1, tokens, cot, gain, *gate_pieces, *a_pieces, *b_pieces)


def swap(value, axis, bit):
    count = lax.axis_size(axis)
    return lax.ppermute(value, axis, [(i, i ^ bit) for i in range(count)])


def exchange(value, axis):
    return lax.all_to_all(value, axis, split_axis=0, concat_axis=0, tiled=True)


def tie(value, *others):
    return lax.optimization_barrier((value, others))[0]


def to_owners(value, groups=1):
    count = lax.axis_size("seq")
    pieces, rows, lanes = value.shape
    if count != pieces:
        lanes //= groups
        width = pieces * lanes // count
        split = value.reshape(pieces, rows, groups, lanes // width, width)
        value = split.transpose(0, 3, 1, 2, 4).reshape(count, rows, groups * width)
    return exchange(value, "seq")


def from_owners(value, groups=1, pieces=PIECES, lanes=128):
    value = exchange(value, "seq")
    count, rows, width = value.shape
    if count == pieces:
        return value
    width //= groups
    split = value.reshape(pieces, lanes // width, rows, groups, width)
    return split.transpose(0, 2, 3, 1, 4).reshape(pieces, rows, groups * lanes)


def send_core(grads):
    sent, held = grads
    return held, swap(sent, "wshard", 1)


def send_x(state, axis=1):
    held, got = state
    own, other = jnp.split(held, 2, axis=axis)
    got_own, got_other = jnp.split(got, 2, axis=axis)
    return (
        own + got_own.astype(f32),
        swap((other + got_other.astype(f32)).astype(bf16), "wshard", 2),
    )


def sum_pair(state):
    mine, got = state
    return (mine + got.astype(f32)).astype(bf16)


def send_near(state):
    mine, got = state
    total = mine + got.astype(f32)
    half = total.shape[0] // 2
    bit = lax.axis_index("seq") & 1
    theirs = lax.dynamic_slice_in_dim(total, (1 - bit) * half, half, axis=0).astype(bf16)
    return lax.dynamic_slice_in_dim(total, bit * half, half, axis=0), swap(theirs, "seq", 1)


def send_far(state):
    mine, got = state
    total = mine + got.astype(f32)
    group = lax.axis_size("seq") // 2
    place = lax.axis_index("seq") >> 1
    part = total.shape[0] // group
    piece = lambda k: lax.dynamic_slice_in_dim(total, (place ^ k) * part, part, axis=0)
    return piece(0), [swap(piece(k).astype(bf16), "seq", 2 * k) for k in range(1, group)]


def share_far(state):
    mine, got = state
    owned = (mine + sum(piece.astype(f32) for piece in got)).astype(bf16)
    return [owned] + [swap(owned, "seq", 2 * k) for k in range(1, len(got) + 1)]


def in_order(pieces, place):
    bit = 1
    while bit < len(pieces):
        odd = (place & bit) != 0
        pieces = [jnp.where(odd, pieces[k ^ bit], pieces[k]) for k in range(len(pieces))]
        bit *= 2
    return jnp.concatenate(pieces, axis=0)


def share_near(pieces):
    half = in_order(pieces, lax.axis_index("seq") >> 1)
    return [half, swap(half, "seq", 1)]


def whole_rows(pieces):
    return in_order(pieces, lax.axis_index("seq") & 1)


def local(
    block_in, norm_gain, in_weight, conv_x, conv_x_bias, conv_bc, conv_bc_bias,
    a_log, skip, dt_bias, out_gain, out_weight, cotangent,
):
    tokens = block_in[0]
    cot = cotangent[0]
    length, width = tokens.shape
    seq = lax.axis_size("seq")
    shards = lax.axis_size("wshard")
    own_heads = HEADS // seq
    own_ch = INNER // seq
    me = lax.axis_index("wshard")
    order = jnp.stack([me ^ k for k in range(4)]).astype(jnp.int32)

    a_piece = jnp.concatenate(
        [in_weight[:, INNER : INNER + GW], jnp.pad(in_weight[:, 2 * INNER :], ((0, 0), (0, XCOLS - XUSED)))], axis=1
    )
    b_piece = in_weight[:, INNER + GW : 2 * INNER]
    gate_piece = in_weight[:, :INNER]
    edge = lax.ppermute(tokens[length - EDGE :], "seq", [(i, i + 1) for i in range(seq - 1)])
    small = jnp.concatenate(
        [
            conv_x,
            conv_x_bias[None],
            jnp.pad(jnp.stack([a_log, skip, dt_bias]), ((0, 0), (0, own_ch - own_heads))),
        ],
        axis=0,
    )
    a_across, a_beside = swap(a_piece, "wshard", 2), swap(a_piece, "wshard", 1)
    small_all = exchange(jnp.broadcast_to(small[None], (seq,) + small.shape), "seq")
    x_params = small_all[:, :5].transpose(1, 0, 2).reshape(5, INNER)
    head_params = small_all[:, 5:, :own_heads].transpose(1, 0, 2).reshape(3, HEADS)
    taps, bias = x_params[:4], x_params[4:5]
    heads = jnp.pad(head_params, ((0, 5), (0, 128 - HEADS)))
    skip_row = jnp.repeat(head_params[1], INNER // HEADS)[None]
    bias_bc = conv_bc_bias[None]
    a_across = tie(a_across, small_all, edge, a_beside)
    a_pieces = (a_piece, a_beside, a_across, swap(a_across, "wshard", 1))
    b_piece, gate_piece, out_piece = tie((b_piece, gate_piece, out_weight), a_across)
    b_across, b_beside = swap(b_piece, "wshard", 2), swap(b_piece, "wshard", 1)

    normed, proj0, rest, proj_edge0, rest_edge = project(order, tokens, edge, norm_gain[None], a_pieces)
    gate_across, gate_beside = swap(gate_piece, "wshard", 2), swap(gate_piece, "wshard", 1)
    out_across, out_beside = swap(out_piece, "wshard", 2), swap(out_piece, "wshard", 1)
    bc_act, aux, cum_t = factors(rest, rest_edge, conv_bc, bias_bc, heads)
    b_across = tie(b_across, bc_act)
    b_pieces = (b_piece, b_beside, b_across, swap(b_across, "wshard", 1))
    x_act0, local0, payload0 = states(0, proj0, proj_edge0, taps, bias, bc_act, aux)
    arrived0 = to_owners(payload0)
    proj1, proj_edge1 = project_more(order, tie(normed, payload0), edge, norm_gain[None], b_pieces)
    x_act1, local1, payload1 = states(1, proj1, proj_edge1, taps, bias, bc_act, aux)
    arrived1 = to_owners(payload1)
    y0 = within(0, tie(x_act0, payload1), bc_act, aux, cum_t, skip_row)
    gate_pieces = (gate_piece, gate_beside, gate_across, swap(gate_across, "wshard", 1))
    gate = gate_project(order, tie(normed, y0), gate_pieces)
    entering0 = chain(True, *tie((arrived0, arrived0[:, STATE:, :]), gate))
    totals0, totals1 = arrived0[:, STATE:, :], arrived1[:, STATE:, :]
    back0 = from_owners(entering0)
    entering1 = chain(True, *tie((arrived1, totals1), entering0))
    back1 = from_owners(entering1)
    y1 = within(1, tie(x_act1, entering1), bc_act, aux, cum_t, skip_row)
    entering0, entering1 = tie((back0, back1), y1)
    out_pieces = (out_piece, out_beside, out_across, swap(out_across, "wshard", 1))
    (normed_out, output, dy, grad_gate, ends, back_states, begin, back_payload, y_dot, out_gain_grad) = middle(
        order, (y0, y1), bc_act, aux, (local0, local1), (entering0, entering1), gate, tokens, cot, out_gain[None], out_pieces
    )

    back_arrived = to_owners(back_payload, 2)
    totals = jnp.concatenate([totals0, totals1], axis=2)
    normed_parts = quarters(normed, order)
    out_grads = out_weight_sums(quarters(normed_out, order), cot)
    out_core = send_core(out_grads)
    gate_grads = weight_grad(normed_parts, tie(grad_gate, out_grads))
    gate_core = send_core(gate_grads)
    du0, slope0, grad_bc0, k_dot0 = within_back(
        0, tie(x_act0, gate_grads), bc_act, aux, cum_t, dy, proj0, proj_edge0, taps, bias, ends, begin
    )
    out_x = send_x(tie(out_core, du0), axis=0)
    gate_x = send_x(tie(gate_core, out_x[0]))
    leaving = chain(False, *tie((back_arrived, totals), gate_x[0]))
    leave = from_owners(leaving, 2)
    du1, slope1, grad_bc1, k_dot1 = within_back(
        1, tie(x_act1, leaving), bc_act, aux, cum_t, dy, proj1, proj_edge1, taps, bias, ends, begin
    )
    out_pair = sum_pair(tie(out_x, du1))
    leave = tie(leave, out_pair)
    grad_x0, grad_taps0, tail0, start0, x_dot0, edge_dot0, b_sum0 = backward(
        0, proj0, proj_edge0, taps, skip_row, dy, du0, slope0, x_act0, bc_act, aux, ends, back_states, leave
    )
    all_taps = jnp.concatenate([taps[:, GW:], conv_bc], axis=1)
    backwards = [(i, i - 1) for i in range(1, seq)]

    def fix(grad, tail, start, tap_values):
        fixes = [
            tail[EDGE - 3 + a] + sum(tap_values[k] * start[a - k] for k in range(a + 1)) for a in range(3)
        ]
        fixed_rows = jnp.concatenate([tail[: EDGE - 3], jnp.stack(fixes)], axis=0).astype(bf16)
        return lax.dynamic_update_slice(grad, fixed_rows, (length - EDGE, 0))

    after0 = lax.ppermute(start0, "seq", backwards)
    gate_pair = sum_pair(tie(gate_x, grad_x0))
    out_sum, gate_sum = lax.psum((out_pair, gate_pair), "seq")
    grad_x0 = fix(tie(grad_x0, gate_pair), tail0, after0, taps[:, :GW])
    x0_grads = weight_grad(normed_parts, grad_x0)
    x0_core = send_core(x0_grads)
    grad_x1, grad_taps1, tail1, start1, grad_taps_bc, grad_heads = backward(
        1, proj1, proj_edge1, taps, skip_row, tie(dy, x0_grads), du1, slope1, x_act1, bc_act, aux, ends, back_states,
        leave,
        (rest, rest, rest_edge, conv_bc, bias_bc, heads, y_dot, k_dot0, k_dot1, x_dot0, edge_dot0, b_sum0, grad_bc0, grad_bc1),
    )
    after1 = lax.ppermute(start1, "seq", backwards)
    x0_x = send_x(tie(x0_core, grad_x1))
    grad_x1 = fix(tie(grad_x1, x0_x[0]), tail1, after1, all_taps)
    x1_grads = weight_grad(normed_parts, grad_x1)
    x1_core = send_core(x1_grads)
    x0_near = send_near(tie(x0_x, x1_grads))
    x1_x = send_x(tie(x1_core, x0_near[0]))
    input_grad, norm_gain_grad = input_back(
        order, tie(grad_gate, x1_x[0]), grad_x0, grad_x1, tokens, cot, norm_gain[None], gate_pieces, a_pieces, b_pieces
    )
    x0_far = send_far(tie(x0_near, input_grad))
    x1_near = send_near(tie(x1_x, x0_far[0]))
    x0_all = share_far(tie(x0_far, x1_near[0]))
    x1_far = send_far(tie(x1_near, x0_all[0]))
    x0_half = share_near(tie(x0_all, x1_far[0]))
    x1_half = share_near(share_far(tie(x1_far, x0_half[0])))

    grad_taps = jnp.concatenate([grad_taps0, grad_taps1], axis=1)
    shared = jnp.concatenate(
        [norm_gain_grad[0], out_gain_grad[0], grad_taps_bc[:5].reshape(-1)]
    )
    mine = jnp.concatenate(
        [
            grad_taps[:5].reshape(5, seq, own_ch).transpose(1, 0, 2).reshape(seq, 5 * own_ch),
            grad_heads[:3, :HEADS].reshape(3, seq, own_heads).transpose(1, 0, 2).reshape(seq, 3 * own_heads),
        ],
        axis=1,
    )
    shared_size, mine_size = shared.shape[0], mine.shape[1]
    pad = -(shared_size + mine_size) % 1024
    small_out = jnp.concatenate(
        [jnp.broadcast_to(shared[None], (seq, shared_size)), mine, jnp.zeros((seq, pad), f32)], axis=1
    )
    small_out = jnp.broadcast_to(small_out[:, None], (seq, shards, small_out.shape[1]))
    small_sum = jnp.sum(
        exchange(small_out.reshape(seq * shards, 8, -1), ("seq", "wshard")), axis=0
    ).reshape(-1)
    out_owned = out_sum.astype(f32)
    in_owned = jnp.concatenate(
        [gate_sum, whole_rows(x0_half), whole_rows(x1_half)[: XUSED - GW]], axis=0
    ).astype(f32).T
    pos = [0]

    def take(shape):
        size = 1
        for extent in shape:
            size *= extent
        out = small_sum[pos[0] : pos[0] + size].reshape(shape)
        pos[0] += size
        return out

    norm_gain_sum = take((width,))
    out_gain_sum = take((INNER,))
    bc_sum = take((5, BC))
    x_sum = take((5, own_ch))
    head_sum = take((3, own_heads))
    return (
        output[None],
        input_grad[None],
        norm_gain_sum,
        in_owned,
        x_sum[:4],
        x_sum[4],
        bc_sum[:4],
        bc_sum[4],
        head_sum[0],
        head_sum[1],
        head_sum[2],
        out_gain_sum,
        out_owned,
    )


def solution(mesh):
    in_specs = (
        P("wshard", "seq", None),
        P(),
        P("wshard", None),
        P(None, "seq"),
        P("seq"),
        P(),
        P(),
        P("seq"),
        P("seq"),
        P("seq"),
        P(),
        P("wshard", None),
        P("wshard", "seq", None),
    )
    out_specs = (
        P("wshard", "seq", None),
        P("wshard", "seq", None),
        P(),
        P("wshard", None),
        P(None, "seq"),
        P("seq"),
        P(),
        P(),
        P("seq"),
        P("seq"),
        P("seq"),
        P(),
        P("wshard", None),
    )
    return jax.shard_map(local, mesh=mesh, in_specs=in_specs, out_specs=out_specs, check_vma=False)
```

time: 648 us -> 533 us (0.82)
  waiting for transfers between devices: 182 us -> 106 us
  Pallas kernels: 277 us -> 230 us
  other arithmetic: 42.5 us -> 26.2 us
  between operations: 1.57 us -> 15.4 us
  local copies, waits for them, and re-layouts: 39.3 us -> 27.2 us
  starting transfers between devices: 78 us -> 89.6 us
  matrix products: 20.8 us -> 29.6 us
    ppermute x21 -> x36, waiting for transfers between devices: 118 us -> 68.6 us  [swap(): return lax.ppermute(value, axis, [(i, i ^ bit) for i in range(count)])]
    all_to_all x6 -> x0, waiting for transfers between devices: 48.2 us -> none  [sum_to_rows(): lax.all_to_all(v, 'seq', split_axis=0, concat_axis=0, tiled=True, axis_in...]
    pallas_call x4 -> x10, Pallas kernels: 173 us -> 144 us  [the longest x2 49.8 us: backward(): pl.pallas_call(functools.partial(back_kernel, group), grid=(chunks,), in_...]
    all_to_all x6 -> x0, starting transfers between devices: 24.6 us -> none  [sum_to_rows(): lax.all_to_all(v, 'seq', split_axis=0, concat_axis=0, tiled=True, axis_in...]
    ppermute x21 -> x36, starting transfers between devices: 19 us -> 41.1 us  [swap(): return lax.ppermute(value, axis, [(i, i ^ bit) for i in range(count)])]
    psum x0 -> x1, waiting for transfers between devices: none -> 16 us  [local(): out_sum, gate_sum = lax.psum((out_pair, gate_pair), 'seq')]
    pallas_call x1, Pallas kernels: 58.5 us -> 42.7 us  [middle(): pl.pallas_call(middle_kernel, grid_spec=pltpu.PrefetchScalarGridSpec(num_...]
    unnamed x70 -> x91, local copies, waits for them, and re-layouts: 21.5 us -> 6.45 us
  transfers between devices with their start and end apart: 35 -> 48, of which waited for: 16 -> 18; matrix products, arithmetic and copies ran while one was open for 11% -> 11% of each run, Pallas kernels for 27% -> 35%
where the time goes in v2:
time: 533 us; the launch traced here: 524 us
  Pallas kernels  230 us (43%)
  waiting for transfers between devices  106 us (20%)
  starting transfers between devices  89.6 us (17%)
  matrix products  29.6 us (6%)
  local copies, waits for them, and re-layouts  27.2 us (5%)
  other arithmetic  26.2 us (5%)
  between operations  15.4 us (3%)
    ppermute x36, waiting for transfers between devices, swap(): return lax.ppermute(value, axis, [(i, i ^ bit) for i in range(count)])  68.6 us
    pallas_call x2, Pallas kernels, backward(): pl.pallas_call(functools.partial(back_kernel, group), grid=(chunks,), in_...  49.8 us
    pallas_call x1, Pallas kernels, middle(): pl.pallas_call(middle_kernel, grid_spec=pltpu.PrefetchScalarGridSpec(num_...  42.7 us
    all_to_all x8, starting transfers between devices, exchange(): return lax.all_to_all(value, axis, split_axis=0, concat_axis=0, tiled=True)  41.8 us
    ppermute x36, starting transfers between devices, swap(): return lax.ppermute(value, axis, [(i, i ^ bit) for i in range(count)])  41.1 us
    pallas_call x2, Pallas kernels, within_back(): pl.pallas_call(functools.partial(within_back_kernel, group), grid=(length...  37.8 us
    dot_general x8, matrix products, dot_rows(): lax.dot_general(a, b, (((0,), (0,)), ((), ())), preferred_element_type=f32)  29.6 us
    pallas_call x2, Pallas kernels, within(): pl.pallas_call(functools.partial(within_kernel, group), grid=(length // Q...  22.8 us
  transfers between devices with their start and end apart: 48, of which 18 were waited for; matrix products, arithmetic and copies ran while one was open for 11% of the time, Pallas kernels for 35%

profile of v2, /device:TPU:0, one launch (start us, length us, event | category | flops | bytes accessed | tf_op | source)
XLA Modules:
  0.0 524.0 jit_solution(10274752049701540485)
XLA Ops:
  36.4 8.7 %project.1 = (bf16[1024,1024]{1,0:T(8,128)(2,1)}, bf16[1024,1024]{1,0:T(8,128)(2,1)}, bf16[1024,384]{1,0:T(8,128)(2,1)}, bf16[16,1024]{1,0:T(8,128)(2,1)}, bf16[16,384]{1,0:T(8,128)(2,1)}) custom-call(s32[4]{0:T(128)} %pad_add_fusion.order, bf16[1024,1024]{1,0:T(8,128)(2,1)} %bitcast.46, bf16[16,1024]{1,0:T(8,128)(2,1)} %copy-done.31, f32[1,1024]{1,0:T(1,128)} %bitcast.66, ...), custom_call_target="tpu_custom_call" | custom-call | flops 59055800 | bytes 188743 | tf_op jit(solution)/shard_map/project/pallas_call | solution.py:199
  50.2 10.5 %states.2 = (f32[1024,1024]{1,0:T(8,128)}, f32[4,4,128,256]{3,2,1,0:T(8,128)}, f32[8,136,128]{2,1,0:T(8,128)}) custom-call(bf16[1024,1024]{1,0:T(8,128)(2,1)} %get-tuple-element.120.now.prior, bf16[1024,1024]{1,0:T(8,128)(2,1)} %get-tuple-element.120.now.prior, bf16[16,1024]{1,0:T(8,128)(2,1)} %get-tuple-element.121.edge, f32[4,2048]{1,0:T(4,128)} %bitcast.51, ...), custom_call_target="tpu_custom_call" | custom-call | flops 200000000 | bytes 209715 | tf_op jit(solution)/shard_map/states/pallas_call | solution.py:353
  60.7 6.1 %all-to-all-start.2 = ((f32[8,136,128]{2,1,0:T(8,128)}), f32[8,136,128]{2,1,0:T(8,128)S(1)}, u32[]{:S(2)}, u32[]{:S(2)}) async-start(f32[8,136,128]{2,1,0:T(8,128)} %get-tuple-element.128), calls=%async_computation.2 | async-start | bytes 1114112 | tf_op jit(solution)/shard_map/all_to_all | solution.py:946
  71.3 7.2 %project_more.1 = (bf16[1024,1024]{1,0:T(8,128)(2,1)}, bf16[16,1024]{1,0:T(8,128)(2,1)}) custom-call(s32[4]{0:T(128)} %pad_add_fusion.order, bf16[1024,1024]{1,0:T(8,128)(2,1)} %get-tuple-element.138.normed, bf16[16,1024]{1,0:T(8,128)(2,1)} %copy-done.31, f32[1,1024]{1,0:T(1,128)} %bitcast.67, bf16[256,1024]{1,0:T(8,128)(2,1)} %copy-done.6, ...), custom_call_target="tpu_custom_call" | custom-call | flops 42949672 | bytes 125829 | tf_op jit(solution)/shard_map/project_more/pallas_call | solution.py:224
  78.5 10.5 %states.3 = (f32[1024,1024]{1,0:T(8,128)}, f32[4,4,128,256]{3,2,1,0:T(8,128)}, f32[8,136,128]{2,1,0:T(8,128)}) custom-call(bf16[1024,1024]{1,0:T(8,128)(2,1)} %get-tuple-element.132.now.prior, bf16[1024,1024]{1,0:T(8,128)(2,1)} %get-tuple-element.132.now.prior, bf16[16,1024]{1,0:T(8,128)(2,1)} %get-tuple-element.133.edge, f32[4,2048]{1,0:T(4,128)} %bitcast.52, ...), custom_call_target="tpu_custom_call" | custom-call | flops 200000000 | bytes 209715 | tf_op jit(solution)/shard_map/states/pallas_call | solution.py:353
  89.0 6.2 %all-to-all-start.1 = ((f32[8,136,128]{2,1,0:T(8,128)}), f32[8,136,128]{2,1,0:T(8,128)}, u32[]{:S(2)}, u32[]{:S(2)}) async-start(f32[8,136,128]{2,1,0:T(8,128)} %get-tuple-element.134), calls=%async_computation.1 | async-start | bytes 1114112 | tf_op jit(solution)/shard_map/all_to_all | solution.py:946
  97.6 11.5 %within.2.y_in0 = f32[1024,1024]{1,0:T(8,128)} custom-call(f32[1024,1024]{1,0:T(8,128)} %get-tuple-element.155.x_act, f32[1024,256]{1,0:T(8,128)} %get-tuple-element.124.bc_act, f32[1024,128]{1,0:T(8,128)} %get-tuple-element.125.aux, f32[32,1024]{1,0:T(8,128)} %get-tuple-element.136.cum_t, f32[1,2048]{1,0:T(1,128)} %broadcast_in_dim_reshape.3.skip), custom_call_target="tpu_custom_call" | custom-call | flops 200000000 | bytes 209715 | tf_op jit(solution)/shard_map/within/pallas_call | solution.py:459
  109.8 9.5 %gate_project.1.gate = bf16[1024,2048]{1,0:T(8,128)(2,1)} custom-call(s32[4]{0:T(128)} %pad_add_fusion.order, bf16[1024,1024]{1,0:T(8,128)(2,1)} %get-tuple-element.138.normed, bf16[256,2048]{1,0:T(8,128)(2,1)} %copy-done.2, bf16[256,2048]{1,0:T(8,128)(2,1)} %collective-permute-done.7.w1.g1, bf16[256,2048]{1,0:T(8,128)(2,1)} %copy-done.11, ...), custom_call_target="tpu_custom_call" | custom-call | flops 85899344 | bytes 209715 | tf_op jit(solution)/shard_map/gate_project/pallas_call | solution.py:253
  131.1 10.3 %all-to-all-done.3.entering0 = f32[8,128,128]{2,1,0:T(8,128)S(1)} async-done(((f32[8,128,128]{2,1,0:T(8,128)}), f32[8,128,128]{2,1,0:T(8,128)S(1)}, u32[]{:S(2)}, u32[]{:S(2)}) %all-to-all-start.3) | async-done | bytes 524320 | tf_op jit(solution)/shard_map/all_to_all | solution.py:946
  146.5 11.3 %within.3.y_in1 = f32[1024,1024]{1,0:T(8,128)} custom-call(f32[1024,1024]{1,0:T(8,128)} %get-tuple-element.168.x_act, f32[1024,256]{1,0:T(8,128)} %get-tuple-element.124.bc_act, f32[1024,128]{1,0:T(8,128)} %get-tuple-element.125.aux, f32[32,1024]{1,0:T(8,128)} %get-tuple-element.136.cum_t, f32[1,2048]{1,0:T(1,128)} %broadcast_in_dim_reshape.3.skip), custom_call_target="tpu_custom_call" | custom-call | flops 200000000 | bytes 209715 | tf_op jit(solution)/shard_map/within/pallas_call | solution.py:459
  160.2 42.7 %middle.1 = (bf16[1024,2048]{1,0:T(8,128)(2,1)}, bf16[1024,1024]{1,0:T(8,128)(2,1)}, bf16[1024,2048]{1,0:T(8,128)(2,1)}, bf16[1024,2048]{1,0:T(8,128)(2,1)}, f32...) custom-call(s32[4]{0:T(128)} %pad_add_fusion.order, ...), custom_call_target="tpu_custom_call" | custom-call | flops 800000000 | bytes 838860 | tf_op jit(solution)/shard_map/middle/pallas_call | solution.py:684
  223.4 6.8 %fusion.16 = f32[2048,512]{1,0:T(8,128)} fusion(bf16[1024,2048]{1,0:T(8,128)(2,1)} %get-tuple-element.199.grad_gate, bf16[1024,256]{1,0:T(8,128)(2,1)} %get-tuple-element.242, bf16[1024,256]{1,0:T(8,128)(2,1)} %get-tuple-element.241), kind=kOutput, calls=%fused_computation.41 | convolution fusion | flops 2149580800 | bytes 9437184 | tf_op jit(solution)/shard_map/dot_general | solution.py:50
  230.2 18.8 %within_back.2 = (bf16[1024,1024]{1,0:T(8,128)(2,1)}, bf16[1024,1024]{1,0:T(8,128)(2,1)}, f32[1024,256]{1,0:T(8,128)}, f32[1024,128]{1,0:T(8,128)}) custom-call(f32[1024,1024]{1,0:T(8,128)} %get-tuple-element.155.x_act, f32[1024,256]{1,0:T(8,128)} %get-tuple-element.124.bc_act, f32[1024,128]{1,0:T(8,128)} %get-tuple-element.125.aux, ...), custom_call_target="tpu_custom_call" | custom-call | flops 400000000 | bytes 293601 | tf_op jit(solution)/shard_map/within_back/pallas_call | solution.py:559
  266.5 19.1 %within_back.3 = (bf16[1024,1024]{1,0:T(8,128)(2,1)}, bf16[1024,1024]{1,0:T(8,128)(2,1)}, f32[1024,256]{1,0:T(8,128)}, f32[1024,128]{1,0:T(8,128)}) custom-call(f32[1024,1024]{1,0:T(8,128)} %get-tuple-element.168.x_act, f32[1024,256]{1,0:T(8,128)} %get-tuple-element.124.bc_act, f32[1024,128]{1,0:T(8,128)} %get-tuple-element.125.aux, ...), custom_call_target="tpu_custom_call" | custom-call | flops 400000000 | bytes 293601 | tf_op jit(solution)/shard_map/within_back/pallas_call | solution.py:559
  293.1 21.7 %backward.2 = (bf16[1024,1024]{1,0:T(8,128)(2,1)}, f32[8,1024]{1,0:T(8,128)}, f32[16,1024]{1,0:T(8,128)}, f32[8,1024]{1,0:T(8,128)}, f32[1024,128]{1,0:T(8,128)}...) custom-call(bf16[1024,1024]{1,0:T(8,128)(2,1)} %get-tuple-element.120.now.prior, bf16[16,1024]{1,0:T(8,128)(2,1)} %get-tuple-element.121.edge, ...), custom_call_target="tpu_custom_call" | custom-call | flops 400000000 | bytes 419430 | tf_op jit(solution)/shard_map/backward/pallas_call | solution.py:865
  327.0 28.1 %backward.3 = (bf16[1024,1408]{1,0:T(8,128)(2,1)}, f32[8,1024]{1,0:T(8,128)}, f32[16,1280]{1,0:T(8,128)}, f32[8,1280]{1,0:T(8,128)}, f32[8,256]{1,0:T(8,128)}, /*index=5*/f32[8,128]{1,0:T(8,128)}) custom-call(bf16[1024,1024]{1,0:T(8,128)(2,1)} %get-tuple-element.132.now.prior, bf16[16,1024]{1,0:T(8,128)(2,1)} %get-tuple-element.133.edge, ...), custom_call_target="tpu_custom_call" | custom-call | flops 400000000 | bytes 419430 | tf_op jit(solution)/shard_map/backward/pallas_call | solution.py:865
  372.9 10.1 %collective-permute-done.21 = bf16[1024,256]{1,0:T(8,128)(2,1)} collective-permute-done((bf16[1024,256]{1,0:T(8,128)(2,1)S(1)}, bf16[1024,256]{1,0:T(8,128)(2,1)}, u32[]{:S(2)}, u32[]{:S(2)}) %collective-permute-start.21) | collective-permute-done | bytes 524320 | tf_op jit(solution)/shard_map/ppermute | solution.py:942
  389.8 19.4 %input_back.1 = (f32[1024,1024]{1,0:T(8,128)}, f32[1,1024]{1,0:T(1,128)}) custom-call(s32[4]{0:T(128)} %pad_add_fusion.order, bf16[1024,2048]{1,0:T(8,128)(2,1)} %get-tuple-element.199.grad_gate, bf16[1024,1024]{1,0:T(8,128)(2,1)} %maximum_dynamic-update-slice_fusion.1.grad_x0, bf16[1024,1408]{1,0:T(8,128)(2,1)} %copy-done.14, bf16[1024,1024]{1,0:T(8,128)(2,1)} %bitcast.48, ...), custom_call_target="tpu_custom_call" | custom-call | flops 187904816 | bytes 545259 | tf_op jit(solution)/shard_map/input_back/pallas_call | solution.py:922
  428.2 14.2 %collective-permute-done.30 = bf16[704,256]{1,0:T(8,128)(2,1)S(1)} collective-permute-done((bf16[704,256]{1,0:T(8,128)(2,1)S(1)}, bf16[704,256]{1,0:T(8,128)(2,1)S(1)}, u32[]{:S(2)}, u32[]{:S(2)}) %collective-permute-start.30) | collective-permute-done | bytes 360480 | tf_op jit(solution)/shard_map/ppermute | solution.py:942
  442.5 8.8 %collective-permute-done.28 = bf16[128,256]{1,0:T(8,128)(2,1)S(1)} collective-permute-done((bf16[128,256]{1,0:T(8,128)(2,1)S(1)}, bf16[128,256]{1,0:T(8,128)(2,1)S(1)}, u32[]{:S(2)}, u32[]{:S(2)}) %collective-permute-start.28) | collective-permute-done | bytes 65568 | tf_op jit(solution)/shard_map/ppermute | solution.py:942
  457.4 11.5 %collective-permute-done.33 = bf16[176,256]{1,0:T(8,128)(2,1)S(1)} collective-permute-done((bf16[176,256]{1,0:T(8,128)(2,1)S(1)}, bf16[176,256]{1,0:T(8,128)(2,1)S(1)}, u32[]{:S(2)}, u32[]{:S(2)}) %collective-permute-start.33) | collective-permute-done | bytes 90144 | tf_op jit(solution)/shard_map/ppermute | solution.py:942
  470.1 8.2 %collective-permute-start.36 = (bf16[176,256]{1,0:T(8,128)(2,1)S(1)}, bf16[176,256]{1,0:T(8,128)(2,1)S(1)}, u32[]{:S(2)}, u32[]{:S(2)}) collective-permute-start(bf16[176,256]{1,0:T(8,128)(2,1)S(1)} %add_convert_fusion.6), channel_id=1, source_target_pairs={{0,16},{4,20},{8,24},{12,28},{16,0},{20,4},{24,8},{28,12},{1,17},{... | collective-permute-start | bytes 270344 | tf_op jit(solution)/shard_map/ppermute | solution.py:942
  478.4 16.0 %all-reduce.6.cloned.1.call-done = (bf16[2048,256]{1,0:T(8,128)(2,1)}, bf16[512,1024]{1,0:T(8,128)(2,1)}) async-done(((bf16[2048,256]{1,0:T(8,128)(2,1)}, bf16[512,1024]{1,0:T(8,128)(2,1)}), (bf16[2048,256]{1,0:T(8,128)(2,1)}, bf16[512,1024]{1,0:T(8,128)(2,1)})) %all-reduce.6.cloned.1.call-update) | async-done | bytes 2097168 | tf_op jit(solution)/shard_map/psum | solution.py:1138
  499.3 7.0 %collective-permute-done.31 = bf16[512,256]{1,0:T(8,128)(2,1)S(1)} collective-permute-done((bf16[512,256]{1,0:T(8,128)(2,1)S(1)}, bf16[512,256]{1,0:T(8,128)(2,1)S(1)}, u32[]{:S(2)}, u32[]{:S(2)}) %collective-permute-start.31) | collective-permute-done | bytes 262176 | tf_op jit(solution)/shard_map/ppermute | solution.py:942
  (274 shorter events, 184.6 us)
Async XLA Ops:
  32.4 34.4 %collective-permute-start.5 = (bf16[256,1024]{1,0:T(8,128)(2,1)S(1)}, bf16[256,1024]{1,0:T(8,128)(2,1)}, u32[]{:S(2)}, u32[]{:S(2)}) collective-permute-start(bf16[256,1024]{1,0:T(8,128)(2,1)S(1)} %copy.56.w0.b0), channel_id=1, source_target_pairs={{0,2},{1,3},{2,0},{3,1},{4,6},{5,7},{6,4},{7,5},{8,10},{9,11},{10,... | collective-permute-start | bytes 1572872 | tf_op jit(solution)/shard_map/ppermute | solution.py:942
  34.2 35.1 %collective-permute-start.8 = (bf16[256,2048]{1,0:T(8,128)(2,1)S(1)}, bf16[256,2048]{1,0:T(8,128)(2,1)S(1)}, u32[]{:S(2)}, u32[]{:S(2)}) collective-permute-start(bf16[256,2048]{1,0:T(8,128)(2,1)S(1)} %copy.57.w0.g0), channel_id=1, source_target_pairs={{0,2},{1,3},{2,0},{3,1},{4,6},{5,7},{6,4},{7,5},{8,10},{9,11},{10,... | collective-permute-start | bytes 3145736 | tf_op jit(solution)/shard_map/ppermute | solution.py:942
  60.7 28.3 %all-to-all-start.2 = ((f32[8,136,128]{2,1,0:T(8,128)}), f32[8,136,128]{2,1,0:T(8,128)S(1)}, u32[]{:S(2)}, u32[]{:S(2)}) async-start(f32[8,136,128]{2,1,0:T(8,128)} %get-tuple-element.128), calls=%async_computation.2 | async-start | bytes 1114112 | tf_op jit(solution)/shard_map/all_to_all | solution.py:946
  67.4 42.4 %collective-permute-start.7 = (bf16[256,2048]{1,0:T(8,128)(2,1)S(1)}, bf16[256,2048]{1,0:T(8,128)(2,1)}, u32[]{:S(2)}, u32[]{:S(2)}) collective-permute-start(bf16[256,2048]{1,0:T(8,128)(2,1)S(1)} %copy.57.w0.g0), channel_id=1, source_target_pairs={{0,1},{1,0},{2,3},{3,2},{4,5},{5,4},{6,7},{7,6},{8,9},{9,8},{10,11... | collective-permute-start | bytes 3145736 | tf_op jit(solution)/shard_map/ppermute | solution.py:942
  69.3 40.5 %collective-permute-start.9 = (bf16[256,2048]{1,0:T(8,128)(2,1)S(1)}, bf16[256,2048]{1,0:T(8,128)(2,1)}, u32[]{:S(2)}, u32[]{:S(2)}) collective-permute-start(bf16[256,2048]{1,0:T(8,128)(2,1)S(1)} %collective-permute-done.8.w2.g2), channel_id=1, source_target_pairs={{0,1},{1,0},{2,3},{3,2},{4,5},{5,4},{6,7},{7,6},{8,9},{9,8},{10,11... | collective-permute-start | bytes 3145736 | tf_op jit(solution)/shard_map/ppermute | solution.py:942
  89.0 32.3 %all-to-all-start.1 = ((f32[8,136,128]{2,1,0:T(8,128)}), f32[8,136,128]{2,1,0:T(8,128)}, u32[]{:S(2)}, u32[]{:S(2)}) async-start(f32[8,136,128]{2,1,0:T(8,128)} %get-tuple-element.134), calls=%async_computation.1 | async-start | bytes 1114112 | tf_op jit(solution)/shard_map/all_to_all | solution.py:946
  95.2 32.1 %collective-permute-start.11 = (bf16[512,1024]{1,0:T(8,128)(2,1)}, bf16[512,1024]{1,0:T(8,128)(2,1)}, u32[]{:S(2)}, u32[]{:S(2)}) collective-permute-start(bf16[512,1024]{1,0:T(8,128)(2,1)} %w0), channel_id=1, source_target_pairs={{0,2},{1,3},{2,0},{3,1},{4,6},{5,7},{6,4},{7,5},{8,10},{9,11},{10,... | collective-permute-start | bytes 3145736 | tf_op jit(solution)/shard_map/ppermute | solution.py:942
  127.3 32.0 %collective-permute-start.10 = (bf16[512,1024]{1,0:T(8,128)(2,1)}, bf16[512,1024]{1,0:T(8,128)(2,1)}, u32[]{:S(2)}, u32[]{:S(2)}) collective-permute-start(bf16[512,1024]{1,0:T(8,128)(2,1)} %w0), channel_id=1, source_target_pairs={{0,1},{1,0},{2,3},{3,2},{4,5},{5,4},{6,7},{7,6},{8,9},{9,8},{10,11... | collective-permute-start | bytes 3145736 | tf_op jit(solution)/shard_map/ppermute | solution.py:942
  127.4 32.0 %collective-permute-start.12 = (bf16[512,1024]{1,0:T(8,128)(2,1)}, bf16[512,1024]{1,0:T(8,128)(2,1)}, u32[]{:S(2)}, u32[]{:S(2)}) collective-permute-start(bf16[512,1024]{1,0:T(8,128)(2,1)} %collective-permute-done.11.w2), channel_id=1, source_target_pairs={{0,1},{1,0},{2,3},{3,2},{4,5},{5,4},{6,7},{7,6},{8,9},{9,8},{10,11... | collective-permute-start | bytes 3145736 | tf_op jit(solution)/shard_map/ppermute | solution.py:942
  209.4 39.6 %collective-permute-start.14 = (bf16[1024,1024]{1,0:T(8,128)(2,1)}, bf16[1024,1024]{1,0:T(8,128)(2,1)S(1)}, u32[]{:S(2)}, u32[]{:S(2)}) collective-permute-start(bf16[1024,1024]{1,0:T(8,128)(2,1)} %fusion.9), channel_id=1, source_target_pairs={{0,1},{1,0},{2,3},{3,2},{4,5},{5,4},{6,7},{7,6},{8,9},{9,8},{10,11... | collective-permute-start | bytes 6291464 | tf_op jit(solution)/shard_map/ppermute | solution.py:942
  217.6 34.0 %collective-permute-start.13 = (bf16[2048,512]{1,0:T(8,128)(2,1)}, bf16[2048,512]{1,0:T(8,128)(2,1)}, u32[]{:S(2)}, u32[]{:S(2)}) collective-permute-start(bf16[2048,512]{1,0:T(8,128)(2,1)} %convolution_convert_fusion), channel_id=1, source_target_pairs={{0,1},{1,0},{2,3},{3,2},{4,5},{5,4},{6,7},{7,6},{8,9},{9,8},{10,11... | collective-permute-start | bytes 6291464 | tf_op jit(solution)/shard_map/ppermute | solution.py:942
  218.1 37.0 %all-to-all-start.5 = ((f32[8,128,256]{2,1,0:T(8,128)}), f32[8,128,256]{2,1,0:T(8,128)S(1)}, u32[]{:S(2)}, u32[]{:S(2)}) async-start(f32[8,128,256]{2,1,0:T(8,128)} %get-tuple-element.161), calls=%async_computation.5 | async-start | bytes 2097152 | tf_op jit(solution)/shard_map/all_to_all | solution.py:946
  258.3 33.8 %all-to-all-start.6 = ((f32[8,128,256]{2,1,0:T(8,128)}), f32[8,128,256]{2,1,0:T(8,128)S(1)}, u32[]{:S(2)}, u32[]{:S(2)}) async-start(f32[8,128,256]{2,1,0:T(8,128)} %chain.5), calls=%async_computation.6 | async-start | bytes 2097152 | tf_op jit(solution)/shard_map/all_to_all | solution.py:946
  264.3 230.0 %all-reduce.6.cloned.1.call-start = ((), (), s32[]{:S(2)}) async-start(), calls=%async_computation.8 | async-start | bytes 4194304 | tf_op jit(solution)/shard_map/psum | solution.py:1138
  264.4 26.4 %collective-permute-start.15 = (bf16[512,1024]{1,0:T(8,128)(2,1)}, bf16[512,1024]{1,0:T(8,128)(2,1)S(1)}, u32[]{:S(2)}, u32[]{:S(2)}) collective-permute-start(bf16[512,1024]{1,0:T(8,128)(2,1)} %get-tuple-element.229), channel_id=1, source_target_pairs={{0,2},{1,3},{2,0},{3,1},{4,6},{5,7},{6,4},{7,5},{8,10},{9,11},{10,... | collective-permute-start | bytes 3145736 | tf_op jit(solution)/shard_map/ppermute | solution.py:942
  265.0 49.8 %collective-permute-start.16 = (bf16[2048,256]{1,0:T(8,128)(2,1)}, bf16[2048,256]{1,0:T(8,128)(2,1)}, u32[]{:S(2)}, u32[]{:S(2)}) collective-permute-start(bf16[2048,256]{1,0:T(8,128)(2,1)} %get-tuple-element.227), channel_id=1, source_target_pairs={{0,2},{1,3},{2,0},{3,1},{4,6},{5,7},{6,4},{7,5},{8,10},{9,11},{10,... | collective-permute-start | bytes 3145736 | tf_op jit(solution)/shard_map/ppermute | solution.py:942
  325.6 38.3 %collective-permute-start.18 = (bf16[1024,512]{1,0:T(8,128)(2,1)S(1)}, bf16[1024,512]{1,0:T(8,128)(2,1)S(1)}, u32[]{:S(2)}, u32[]{:S(2)}) collective-permute-start(bf16[1024,512]{1,0:T(8,128)(2,1)S(1)} %convolution_convert_fusion.2), channel_id=1, source_target_pairs={{0,1},{1,0},{2,3},{3,2},{4,5},{5,4},{6,7},{7,6},{8,9},{9,8},{10,11... | collective-permute-start | bytes 3145736 | tf_op jit(solution)/shard_map/ppermute | solution.py:942
  384.9 24.2 %collective-permute-start.22 = (bf16[512,256]{1,0:T(8,128)(2,1)}, bf16[512,256]{1,0:T(8,128)(2,1)}, u32[]{:S(2)}, u32[]{:S(2)}) collective-permute-start(bf16[512,256]{1,0:T(8,128)(2,1)} %dynamic-slice_convert_fusion.1), channel_id=1, source_target_pairs={{0,4},{4,0},{8,12},{12,8},{16,20},{20,16},{24,28},{28,24},{1,5},{5... | collective-permute-start | bytes 786440 | tf_op jit(solution)/shard_map/ppermute | solution.py:942
  389.0 31.3 %collective-permute-start.26 = (bf16[1408,256]{1,0:T(8,128)(2,1)}, bf16[1408,256]{1,0:T(8,128)(2,1)}, u32[]{:S(2)}, u32[]{:S(2)}) collective-permute-start(bf16[1408,256]{1,0:T(8,128)(2,1)} %get-tuple-element.231), channel_id=1, source_target_pairs={{0,2},{1,3},{2,0},{3,1},{4,6},{5,7},{6,4},{7,5},{8,10},{9,11},{10,... | collective-permute-start | bytes 2162696 | tf_op jit(solution)/shard_map/ppermute | solution.py:942
  416.9 89.5 %all-to-all-start.7 = ((f32[32,8,768]{2,1,0:T(8,128)}), f32[32,8,768]{2,1,0:T(8,128)S(1)}, u32[]{:S(2)}, u32[]{:S(2)}) async-start(f32[32,8,768]{2,1,0:T(8,128)} %reshape.86), calls=%async_computation.7 | async-start | bytes 1572864 | tf_op jit(solution)/shard_map/all_to_all | solution.py:946
  425.2 26.0 %collective-permute-start.28 = (bf16[128,256]{1,0:T(8,128)(2,1)S(1)}, bf16[128,256]{1,0:T(8,128)(2,1)S(1)}, u32[]{:S(2)}, u32[]{:S(2)}) collective-permute-start(bf16[128,256]{1,0:T(8,128)(2,1)S(1)} %add_convert_fusion.7), channel_id=1, source_target_pairs={{0,16},{4,20},{8,24},{12,28},{16,0},{20,4},{24,8},{28,12},{1,17},{... | collective-permute-start | bytes 196616 | tf_op jit(solution)/shard_map/ppermute | solution.py:942
  427.7 23.6 %collective-permute-start.29 = (bf16[128,256]{1,0:T(8,128)(2,1)S(1)}, bf16[128,256]{1,0:T(8,128)(2,1)S(1)}, u32[]{:S(2)}, u32[]{:S(2)}) collective-permute-start(bf16[128,256]{1,0:T(8,128)(2,1)S(1)} %add_convert_fusion.7), channel_id=1, source_target_pairs={{0,24},{4,28},{8,16},{12,20},{16,8},{20,12},{24,0},{28,4},{1,25},{... | collective-permute-start | bytes 196616 | tf_op jit(solution)/shard_map/ppermute | solution.py:942
  468.9 29.8 %collective-permute-start.35 = (bf16[176,256]{1,0:T(8,128)(2,1)S(1)}, bf16[176,256]{1,0:T(8,128)(2,1)S(1)}, u32[]{:S(2)}, u32[]{:S(2)}) collective-permute-start(bf16[176,256]{1,0:T(8,128)(2,1)S(1)} %add_convert_fusion.6), channel_id=1, source_target_pairs={{0,24},{4,28},{8,16},{12,20},{16,8},{20,12},{24,0},{28,4},{1,25},{... | collective-permute-start | bytes 270344 | tf_op jit(solution)/shard_map/ppermute | solution.py:942
  470.1 28.7 %collective-permute-start.36 = (bf16[176,256]{1,0:T(8,128)(2,1)S(1)}, bf16[176,256]{1,0:T(8,128)(2,1)S(1)}, u32[]{:S(2)}, u32[]{:S(2)}) collective-permute-start(bf16[176,256]{1,0:T(8,128)(2,1)S(1)} %add_convert_fusion.6), channel_id=1, source_target_pairs={{0,16},{4,20},{8,24},{12,28},{16,0},{20,4},{24,8},{28,12},{1,17},{... | collective-permute-start | bytes 270344 | tf_op jit(solution)/shard_map/ppermute | solution.py:942
  (70 other events, 749.6 us)
Sparse Core Ops, SparseCore 0:
  369.3 125.0 all-reduce.5

commit v3 on v2

--- a/solution.py
+++ b/solution.py
@@ -93,6 +93,18 @@
     a_high, a_low = halves(a)
     b_high, b_low = halves(b)
     return product(a_high, b_high) + (product(a_high, b_low) + product(a_low, b_high))
+
+
+def fine_with(product, a_terms, b):
+    a_high, a_low = a_terms
+    b_high, b_low = halves(b)
+    return product(a_high, b_high) + (product(a_high, b_low) + product(a_low, b_high))
+
+
+def fine_short(a_terms, b):
+    a_high, a_both = a_terms
+    b_high, b_low = halves(b)
+    return dot(a_both, jnp.concatenate([b_high, b_high], axis=0)) + dot(a_high, b_low)
 
 
 def head_select(tile):
@@ -604,8 +616,9 @@
         gain_grad[...] = jnp.zeros_like(gain_grad)
 
     keep = aux[...]
-    c_cols = bc_act[:, STATE:]
-    c_rows = bc_act[:, STATE:].T
+    c_high, c_low = halves(bc_act[:, STATE:])
+    c_cols = (c_high, jnp.concatenate([c_high, c_low], axis=1))
+    c_rows = halves(bc_act[:, STATE:].T)
 
     decayed2 = terms2(keep[:, 3 * HEADS :])
     ends4 = terms4(jnp.concatenate([keep[Q - 8 :, 3 * HEADS :], keep[Q - 8 :, :HEADS]], axis=0))
@@ -613,7 +626,7 @@
     def mix(y_in, local, shift, place, squares):
         j = place + shift
         cols = tile_at(j)
-        carried = fine(dot, c_cols, state[j])
+        carried = fine_short(c_cols, state[j])
         y = y_in[:, tile_at(place)] + dot(decayed2, spread(2, TILE, 4 * j, 6)) * carried
         y_keep[:, cols] = y
         raw = gate[:, cols].astype(f32)
@@ -641,7 +654,7 @@
         both = grad * gains * gated
         return products + (both[:, :128] + both[:, 128:])
 
-    products = lax.fori_loop(0, TILES, back_out, jnp.zeros((Q, 128), f32), unroll=4)
+    products = lax.fori_loop(0, TILES, back_out, jnp.zeros((Q, 128), f32), unroll=8)
     shared = jnp.sum(products, axis=1, keepdims=True) / INNER * (scale * scale * scale)
     for start in range(0, output.shape[1], TILE):
         cols = slice(start, start + TILE)
@@ -659,13 +672,13 @@
         mixed = y.astype(bf16).astype(f32)
         grad_gate[:, cols] = (grad_gated * mixed * (sig * (1.0 + raw * (1.0 - sig)))).astype(bf16)
         wide = dy.astype(f32)
-        piece = fine(dot, c_rows, wide * dot(decayed2, spread(2, TILE, 4 * j, 6)))
+        piece = fine_with(dot, c_rows, wide * dot(decayed2, spread(2, TILE, 4 * j, 6)))
         back_states[0, j] = piece
         back[j] += jnp.exp(before[:, cols]) * piece
         before[:, cols] += dot(ends4, spread(4, TILE, 4 * j, 6))[15:16]
         return y_sum + split_dot(wide * y, head_select(j))
 
-    y_dot[...] = lax.fori_loop(0, TILES, finish, jnp.zeros((Q, 128), f32), unroll=4)
+    y_dot[...] = lax.fori_loop(0, TILES, finish, jnp.zeros((Q, 128), f32), unroll=8)
 
     @pl.when(c == pl.num_programs(0) - 1)
     def _():
@@ -790,7 +803,7 @@
         grad_taps[:, cols] += through(cols, dv, now[:, cols].astype(f32), edge[:, cols], taps[:, cols])
         return carry
 
-    lax.fori_loop(0, GT, body, 0, unroll=2)
+    lax.fori_loop(0, GT, body, 0, unroll=2 if last_group else GT)
 
     if last_group:
         band = slice(GW, GW + BC)
@@ -883,12 +896,12 @@
 
 def weight_grad(parts, right):
     sent, held = parts
-    return dot_rows(right, sent).astype(bf16), dot_rows(right, held)
+    return dot_rows(right, sent).astype(bf16), dot_rows(right, held).astype(bf16)
 
 
 def out_weight_sums(parts, right):
     sent, held = parts
-    return dot_rows(sent, right).astype(bf16), dot_rows(held, right)
+    return dot_rows(sent, right).astype(bf16), dot_rows(held, right).astype(bf16)
 
 
 def input_kernel(
@@ -981,14 +994,29 @@
     own, other = jnp.split(held, 2, axis=axis)
     got_own, got_other = jnp.split(got, 2, axis=axis)
     return (
-        own + got_own.astype(f32),
-        swap((other + got_other.astype(f32)).astype(bf16), "wshard", 2),
+        own.astype(f32) + got_own.astype(f32),
+        swap((other.astype(f32) + got_other.astype(f32)).astype(bf16), "wshard", 2),
     )
 
 
 def sum_pair(state):
     mine, got = state
-    return (mine + got.astype(f32)).astype(bf16)
+    return mine + got.astype(f32)
+
+
+def fold(value):
+    rows, cols = value.shape
+    return value.reshape(rows, cols // TILE, TILE).swapaxes(0, 1).reshape(-1, TILE)
+
+
+def unfold(value, cols):
+    return value.reshape(cols // TILE, -1, TILE).swapaxes(0, 1).reshape(-1, cols)
+
+
+def send_near_pair(even, odd):
+    is_even = (lax.axis_index("seq") & 1) == 0
+    theirs = jnp.where(is_even, odd, even).astype(bf16)
+    return jnp.where(is_even, even, odd), swap(theirs, "seq", 1)
 
 
 def send_near(state):
@@ -1016,13 +1044,13 @@
     return [owned] + [swap(owned, "seq", 2 * k) for k in range(1, len(got) + 1)]
 
 
-def in_order(pieces, place):
+def in_order(pieces, place, join=True):
     bit = 1
     while bit < len(pieces):
         odd = (place & bit) != 0
         pieces = [jnp.where(odd, pieces[k ^ bit], pieces[k]) for k in range(len(pieces))]
         bit *= 2
-    return jnp.concatenate(pieces, axis=0)
+    return jnp.concatenate(pieces, axis=0) if join else pieces
 
 
 def share_near(pieces):
@@ -1047,6 +1075,7 @@
     own_ch = INNER // seq
     me = lax.axis_index("wshard")
     order = jnp.stack([me ^ k for k in range(4)]).astype(jnp.int32)
+    place = lax.axis_index("seq")
 
     a_piece = jnp.concatenate(
         [in_weight[:, INNER : INNER + GW], jnp.pad(in_weight[:, 2 * INNER :], ((0, 0), (0, XCOLS - XUSED)))], axis=1
@@ -1118,8 +1147,8 @@
     du1, slope1, grad_bc1, k_dot1 = within_back(
         1, tie(x_act1, leaving), bc_act, aux, cum_t, dy, proj1, proj_edge1, taps, bias, ends, begin
     )
-    out_pair = sum_pair(tie(out_x, du1))
-    leave = tie(leave, out_pair)
+    out_fold = fold(sum_pair(tie(out_x, du1)))
+    leave = tie(leave, out_fold)
     grad_x0, grad_taps0, tail0, start0, x_dot0, edge_dot0, b_sum0 = backward(
         0, proj0, proj_edge0, taps, skip_row, dy, du0, slope0, x_act0, bc_act, aux, ends, back_states, leave
     )
@@ -1135,32 +1164,31 @@
 
     after0 = lax.ppermute(start0, "seq", backwards)
     gate_pair = sum_pair(tie(gate_x, grad_x0))
-    out_sum, gate_sum = lax.psum((out_pair, gate_pair), "seq")
-    grad_x0 = fix(tie(grad_x0, gate_pair), tail0, after0, taps[:, :GW])
+    early_near = send_near_pair(gate_pair, out_fold)
+    grad_x0 = fix(tie(grad_x0, early_near[0]), tail0, after0, taps[:, :GW])
     x0_grads = weight_grad(normed_parts, grad_x0)
     x0_core = send_core(x0_grads)
+    x0_x = send_x(x0_core)
     grad_x1, grad_taps1, tail1, start1, grad_taps_bc, grad_heads = backward(
-        1, proj1, proj_edge1, taps, skip_row, tie(dy, x0_grads), du1, slope1, x_act1, bc_act, aux, ends, back_states,
+        1, proj1, proj_edge1, taps, skip_row, tie(dy, x0_x[0]), du1, slope1, x_act1, bc_act, aux, ends, back_states,
         leave,
         (rest, rest, rest_edge, conv_bc, bias_bc, heads, y_dot, k_dot0, k_dot1, x_dot0, edge_dot0, b_sum0, grad_bc0, grad_bc1),
     )
-    after1 = lax.ppermute(start1, "seq", backwards)
-    x0_x = send_x(tie(x0_core, grad_x1))
-    grad_x1 = fix(tie(grad_x1, x0_x[0]), tail1, after1, all_taps)
+    x0_near = send_near(tie(x0_x, grad_x1))
+    early_far = send_far(tie(early_near, x0_near[0]))
+    after1 = lax.ppermute(tie(start1, x0_near[0]), "seq", backwards)
+    grad_x1 = fix(tie(grad_x1, early_far[0]), tail1, after1, all_taps)
     x1_grads = weight_grad(normed_parts, grad_x1)
     x1_core = send_core(x1_grads)
-    x0_near = send_near(tie(x0_x, x1_grads))
-    x1_x = send_x(tie(x1_core, x0_near[0]))
+    x0_far = send_far(tie(x0_near, x1_grads))
+    x1_x = send_x(tie(x1_core, x0_far[0]))
+    early_all = share_far(tie(early_far, x1_x[0]))
+    x0_all = share_far(tie(x0_far, early_all[0]))
     input_grad, norm_gain_grad = input_back(
-        order, tie(grad_gate, x1_x[0]), grad_x0, grad_x1, tokens, cot, norm_gain[None], gate_pieces, a_pieces, b_pieces
-    )
-    x0_far = send_far(tie(x0_near, input_grad))
-    x1_near = send_near(tie(x1_x, x0_far[0]))
-    x0_all = share_far(tie(x0_far, x1_near[0]))
-    x1_far = send_far(tie(x1_near, x0_all[0]))
-    x0_half = share_near(tie(x0_all, x1_far[0]))
-    x1_half = share_near(share_far(tie(x1_far, x0_half[0])))
-
+        order, tie(grad_gate, x0_all[0]), grad_x0, grad_x1, tokens, cot, norm_gain[None], gate_pieces, a_pieces, b_pieces
+    )
+    x1_near = send_near(tie(x1_x, input_grad))
+    norm_gain_grad = tie(norm_gain_grad, x1_near[0])
     grad_taps = jnp.concatenate([grad_taps0, grad_taps1], axis=1)
     shared = jnp.concatenate(
         [norm_gain_grad[0], out_gain_grad[0], grad_taps_bc[:5].reshape(-1)]
@@ -1181,7 +1209,13 @@
     small_sum = jnp.sum(
         exchange(small_out.reshape(seq * shards, 8, -1), ("seq", "wshard")), axis=0
     ).reshape(-1)
-    out_owned = out_sum.astype(f32)
+    early_half = share_near(tie(early_all, small_out))
+    x0_half = share_near(tie(x0_all, early_half[0]))
+    x1_far = send_far(tie(x1_near, x0_half[0]))
+    x1_all = share_far(x1_far)
+    x1_half = share_near(tie(x1_all, small_sum, early_half[1]))
+    gate_sum, out_sum = in_order(early_half, place & 1, join=False)
+    out_owned = unfold(out_sum, width).astype(f32)
     in_owned = jnp.concatenate(
         [gate_sum, whole_rows(x0_half), whole_rows(x1_half)[: XUSED - GW]], axis=0
     ).astype(f32).T

time: 533 us -> 498 us (0.934)
  waiting for transfers between devices: 106 us -> 68.1 us
  between operations: 15.4 us -> 1.93 us
  starting transfers between devices: 89.6 us -> 103 us
  Pallas kernels: 230 us -> 220 us
  local copies, waits for them, and re-layouts: 27.2 us -> 36.6 us
  other arithmetic: 26.2 us -> 34.3 us
    ppermute x36 -> x44, waiting for transfers between devices: 68.6 us -> 50.8 us  [swap(): return lax.ppermute(value, axis, [(i, i ^ bit) for i in range(count)])]
    psum x1 -> x0, waiting for transfers between devices: 16 us -> none  [local(): out_sum, gate_sum = lax.psum((out_pair, gate_pair), 'seq')]
    ppermute x36 -> x44, starting transfers between devices: 41.1 us -> 51.5 us  [swap(): return lax.ppermute(value, axis, [(i, i ^ bit) for i in range(count)])]
    pallas_call x1, Pallas kernels: 42.7 us -> 35.5 us  [middle(): pl.pallas_call(middle_kernel, grid_spec=pltpu.PrefetchScalarGridSpec(num_...]
    convert_element_type x7 -> x5, other arithmetic: 13.6 us -> 11.2 us  [the longest x4 8.58 us: send_x(): (other.astype(f32) + got_other.astype(f32)).astype(bf16)]
  transfers between devices with their start and end apart: 48 -> 55, of which waited for: 18 -> 14; matrix products, arithmetic and copies ran while one was open for 11% -> 15% of each run, Pallas kernels for 35% -> 37%
where the time goes in v3:
time: 498 us; the launch traced here: 489 us
  Pallas kernels  220 us (44%)
  starting transfers between devices  103 us (21%)
  waiting for transfers between devices  68.1 us (14%)
  local copies, waits for them, and re-layouts  36.6 us (7%)
  other arithmetic  34.3 us (7%)
  matrix products  25 us (5%)
    ppermute x44, starting transfers between devices, swap(): return lax.ppermute(value, axis, [(i, i ^ bit) for i in range(count)])  51.5 us
    ppermute x44, waiting for transfers between devices, swap(): return lax.ppermute(value, axis, [(i, i ^ bit) for i in range(count)])  50.8 us
    pallas_call x2, Pallas kernels, backward(): pl.pallas_call(functools.partial(back_kernel, group), grid=(chunks,), in_...  47.3 us
    all_to_all x8, starting transfers between devices, exchange(): return lax.all_to_all(value, axis, split_axis=0, concat_axis=0, tiled=True)  43.6 us
    pallas_call x2, Pallas kernels, within_back(): pl.pallas_call(functools.partial(within_back_kernel, group), grid=(length...  37.7 us
    pallas_call x1, Pallas kernels, middle(): pl.pallas_call(middle_kernel, grid_spec=pltpu.PrefetchScalarGridSpec(num_...  35.5 us
    dot_general x8, matrix products, dot_rows(): lax.dot_general(a, b, (((0,), (0,)), ((), ())), preferred_element_type=f32)  25 us
    pallas_call x2, Pallas kernels, within(): pl.pallas_call(functools.partial(within_kernel, group), grid=(length // Q...  22.8 us
  transfers between devices with their start and end apart: 55, of which 14 were waited for; matrix products, arithmetic and copies ran while one was open for 15% of the time, Pallas kernels for 37%

profile of v3, /device:TPU:0, one launch (start us, length us, event | category | flops | bytes accessed | tf_op | source)
XLA Modules:
  0.0 488.6 jit_solution(346764745924499887)
XLA Ops:
  7.1 5.8 %all-to-all-start = ((f32[8,8,256]{2,1,0:T(8,128)}), f32[8,8,256]{2,1,0:T(8,128)S(1)}, u32[]{:S(2)}, u32[]{:S(2)}) async-start(f32[8,8,256]{2,1,0:T(8,128)} %broadcast_in_dim.46), calls=%async_computation | async-start | bytes 131072 | tf_op jit(solution)/shard_map/all_to_all | solution.py:959
  29.9 8.7 %project.1 = (bf16[1024,1024]{1,0:T(8,128)(2,1)}, bf16[1024,1024]{1,0:T(8,128)(2,1)}, bf16[1024,384]{1,0:T(8,128)(2,1)}, bf16[16,1024]{1,0:T(8,128)(2,1)}, bf16[16,384]{1,0:T(8,128)(2,1)}) custom-call(s32[4]{0:T(128)} %pad_add_fusion.order, bf16[1024,1024]{1,0:T(8,128)(2,1)} %bitcast.56, bf16[16,1024]{1,0:T(8,128)(2,1)} %copy-done.47, f32[1,1024]{1,0:T(1,128)} %bitcast.79, ...), custom_call_target="tpu_custom_call" | custom-call | flops 59055800 | bytes 188743 | tf_op jit(solution)/shard_map/project/pallas_call | solution.py:211
  43.7 10.5 %states.2 = (f32[1024,1024]{1,0:T(8,128)}, f32[4,4,128,256]{3,2,1,0:T(8,128)}, f32[8,136,128]{2,1,0:T(8,128)}) custom-call(bf16[1024,1024]{1,0:T(8,128)(2,1)} %get-tuple-element.130.now.prior, bf16[1024,1024]{1,0:T(8,128)(2,1)} %get-tuple-element.130.now.prior, bf16[16,1024]{1,0:T(8,128)(2,1)} %get-tuple-element.131.edge, f32[4,2048]{1,0:T(4,128)} %bitcast.64, ...), custom_call_target="tpu_custom_call" | custom-call | flops 200000000 | bytes 209715 | tf_op jit(solution)/shard_map/states/pallas_call | solution.py:365
  54.2 6.1 %all-to-all-start.2 = ((f32[8,136,128]{2,1,0:T(8,128)}), f32[8,136,128]{2,1,0:T(8,128)S(1)}, u32[]{:S(2)}, u32[]{:S(2)}) async-start(f32[8,136,128]{2,1,0:T(8,128)} %get-tuple-element.138), calls=%async_computation.2 | async-start | bytes 1114112 | tf_op jit(solution)/shard_map/all_to_all | solution.py:959
  64.8 7.2 %project_more.1 = (bf16[1024,1024]{1,0:T(8,128)(2,1)}, bf16[16,1024]{1,0:T(8,128)(2,1)}) custom-call(s32[4]{0:T(128)} %pad_add_fusion.order, bf16[1024,1024]{1,0:T(8,128)(2,1)} %get-tuple-element.148.normed, bf16[16,1024]{1,0:T(8,128)(2,1)} %copy-done.47, f32[1,1024]{1,0:T(1,128)} %bitcast.80, bf16[256,1024]{1,0:T(8,128)(2,1)} %copy-done.8, ...), custom_call_target="tpu_custom_call" | custom-call | flops 42949672 | bytes 125829 | tf_op jit(solution)/shard_map/project_more/pallas_call | solution.py:236
  71.9 10.5 %states.3 = (f32[1024,1024]{1,0:T(8,128)}, f32[4,4,128,256]{3,2,1,0:T(8,128)}, f32[8,136,128]{2,1,0:T(8,128)}) custom-call(bf16[1024,1024]{1,0:T(8,128)(2,1)} %get-tuple-element.142.now.prior, bf16[1024,1024]{1,0:T(8,128)(2,1)} %get-tuple-element.142.now.prior, bf16[16,1024]{1,0:T(8,128)(2,1)} %get-tuple-element.143.edge, f32[4,2048]{1,0:T(4,128)} %bitcast.65, ...), custom_call_target="tpu_custom_call" | custom-call | flops 200000000 | bytes 209715 | tf_op jit(solution)/shard_map/states/pallas_call | solution.py:365
  82.5 6.5 %all-to-all-start.1 = ((f32[8,136,128]{2,1,0:T(8,128)}), f32[8,136,128]{2,1,0:T(8,128)}, u32[]{:S(2)}, u32[]{:S(2)}) async-start(f32[8,136,128]{2,1,0:T(8,128)} %get-tuple-element.144), calls=%async_computation.1 | async-start | bytes 1114112 | tf_op jit(solution)/shard_map/all_to_all | solution.py:959
  91.4 11.5 %within.2.y_in0 = f32[1024,1024]{1,0:T(8,128)} custom-call(f32[1024,1024]{1,0:T(8,128)} %get-tuple-element.165.x_act, f32[1024,256]{1,0:T(8,128)} %get-tuple-element.134.bc_act, f32[1024,128]{1,0:T(8,128)} %get-tuple-element.135.aux, f32[32,1024]{1,0:T(8,128)} %get-tuple-element.146.cum_t, f32[1,2048]{1,0:T(1,128)} %broadcast_in_dim_reshape.3.skip), custom_call_target="tpu_custom_call" | custom-call | flops 200000000 | bytes 209715 | tf_op jit(solution)/shard_map/within/pallas_call | solution.py:471
  103.5 9.6 %gate_project.1.gate = bf16[1024,2048]{1,0:T(8,128)(2,1)} custom-call(s32[4]{0:T(128)} %pad_add_fusion.order, bf16[1024,1024]{1,0:T(8,128)(2,1)} %get-tuple-element.148.normed, bf16[256,2048]{1,0:T(8,128)(2,1)} %copy-done.3, bf16[256,2048]{1,0:T(8,128)(2,1)} %collective-permute-done.7.w1.g1, bf16[256,2048]{1,0:T(8,128)(2,1)} %copy-done.11, ...), custom_call_target="tpu_custom_call" | custom-call | flops 85899344 | bytes 209715 | tf_op jit(solution)/shard_map/gate_project/pallas_call | solution.py:265
  115.1 6.0 %all-to-all-start.3 = ((f32[8,128,128]{2,1,0:T(8,128)}), f32[8,128,128]{2,1,0:T(8,128)S(1)}, u32[]{:S(2)}, u32[]{:S(2)}) async-start(f32[8,128,128]{2,1,0:T(8,128)} %chain.3), calls=%async_computation.3 | async-start | bytes 1048576 | tf_op jit(solution)/shard_map/all_to_all | solution.py:959
  124.9 10.3 %all-to-all-done.3.entering0 = f32[8,128,128]{2,1,0:T(8,128)S(1)} async-done(((f32[8,128,128]{2,1,0:T(8,128)}), f32[8,128,128]{2,1,0:T(8,128)S(1)}, u32[]{:S(2)}, u32[]{:S(2)}) %all-to-all-start.3) | async-done | bytes 524320 | tf_op jit(solution)/shard_map/all_to_all | solution.py:959
  140.2 11.3 %within.3.y_in1 = f32[1024,1024]{1,0:T(8,128)} custom-call(f32[1024,1024]{1,0:T(8,128)} %get-tuple-element.178.x_act, f32[1024,256]{1,0:T(8,128)} %get-tuple-element.134.bc_act, f32[1024,128]{1,0:T(8,128)} %get-tuple-element.135.aux, f32[32,1024]{1,0:T(8,128)} %get-tuple-element.146.cum_t, f32[1,2048]{1,0:T(1,128)} %broadcast_in_dim_reshape.3.skip), custom_call_target="tpu_custom_call" | custom-call | flops 200000000 | bytes 209715 | tf_op jit(solution)/shard_map/within/pallas_call | solution.py:471
  153.9 35.5 %middle.1 = (bf16[1024,2048]{1,0:T(8,128)(2,1)}, bf16[1024,1024]{1,0:T(8,128)(2,1)}, bf16[1024,2048]{1,0:T(8,128)(2,1)}, bf16[1024,2048]{1,0:T(8,128)(2,1)}, f32...) custom-call(s32[4]{0:T(128)} %pad_add_fusion.order, ...), custom_call_target="tpu_custom_call" | custom-call | flops 800000000 | bytes 838860 | tf_op jit(solution)/shard_map/middle/pallas_call | solution.py:697
  214.2 18.8 %within_back.2 = (bf16[1024,1024]{1,0:T(8,128)(2,1)}, bf16[1024,1024]{1,0:T(8,128)(2,1)}, f32[1024,256]{1,0:T(8,128)}, f32[1024,128]{1,0:T(8,128)}) custom-call(f32[1024,1024]{1,0:T(8,128)} %get-tuple-element.165.x_act, f32[1024,256]{1,0:T(8,128)} %get-tuple-element.134.bc_act, f32[1024,128]{1,0:T(8,128)} %get-tuple-element.135.aux, ...), custom_call_target="tpu_custom_call" | custom-call | flops 400000000 | bytes 293601 | tf_op jit(solution)/shard_map/within_back/pallas_call | solution.py:571
  241.9 6.3 %all-to-all-start.6 = ((f32[8,128,256]{2,1,0:T(8,128)}), f32[8,128,256]{2,1,0:T(8,128)S(1)}, u32[]{:S(2)}, u32[]{:S(2)}) async-start(f32[8,128,256]{2,1,0:T(8,128)} %chain.5), calls=%async_computation.6 | async-start | bytes 2097152 | tf_op jit(solution)/shard_map/all_to_all | solution.py:959
  250.3 18.9 %within_back.3 = (bf16[1024,1024]{1,0:T(8,128)(2,1)}, bf16[1024,1024]{1,0:T(8,128)(2,1)}, f32[1024,256]{1,0:T(8,128)}, f32[1024,128]{1,0:T(8,128)}) custom-call(f32[1024,1024]{1,0:T(8,128)} %get-tuple-element.178.x_act, f32[1024,256]{1,0:T(8,128)} %get-tuple-element.134.bc_act, f32[1024,128]{1,0:T(8,128)} %get-tuple-element.135.aux, ...), custom_call_target="tpu_custom_call" | custom-call | flops 400000000 | bytes 293601 | tf_op jit(solution)/shard_map/within_back/pallas_call | solution.py:571
  269.2 5.4 %collective-permute-done.15 = bf16[512,1024]{1,0:T(8,128)(2,1)} collective-permute-done((bf16[512,1024]{1,0:T(8,128)(2,1)}, bf16[512,1024]{1,0:T(8,128)(2,1)}, u32[]{:S(2)}, u32[]{:S(2)}) %collective-permute-start.15) | collective-permute-done | bytes 1048608 | tf_op jit(solution)/shard_map/ppermute | solution.py:955
  285.2 20.9 %backward.2 = (bf16[1024,1024]{1,0:T(8,128)(2,1)}, f32[8,1024]{1,0:T(8,128)}, f32[16,1024]{1,0:T(8,128)}, f32[8,1024]{1,0:T(8,128)}, f32[1024,128]{1,0:T(8,128)}...) custom-call(bf16[1024,1024]{1,0:T(8,128)(2,1)} %get-tuple-element.130.now.prior, bf16[16,1024]{1,0:T(8,128)(2,1)} %get-tuple-element.131.edge, ...), custom_call_target="tpu_custom_call" | custom-call | flops 400000000 | bytes 419430 | tf_op jit(solution)/shard_map/backward/pallas_call | solution.py:878
  321.4 26.4 %backward.3 = (bf16[1024,1408]{1,0:T(8,128)(2,1)}, f32[8,1024]{1,0:T(8,128)}, f32[16,1280]{1,0:T(8,128)}, f32[8,1280]{1,0:T(8,128)}, f32[8,256]{1,0:T(8,128)}, /*index=5*/f32[8,128]{1,0:T(8,128)}) custom-call(bf16[1024,1024]{1,0:T(8,128)(2,1)} %get-tuple-element.142.now.prior, bf16[16,1024]{1,0:T(8,128)(2,1)} %get-tuple-element.143.edge, ...), custom_call_target="tpu_custom_call" | custom-call | flops 400000000 | bytes 419430 | tf_op jit(solution)/shard_map/backward/pallas_call | solution.py:878
  377.4 8.5 %collective-permute-done.27 = bf16[512,256]{1,0:T(8,128)(2,1)} collective-permute-done((bf16[512,256]{1,0:T(8,128)(2,1)S(1)}, bf16[512,256]{1,0:T(8,128)(2,1)}, u32[]{:S(2)}, u32[]{:S(2)}) %collective-permute-start.27) | collective-permute-done | bytes 262176 | tf_op jit(solution)/shard_map/ppermute | solution.py:955
  390.3 5.3 %collective-permute-start.31 = (bf16[512,256]{1,0:T(8,128)(2,1)S(1)}, bf16[512,256]{1,0:T(8,128)(2,1)}, u32[]{:S(2)}, u32[]{:S(2)}) collective-permute-start(bf16[512,256]{1,0:T(8,128)(2,1)S(1)} %add_convert_fusion.4), channel_id=1, source_target_pairs={{0,8},{4,12},{8,0},{12,4},{16,24},{20,28},{24,16},{28,20},{1,9},{5... | collective-permute-start | bytes 786440 | tf_op jit(solution)/shard_map/ppermute | solution.py:955
  399.2 19.1 %input_back.1 = (f32[1024,1024]{1,0:T(8,128)}, f32[1,1024]{1,0:T(1,128)}) custom-call(s32[4]{0:T(128)} %pad_add_fusion.order, bf16[1024,2048]{1,0:T(8,128)(2,1)} %get-tuple-element.220.grad_gate, bf16[1024,1024]{1,0:T(8,128)(2,1)} %copy-done.27, bf16[1024,1408]{1,0:T(8,128)(2,1)} %copy-done.15, bf16[1024,1024]{1,0:T(8,128)(2,1)} %bitcast.58, ...), custom_call_target="tpu_custom_call" | custom-call | flops 187904816 | bytes 545259 | tf_op jit(solution)/shard_map/input_back/pallas_call | solution.py:935
  443.0 24.6 %collective-permute-done.38 = bf16[512,256]{1,0:T(8,128)(2,1)S(1)} collective-permute-done((bf16[512,256]{1,0:T(8,128)(2,1)S(1)}, bf16[512,256]{1,0:T(8,128)(2,1)S(1)}, u32[]{:S(2)}, u32[]{:S(2)}) %collective-permute-start.38) | collective-permute-done | bytes 262176 | tf_op jit(solution)/shard_map/ppermute | solution.py:955
  480.3 5.7 %collective-permute-done.46 = bf16[704,256]{1,0:T(8,128)(2,1)S(1)} collective-permute-done((bf16[704,256]{1,0:T(8,128)(2,1)S(1)}, bf16[704,256]{1,0:T(8,128)(2,1)S(1)}, u32[]{:S(2)}, u32[]{:S(2)}) %collective-permute-start.46) | collective-permute-done | bytes 360480 | tf_op jit(solution)/shard_map/ppermute | solution.py:955
  (335 shorter events, 187.4 us)
Async XLA Ops:
  25.9 34.4 %collective-permute-start.5 = (bf16[256,1024]{1,0:T(8,128)(2,1)S(1)}, bf16[256,1024]{1,0:T(8,128)(2,1)}, u32[]{:S(2)}, u32[]{:S(2)}) collective-permute-start(bf16[256,1024]{1,0:T(8,128)(2,1)S(1)} %copy.64.w0.b0), channel_id=1, source_target_pairs={{0,2},{1,3},{2,0},{3,1},{4,6},{5,7},{6,4},{7,5},{8,10},{9,11},{10,... | collective-permute-start | bytes 1572872 | tf_op jit(solution)/shard_map/ppermute | solution.py:955
  27.7 35.1 %collective-permute-start.8 = (bf16[256,2048]{1,0:T(8,128)(2,1)S(1)}, bf16[256,2048]{1,0:T(8,128)(2,1)S(1)}, u32[]{:S(2)}, u32[]{:S(2)}) collective-permute-start(bf16[256,2048]{1,0:T(8,128)(2,1)S(1)} %copy.65.w0.g0), channel_id=1, source_target_pairs={{0,2},{1,3},{2,0},{3,1},{4,6},{5,7},{6,4},{7,5},{8,10},{9,11},{10,... | collective-permute-start | bytes 3145736 | tf_op jit(solution)/shard_map/ppermute | solution.py:955
  54.2 28.3 %all-to-all-start.2 = ((f32[8,136,128]{2,1,0:T(8,128)}), f32[8,136,128]{2,1,0:T(8,128)S(1)}, u32[]{:S(2)}, u32[]{:S(2)}) async-start(f32[8,136,128]{2,1,0:T(8,128)} %get-tuple-element.138), calls=%async_computation.2 | async-start | bytes 1114112 | tf_op jit(solution)/shard_map/all_to_all | solution.py:959
  60.9 42.6 %collective-permute-start.7 = (bf16[256,2048]{1,0:T(8,128)(2,1)S(1)}, bf16[256,2048]{1,0:T(8,128)(2,1)}, u32[]{:S(2)}, u32[]{:S(2)}) collective-permute-start(bf16[256,2048]{1,0:T(8,128)(2,1)S(1)} %copy.65.w0.g0), channel_id=1, source_target_pairs={{0,1},{1,0},{2,3},{3,2},{4,5},{5,4},{6,7},{7,6},{8,9},{9,8},{10,11... | collective-permute-start | bytes 3145736 | tf_op jit(solution)/shard_map/ppermute | solution.py:955
  62.7 40.7 %collective-permute-start.9 = (bf16[256,2048]{1,0:T(8,128)(2,1)S(1)}, bf16[256,2048]{1,0:T(8,128)(2,1)}, u32[]{:S(2)}, u32[]{:S(2)}) collective-permute-start(bf16[256,2048]{1,0:T(8,128)(2,1)S(1)} %collective-permute-done.8.w2.g2), channel_id=1, source_target_pairs={{0,1},{1,0},{2,3},{3,2},{4,5},{5,4},{6,7},{7,6},{8,9},{9,8},{10,11... | collective-permute-start | bytes 3145736 | tf_op jit(solution)/shard_map/ppermute | solution.py:955
  82.5 32.6 %all-to-all-start.1 = ((f32[8,136,128]{2,1,0:T(8,128)}), f32[8,136,128]{2,1,0:T(8,128)}, u32[]{:S(2)}, u32[]{:S(2)}) async-start(f32[8,136,128]{2,1,0:T(8,128)} %get-tuple-element.144), calls=%async_computation.1 | async-start | bytes 1114112 | tf_op jit(solution)/shard_map/all_to_all | solution.py:959
  88.9 32.2 %collective-permute-start.11 = (bf16[512,1024]{1,0:T(8,128)(2,1)}, bf16[512,1024]{1,0:T(8,128)(2,1)}, u32[]{:S(2)}, u32[]{:S(2)}) collective-permute-start(bf16[512,1024]{1,0:T(8,128)(2,1)} %w0), channel_id=1, source_target_pairs={{0,2},{1,3},{2,0},{3,1},{4,6},{5,7},{6,4},{7,5},{8,10},{9,11},{10,... | collective-permute-start | bytes 3145736 | tf_op jit(solution)/shard_map/ppermute | solution.py:955
  121.1 32.0 %collective-permute-start.10 = (bf16[512,1024]{1,0:T(8,128)(2,1)}, bf16[512,1024]{1,0:T(8,128)(2,1)}, u32[]{:S(2)}, u32[]{:S(2)}) collective-permute-start(bf16[512,1024]{1,0:T(8,128)(2,1)} %w0), channel_id=1, source_target_pairs={{0,1},{1,0},{2,3},{3,2},{4,5},{5,4},{6,7},{7,6},{8,9},{9,8},{10,11... | collective-permute-start | bytes 3145736 | tf_op jit(solution)/shard_map/ppermute | solution.py:955
  121.1 32.0 %collective-permute-start.12 = (bf16[512,1024]{1,0:T(8,128)(2,1)}, bf16[512,1024]{1,0:T(8,128)(2,1)}, u32[]{:S(2)}, u32[]{:S(2)}) collective-permute-start(bf16[512,1024]{1,0:T(8,128)(2,1)} %collective-permute-done.11.w2), channel_id=1, source_target_pairs={{0,1},{1,0},{2,3},{3,2},{4,5},{5,4},{6,7},{7,6},{8,9},{9,8},{10,11... | collective-permute-start | bytes 3145736 | tf_op jit(solution)/shard_map/ppermute | solution.py:955
  196.0 37.0 %collective-permute-start.14 = (bf16[1024,1024]{1,0:T(8,128)(2,1)}, bf16[1024,1024]{1,0:T(8,128)(2,1)S(1)}, u32[]{:S(2)}, u32[]{:S(2)}) collective-permute-start(bf16[1024,1024]{1,0:T(8,128)(2,1)} %fusion.12), channel_id=1, source_target_pairs={{0,1},{1,0},{2,3},{3,2},{4,5},{5,4},{6,7},{7,6},{8,9},{9,8},{10,11... | collective-permute-start | bytes 6291464 | tf_op jit(solution)/shard_map/ppermute | solution.py:955
  203.5 32.1 %collective-permute-start.13 = (bf16[2048,512]{1,0:T(8,128)(2,1)}, bf16[2048,512]{1,0:T(8,128)(2,1)}, u32[]{:S(2)}, u32[]{:S(2)}) collective-permute-start(bf16[2048,512]{1,0:T(8,128)(2,1)} %convolution_convert_fusion.1), channel_id=1, source_target_pairs={{0,1},{1,0},{2,3},{3,2},{4,5},{5,4},{6,7},{7,6},{8,9},{9,8},{10,11... | collective-permute-start | bytes 6291464 | tf_op jit(solution)/shard_map/ppermute | solution.py:955
  204.0 34.6 %all-to-all-start.5 = ((f32[8,128,256]{2,1,0:T(8,128)}), f32[8,128,256]{2,1,0:T(8,128)S(1)}, u32[]{:S(2)}, u32[]{:S(2)}) async-start(f32[8,128,256]{2,1,0:T(8,128)} %get-tuple-element.171), calls=%async_computation.5 | async-start | bytes 2097152 | tf_op jit(solution)/shard_map/all_to_all | solution.py:959
  241.9 42.3 %all-to-all-start.6 = ((f32[8,128,256]{2,1,0:T(8,128)}), f32[8,128,256]{2,1,0:T(8,128)S(1)}, u32[]{:S(2)}, u32[]{:S(2)}) async-start(f32[8,128,256]{2,1,0:T(8,128)} %chain.5), calls=%async_computation.6 | async-start | bytes 2097152 | tf_op jit(solution)/shard_map/all_to_all | solution.py:959
  248.8 59.1 %collective-permute-start.16 = (bf16[2048,256]{1,0:T(8,128)(2,1)}, bf16[2048,256]{1,0:T(8,128)(2,1)}, u32[]{:S(2)}, u32[]{:S(2)}) collective-permute-start(bf16[2048,256]{1,0:T(8,128)(2,1)} %get-tuple-element.247), channel_id=1, source_target_pairs={{0,2},{1,3},{2,0},{3,1},{4,6},{5,7},{6,4},{7,5},{8,10},{9,11},{10,... | collective-permute-start | bytes 3145736 | tf_op jit(solution)/shard_map/ppermute | solution.py:955
  316.3 35.3 %collective-permute-start.21 = (bf16[2048,256]{1,0:T(8,128)(2,1)}, bf16[2048,256]{1,0:T(8,128)(2,1)}, u32[]{:S(2)}, u32[]{:S(2)}) collective-permute-start(bf16[2048,256]{1,0:T(8,128)(2,1)} %select_convert_fusion), channel_id=1, source_target_pairs={{0,4},{4,0},{8,12},{12,8},{16,20},{20,16},{24,28},{28,24},{1,5},{5... | collective-permute-start | bytes 3145736 | tf_op jit(solution)/shard_map/ppermute | solution.py:955
  320.8 28.1 %collective-permute-start.19 = (bf16[1024,256]{1,0:T(8,128)(2,1)S(1)}, bf16[1024,256]{1,0:T(8,128)(2,1)S(1)}, u32[]{:S(2)}, u32[]{:S(2)}) collective-permute-start(bf16[1024,256]{1,0:T(8,128)(2,1)S(1)} %get-tuple-element.262), channel_id=1, source_target_pairs={{0,2},{1,3},{2,0},{3,1},{4,6},{5,7},{6,4},{7,5},{8,10},{9,11},{10,... | collective-permute-start | bytes 1572872 | tf_op jit(solution)/shard_map/ppermute | solution.py:955
  372.6 45.6 %collective-permute-start.30 = (bf16[1408,256]{1,0:T(8,128)(2,1)}, bf16[1408,256]{1,0:T(8,128)(2,1)}, u32[]{:S(2)}, u32[]{:S(2)}) collective-permute-start(bf16[1408,256]{1,0:T(8,128)(2,1)} %get-tuple-element.253), channel_id=1, source_target_pairs={{0,2},{1,3},{2,0},{3,1},{4,6},{5,7},{6,4},{7,5},{8,10},{9,11},{10,... | collective-permute-start | bytes 2162696 | tf_op jit(solution)/shard_map/ppermute | solution.py:955
  390.3 32.3 %collective-permute-start.31 = (bf16[512,256]{1,0:T(8,128)(2,1)S(1)}, bf16[512,256]{1,0:T(8,128)(2,1)}, u32[]{:S(2)}, u32[]{:S(2)}) collective-permute-start(bf16[512,256]{1,0:T(8,128)(2,1)S(1)} %add_convert_fusion.4), channel_id=1, source_target_pairs={{0,8},{4,12},{8,0},{12,4},{16,24},{20,28},{24,16},{28,20},{1,9},{5... | collective-permute-start | bytes 786440 | tf_op jit(solution)/shard_map/ppermute | solution.py:955
  395.6 28.5 %collective-permute-start.32 = (bf16[512,256]{1,0:T(8,128)(2,1)S(1)}, bf16[512,256]{1,0:T(8,128)(2,1)}, u32[]{:S(2)}, u32[]{:S(2)}) collective-permute-start(bf16[512,256]{1,0:T(8,128)(2,1)S(1)} %add_convert_fusion.4), channel_id=1, source_target_pairs={{0,16},{4,20},{8,24},{12,28},{16,0},{20,4},{24,8},{28,12},{1,17},{... | collective-permute-start | bytes 786440 | tf_op jit(solution)/shard_map/ppermute | solution.py:955
  398.1 31.2 %collective-permute-start.35 = (bf16[128,256]{1,0:T(8,128)(2,1)S(1)}, bf16[128,256]{1,0:T(8,128)(2,1)S(1)}, u32[]{:S(2)}, u32[]{:S(2)}) collective-permute-start(bf16[128,256]{1,0:T(8,128)(2,1)S(1)} %add_convert_fusion.6), channel_id=1, source_target_pairs={{0,8},{4,12},{8,0},{12,4},{16,24},{20,28},{24,16},{28,20},{1,9},{5... | collective-permute-start | bytes 196616 | tf_op jit(solution)/shard_map/ppermute | solution.py:955
  427.8 44.5 %collective-permute-start.34 = (bf16[2048,256]{1,0:T(8,128)(2,1)}, bf16[2048,256]{1,0:T(8,128)(2,1)}, u32[]{:S(2)}, u32[]{:S(2)}) collective-permute-start(bf16[2048,256]{1,0:T(8,128)(2,1)} %pad_maximum_fusion.3), channel_id=1, source_target_pairs={{0,4},{4,0},{8,12},{12,8},{16,20},{20,16},{24,28},{28,24},{1,5},{5... | collective-permute-start | bytes 3145736 | tf_op jit(solution)/shard_map/ppermute | solution.py:955
  432.2 35.5 %collective-permute-start.38 = (bf16[512,256]{1,0:T(8,128)(2,1)S(1)}, bf16[512,256]{1,0:T(8,128)(2,1)S(1)}, u32[]{:S(2)}, u32[]{:S(2)}) collective-permute-start(bf16[512,256]{1,0:T(8,128)(2,1)S(1)} %pad_maximum_fusion.11), channel_id=1, source_target_pairs={{0,4},{4,0},{8,12},{12,8},{16,20},{20,16},{24,28},{28,24},{1,5},{5... | collective-permute-start | bytes 786440 | tf_op jit(solution)/shard_map/ppermute | solution.py:955
  432.7 43.0 %all-to-all-start.7 = ((f32[32,8,768]{2,1,0:T(8,128)}), f32[32,8,768]{2,1,0:T(8,128)S(1)}, u32[]{:S(2)}, u32[]{:S(2)}) async-start(f32[32,8,768]{2,1,0:T(8,128)} %reshape.100), calls=%async_computation.7 | async-start | bytes 1572864 | tf_op jit(solution)/shard_map/all_to_all | solution.py:959
  438.6 29.2 %collective-permute-start.40 = (bf16[176,256]{1,0:T(8,128)(2,1)S(1)}, bf16[176,256]{1,0:T(8,128)(2,1)S(1)}, u32[]{:S(2)}, u32[]{:S(2)}) collective-permute-start(bf16[176,256]{1,0:T(8,128)(2,1)S(1)} %get-tuple-element.274), channel_id=1, source_target_pairs={{0,8},{4,12},{8,0},{12,4},{16,24},{20,28},{24,16},{28,20},{1,9},{5... | collective-permute-start | bytes 270344 | tf_op jit(solution)/shard_map/ppermute | solution.py:955
  (96 other events, 1016.4 us)

commit v4 on v3

--- a/solution.py
+++ b/solution.py
@@ -202,7 +202,7 @@
 
 
 def cost(flops, megabytes):
-    return pl.CostEstimate(flops=int(flops) // 50, bytes_accessed=int(megabytes * 2**20) // 50, transcendentals=0)
+    return pl.CostEstimate(flops=int(flops) // 1, bytes_accessed=int(megabytes * 2**20) // 1, transcendentals=0)
 
 
 def project(order, tokens, edge, gain, pieces):

time: 498 us -> 492 us (0.988)
  transfers between devices with their start and end apart: 55 -> 55, of which waited for: 14 -> 13; matrix products, arithmetic and copies ran while one was open for 15% -> 14% of each run, Pallas kernels for 37% -> 38%
where the time goes in v4:
time: 492 us; the launch traced here: 483 us
  Pallas kernels  221 us (45%)
  starting transfers between devices  101 us (21%)
  waiting for transfers between devices  69.6 us (14%)
  local copies, waits for them, and re-layouts  33.8 us (7%)
  other arithmetic  30.7 us (6%)
  matrix products  24.8 us (5%)
    ppermute x44, starting transfers between devices, swap(): return lax.ppermute(value, axis, [(i, i ^ bit) for i in range(count)])  53.4 us
    ppermute x44, waiting for transfers between devices, swap(): return lax.ppermute(value, axis, [(i, i ^ bit) for i in range(count)])  49 us
    pallas_call x2, Pallas kernels, backward(): pl.pallas_call(functools.partial(back_kernel, group), grid=(chunks,), in_...  47.3 us
    all_to_all x8, starting transfers between devices, exchange(): return lax.all_to_all(value, axis, split_axis=0, concat_axis=0, tiled=True)  40.5 us
    pallas_call x2, Pallas kernels, within_back(): pl.pallas_call(functools.partial(within_back_kernel, group), grid=(length...  37.8 us
    pallas_call x1, Pallas kernels, middle(): pl.pallas_call(middle_kernel, grid_spec=pltpu.PrefetchScalarGridSpec(num_...  35.7 us
    dot_general x8, matrix products, dot_rows(): lax.dot_general(a, b, (((0,), (0,)), ((), ())), preferred_element_type=f32)  24.8 us
    pallas_call x2, Pallas kernels, within(): pl.pallas_call(functools.partial(within_kernel, group), grid=(length // Q...  22.8 us
  transfers between devices with their start and end apart: 55, of which 13 were waited for; matrix products, arithmetic and copies ran while one was open for 14% of the time, Pallas kernels for 38%

profile of v4, /device:TPU:0, one launch (start us, length us, event | category | flops | bytes accessed | tf_op | source)
XLA Modules:
  0.0 483.0 jit_solution(7007666181996685611)
XLA Ops:
  6.3 5.8 %all-to-all-start = ((f32[8,8,256]{2,1,0:T(8,128)}), f32[8,8,256]{2,1,0:T(8,128)S(1)}, u32[]{:S(2)}, u32[]{:S(2)}) async-start(f32[8,8,256]{2,1,0:T(8,128)} %broadcast_in_dim.46), calls=%async_computation | async-start | bytes 131072 | tf_op jit(solution)/shard_map/all_to_all | solution.py:959
  30.9 8.7 %project.1 = (bf16[1024,1024]{1,0:T(8,128)(2,1)}, bf16[1024,1024]{1,0:T(8,128)(2,1)}, bf16[1024,384]{1,0:T(8,128)(2,1)}, bf16[16,1024]{1,0:T(8,128)(2,1)}, bf16[16,384]{1,0:T(8,128)(2,1)}) custom-call(s32[4]{0:T(128)} %pad_add_fusion.order, bf16[1024,1024]{1,0:T(8,128)(2,1)} %bitcast.78, bf16[16,1024]{1,0:T(8,128)(2,1)} %copy-done.68, f32[1,1024]{1,0:T(1,128)} %bitcast.87, ...), custom_call_target="tpu_custom_call" | custom-call | flops 2952790016 | bytes 9437184 | tf_op jit(solution)/shard_map/project/pallas_call | solution.py:211
  39.5 5.2 %factors.1 = (f32[1024,256]{1,0:T(8,128)}, f32[1024,128]{1,0:T(8,128)}, f32[32,1024]{1,0:T(8,128)}) custom-call(bf16[1024,384]{1,0:T(8,128)(2,1)} %get-tuple-element.132.now.prior.others_0_.others_1_, bf16[1024,384]{1,0:T(8,128)(2,1)} %get-tuple-element.132.now.prior.others_0_.others_1_, bf16[16,384]{1,0:T(8,128)(2,1)} %get-tuple-element.133.edge.others_2_, ...), custom_call_target="tpu_custom_call" | custom-call | flops 1000000000 | bytes 4194304 | tf_op jit(solution)/shard_map/factors/pallas_call | solution.py:347
  45.0 10.5 %states.2 = (f32[1024,1024]{1,0:T(8,128)}, f32[4,4,128,256]{3,2,1,0:T(8,128)}, f32[8,136,128]{2,1,0:T(8,128)}) custom-call(bf16[1024,1024]{1,0:T(8,128)(2,1)} %get-tuple-element.130.now.prior, bf16[1024,1024]{1,0:T(8,128)(2,1)} %get-tuple-element.130.now.prior, bf16[16,1024]{1,0:T(8,128)(2,1)} %get-tuple-element.131.edge, f32[4,2048]{1,0:T(4,128)} %bitcast.61, ...), custom_call_target="tpu_custom_call" | custom-call | flops 10000000000 | bytes 10485760 | tf_op jit(solution)/shard_map/states/pallas_call | solution.py:365
  55.5 5.8 %all-to-all-start.2 = ((f32[8,136,128]{2,1,0:T(8,128)}), f32[8,136,128]{2,1,0:T(8,128)S(1)}, u32[]{:S(2)}, u32[]{:S(2)}) async-start(f32[8,136,128]{2,1,0:T(8,128)} %get-tuple-element.138), calls=%async_computation.2 | async-start | bytes 1114112 | tf_op jit(solution)/shard_map/all_to_all | solution.py:959
  62.2 7.2 %project_more.1 = (bf16[1024,1024]{1,0:T(8,128)(2,1)}, bf16[16,1024]{1,0:T(8,128)(2,1)}) custom-call(s32[4]{0:T(128)} %pad_add_fusion.order, bf16[1024,1024]{1,0:T(8,128)(2,1)} %get-tuple-element.148.normed, bf16[16,1024]{1,0:T(8,128)(2,1)} %copy-done.68, f32[1,1024]{1,0:T(1,128)} %bitcast.88, bf16[256,1024]{1,0:T(8,128)(2,1)} %copy-done.24, ...), custom_call_target="tpu_custom_call" | custom-call | flops 2147483648 | bytes 6291456 | tf_op jit(solution)/shard_map/project_more/pallas_call | solution.py:236
  69.4 10.6 %states.3 = (f32[1024,1024]{1,0:T(8,128)}, f32[4,4,128,256]{3,2,1,0:T(8,128)}, f32[8,136,128]{2,1,0:T(8,128)}) custom-call(bf16[1024,1024]{1,0:T(8,128)(2,1)} %get-tuple-element.142.now.prior, bf16[1024,1024]{1,0:T(8,128)(2,1)} %get-tuple-element.142.now.prior, bf16[16,1024]{1,0:T(8,128)(2,1)} %get-tuple-element.143.edge, f32[4,2048]{1,0:T(4,128)} %bitcast.62, ...), custom_call_target="tpu_custom_call" | custom-call | flops 10000000000 | bytes 10485760 | tf_op jit(solution)/shard_map/states/pallas_call | solution.py:365
  80.0 6.3 %all-to-all-start.1 = ((f32[8,136,128]{2,1,0:T(8,128)}), f32[8,136,128]{2,1,0:T(8,128)S(1)}, u32[]{:S(2)}, u32[]{:S(2)}) async-start(f32[8,136,128]{2,1,0:T(8,128)} %get-tuple-element.144), calls=%async_computation.1 | async-start | bytes 1114112 | tf_op jit(solution)/shard_map/all_to_all | solution.py:959
  86.3 11.5 %within.2.y_in0 = f32[1024,1024]{1,0:T(8,128)} custom-call(f32[1024,1024]{1,0:T(8,128)} %get-tuple-element.165.x_act, f32[1024,256]{1,0:T(8,128)} %get-tuple-element.134.bc_act, f32[1024,128]{1,0:T(8,128)} %get-tuple-element.135.aux, f32[32,1024]{1,0:T(8,128)} %get-tuple-element.146.cum_t, f32[1,2048]{1,0:T(1,128)} %broadcast_in_dim_reshape.3.skip), custom_call_target="tpu_custom_call" | custom-call | flops 10000000000 | bytes 10485760 | tf_op jit(solution)/shard_map/within/pallas_call | solution.py:471
  98.4 9.6 %gate_project.1.gate = bf16[1024,2048]{1,0:T(8,128)(2,1)} custom-call(s32[4]{0:T(128)} %pad_add_fusion.order, bf16[1024,1024]{1,0:T(8,128)(2,1)} %get-tuple-element.148.normed, bf16[256,2048]{1,0:T(8,128)(2,1)} %copy-done.15, bf16[256,2048]{1,0:T(8,128)(2,1)} %collective-permute-done.7.w1.g1, bf16[256,2048]{1,0:T(8,128)(2,1)} %collective-permute-done.8.w2.g2, ...), custom_call_target="tpu_custom_call" | custom-call | flops 4294967296 | bytes 10485760 | tf_op jit(solution)/shard_map/gate_project/pallas_call | solution.py:265
  110.0 6.0 %all-to-all-start.3 = ((f32[8,128,128]{2,1,0:T(8,128)}), f32[8,128,128]{2,1,0:T(8,128)S(1)}, u32[]{:S(2)}, u32[]{:S(2)}) async-start(f32[8,128,128]{2,1,0:T(8,128)} %chain.3), calls=%async_computation.3 | async-start | bytes 1048576 | tf_op jit(solution)/shard_map/all_to_all | solution.py:959
  121.9 8.7 %all-to-all-done.3.entering0 = f32[8,128,128]{2,1,0:T(8,128)S(1)} async-done(((f32[8,128,128]{2,1,0:T(8,128)}), f32[8,128,128]{2,1,0:T(8,128)S(1)}, u32[]{:S(2)}, u32[]{:S(2)}) %all-to-all-start.3) | async-done | bytes 524320 | tf_op jit(solution)/shard_map/all_to_all | solution.py:959
  134.3 11.3 %within.3.y_in1 = f32[1024,1024]{1,0:T(8,128)} custom-call(f32[1024,1024]{1,0:T(8,128)} %get-tuple-element.178.x_act, f32[1024,256]{1,0:T(8,128)} %get-tuple-element.134.bc_act, f32[1024,128]{1,0:T(8,128)} %get-tuple-element.135.aux, f32[32,1024]{1,0:T(8,128)} %get-tuple-element.146.cum_t, f32[1,2048]{1,0:T(1,128)} %broadcast_in_dim_reshape.3.skip), custom_call_target="tpu_custom_call" | custom-call | flops 10000000000 | bytes 10485760 | tf_op jit(solution)/shard_map/within/pallas_call | solution.py:471
  150.1 35.7 %middle.1 = (bf16[1024,2048]{1,0:T(8,128)(2,1)}, bf16[1024,1024]{1,0:T(8,128)(2,1)}, bf16[1024,2048]{1,0:T(8,128)(2,1)}, bf16[1024,2048]{1,0:T(8,128)(2,1)}, f32...) custom-call(s32[4]{0:T(128)} %pad_add_fusion.order, ...), custom_call_target="tpu_custom_call" | custom-call | flops 40000000000 | bytes 41943040 | tf_op jit(solution)/shard_map/middle/pallas_call | solution.py:697
  208.0 18.8 %within_back.2 = (bf16[1024,1024]{1,0:T(8,128)(2,1)}, bf16[1024,1024]{1,0:T(8,128)(2,1)}, f32[1024,256]{1,0:T(8,128)}, f32[1024,128]{1,0:T(8,128)}) custom-call(f32[1024,1024]{1,0:T(8,128)} %get-tuple-element.165.x_act, f32[1024,256]{1,0:T(8,128)} %get-tuple-element.134.bc_act, f32[1024,128]{1,0:T(8,128)} %get-tuple-element.135.aux, ...), custom_call_target="tpu_custom_call" | custom-call | flops 20000000000 | bytes 14680064 | tf_op jit(solution)/shard_map/within_back/pallas_call | solution.py:571
  244.0 19.1 %within_back.3 = (bf16[1024,1024]{1,0:T(8,128)(2,1)}, bf16[1024,1024]{1,0:T(8,128)(2,1)}, f32[1024,256]{1,0:T(8,128)}, f32[1024,128]{1,0:T(8,128)}) custom-call(f32[1024,1024]{1,0:T(8,128)} %get-tuple-element.178.x_act, f32[1024,256]{1,0:T(8,128)} %get-tuple-element.134.bc_act, f32[1024,128]{1,0:T(8,128)} %get-tuple-element.135.aux, ...), custom_call_target="tpu_custom_call" | custom-call | flops 20000000000 | bytes 14680064 | tf_op jit(solution)/shard_map/within_back/pallas_call | solution.py:571
  263.1 5.2 %collective-permute-done.15 = bf16[512,1024]{1,0:T(8,128)(2,1)S(1)} collective-permute-done((bf16[512,1024]{1,0:T(8,128)(2,1)}, bf16[512,1024]{1,0:T(8,128)(2,1)S(1)}, u32[]{:S(2)}, u32[]{:S(2)}) %collective-permute-start.15) | collective-permute-done | bytes 1048608 | tf_op jit(solution)/shard_map/ppermute | solution.py:955
  276.7 20.9 %backward.2 = (bf16[1024,1024]{1,0:T(8,128)(2,1)}, f32[8,1024]{1,0:T(8,128)}, f32[16,1024]{1,0:T(8,128)}, f32[8,1024]{1,0:T(8,128)}, f32[1024,128]{1,0:T(8,128)}...) custom-call(bf16[1024,1024]{1,0:T(8,128)(2,1)} %get-tuple-element.130.now.prior, bf16[16,1024]{1,0:T(8,128)(2,1)} %get-tuple-element.131.edge, ...), custom_call_target="tpu_custom_call" | custom-call | flops 20000000000 | bytes 20971520 | tf_op jit(solution)/shard_map/backward/pallas_call | solution.py:878
  315.4 26.4 %backward.3 = (bf16[1024,1408]{1,0:T(8,128)(2,1)}, f32[8,1024]{1,0:T(8,128)}, f32[16,1280]{1,0:T(8,128)}, f32[8,1280]{1,0:T(8,128)}, f32[8,256]{1,0:T(8,128)}, /*index=5*/f32[8,128]{1,0:T(8,128)}) custom-call(bf16[1024,1024]{1,0:T(8,128)(2,1)} %get-tuple-element.142.now.prior, bf16[16,1024]{1,0:T(8,128)(2,1)} %get-tuple-element.143.edge, ...), custom_call_target="tpu_custom_call" | custom-call | flops 20000000000 | bytes 20971520 | tf_op jit(solution)/shard_map/backward/pallas_call | solution.py:878
  371.9 8.0 %collective-permute-done.27 = bf16[512,256]{1,0:T(8,128)(2,1)S(1)} collective-permute-done((bf16[512,256]{1,0:T(8,128)(2,1)S(1)}, bf16[512,256]{1,0:T(8,128)(2,1)S(1)}, u32[]{:S(2)}, u32[]{:S(2)}) %collective-permute-start.27) | collective-permute-done | bytes 262176 | tf_op jit(solution)/shard_map/ppermute | solution.py:955
  380.0 8.4 %collective-permute-start.31 = (bf16[512,256]{1,0:T(8,128)(2,1)S(1)}, bf16[512,256]{1,0:T(8,128)(2,1)S(1)}, u32[]{:S(2)}, u32[]{:S(2)}) collective-permute-start(bf16[512,256]{1,0:T(8,128)(2,1)S(1)} %add_convert_fusion.4), channel_id=1, source_target_pairs={{0,8},{4,12},{8,0},{12,4},{16,24},{20,28},{24,16},{28,20},{1,9},{5... | collective-permute-start | bytes 786440 | tf_op jit(solution)/shard_map/ppermute | solution.py:955
  392.6 19.1 %input_back.1 = (f32[1024,1024]{1,0:T(8,128)}, f32[1,1024]{1,0:T(1,128)}) custom-call(s32[4]{0:T(128)} %pad_add_fusion.order, bf16[1024,2048]{1,0:T(8,128)(2,1)} %get-tuple-element.220.grad_gate, bf16[1024,1024]{1,0:T(8,128)(2,1)} %copy-done.62, bf16[1024,1408]{1,0:T(8,128)(2,1)} %copy-done.59, bf16[1024,1024]{1,0:T(8,128)(2,1)} %bitcast.80, ...), custom_call_target="tpu_custom_call" | custom-call | flops 9395240960 | bytes 27262976 | tf_op jit(solution)/shard_map/input_back/pallas_call | solution.py:935
  435.6 25.2 %collective-permute-done.38 = bf16[512,256]{1,0:T(8,128)(2,1)} collective-permute-done((bf16[512,256]{1,0:T(8,128)(2,1)}, bf16[512,256]{1,0:T(8,128)(2,1)}, u32[]{:S(2)}, u32[]{:S(2)}) %collective-permute-start.38) | collective-permute-done | bytes 262176 | tf_op jit(solution)/shard_map/ppermute | solution.py:955
  474.7 5.4 %collective-permute-done.46 = bf16[704,256]{1,0:T(8,128)(2,1)S(1)} collective-permute-done((bf16[704,256]{1,0:T(8,128)(2,1)S(1)}, bf16[704,256]{1,0:T(8,128)(2,1)S(1)}, u32[]{:S(2)}, u32[]{:S(2)}) %collective-permute-start.46) | collective-permute-done | bytes 360480 | tf_op jit(solution)/shard_map/ppermute | solution.py:955
  (349 shorter events, 181.4 us)
Async XLA Ops:
  28.6 32.8 %collective-permute-start.4 = (bf16[256,1024]{1,0:T(8,128)(2,1)S(1)}, bf16[256,1024]{1,0:T(8,128)(2,1)S(1)}, u32[]{:S(2)}, u32[]{:S(2)}) collective-permute-start(bf16[256,1024]{1,0:T(8,128)(2,1)S(1)} %copy.64.w0.b0), channel_id=1, source_target_pairs={{0,1},{1,0},{2,3},{3,2},{4,5},{5,4},{6,7},{7,6},{8,9},{9,8},{10,11... | collective-permute-start | bytes 1572872 | tf_op jit(solution)/shard_map/ppermute | solution.py:955
  28.8 32.5 %collective-permute-start.8 = (bf16[256,2048]{1,0:T(8,128)(2,1)S(1)}, bf16[256,2048]{1,0:T(8,128)(2,1)}, u32[]{:S(2)}, u32[]{:S(2)}) collective-permute-start(bf16[256,2048]{1,0:T(8,128)(2,1)S(1)} %copy.65.w0.g0), channel_id=1, source_target_pairs={{0,2},{1,3},{2,0},{3,1},{4,6},{5,7},{6,4},{7,5},{8,10},{9,11},{10,... | collective-permute-start | bytes 3145736 | tf_op jit(solution)/shard_map/ppermute | solution.py:955
  29.1 69.3 %collective-permute-start.7 = (bf16[256,2048]{1,0:T(8,128)(2,1)S(1)}, bf16[256,2048]{1,0:T(8,128)(2,1)}, u32[]{:S(2)}, u32[]{:S(2)}) collective-permute-start(bf16[256,2048]{1,0:T(8,128)(2,1)S(1)} %copy.65.w0.g0), channel_id=1, source_target_pairs={{0,1},{1,0},{2,3},{3,2},{4,5},{5,4},{6,7},{7,6},{8,9},{9,8},{10,11... | collective-permute-start | bytes 3145736 | tf_op jit(solution)/shard_map/ppermute | solution.py:955
  29.1 88.4 %collective-permute-start.11 = (bf16[512,1024]{1,0:T(8,128)(2,1)}, bf16[512,1024]{1,0:T(8,128)(2,1)}, u32[]{:S(2)}, u32[]{:S(2)}) collective-permute-start(bf16[512,1024]{1,0:T(8,128)(2,1)} %w0), channel_id=1, source_target_pairs={{0,2},{1,3},{2,0},{3,1},{4,6},{5,7},{6,4},{7,5},{8,10},{9,11},{10,... | collective-permute-start | bytes 3145736 | tf_op jit(solution)/shard_map/ppermute | solution.py:955
  61.4 37.0 %collective-permute-start.9 = (bf16[256,2048]{1,0:T(8,128)(2,1)}, bf16[256,2048]{1,0:T(8,128)(2,1)}, u32[]{:S(2)}, u32[]{:S(2)}) collective-permute-start(bf16[256,2048]{1,0:T(8,128)(2,1)} %collective-permute-done.8.w2.g2), channel_id=1, source_target_pairs={{0,1},{1,0},{2,3},{3,2},{4,5},{5,4},{6,7},{7,6},{8,9},{9,8},{10,11... | collective-permute-start | bytes 3145736 | tf_op jit(solution)/shard_map/ppermute | solution.py:955
  80.0 30.1 %all-to-all-start.1 = ((f32[8,136,128]{2,1,0:T(8,128)}), f32[8,136,128]{2,1,0:T(8,128)S(1)}, u32[]{:S(2)}, u32[]{:S(2)}) async-start(f32[8,136,128]{2,1,0:T(8,128)} %get-tuple-element.144), calls=%async_computation.1 | async-start | bytes 1114112 | tf_op jit(solution)/shard_map/all_to_all | solution.py:959
  116.0 32.9 %collective-permute-start.10 = (bf16[512,1024]{1,0:T(8,128)(2,1)}, bf16[512,1024]{1,0:T(8,128)(2,1)}, u32[]{:S(2)}, u32[]{:S(2)}) collective-permute-start(bf16[512,1024]{1,0:T(8,128)(2,1)} %w0), channel_id=1, source_target_pairs={{0,1},{1,0},{2,3},{3,2},{4,5},{5,4},{6,7},{7,6},{8,9},{9,8},{10,11... | collective-permute-start | bytes 3145736 | tf_op jit(solution)/shard_map/ppermute | solution.py:955
  117.6 31.4 %collective-permute-start.12 = (bf16[512,1024]{1,0:T(8,128)(2,1)}, bf16[512,1024]{1,0:T(8,128)(2,1)S(1)}, u32[]{:S(2)}, u32[]{:S(2)}) collective-permute-start(bf16[512,1024]{1,0:T(8,128)(2,1)} %collective-permute-done.11.w2), channel_id=1, source_target_pairs={{0,1},{1,0},{2,3},{3,2},{4,5},{5,4},{6,7},{7,6},{8,9},{9,8},{10,11... | collective-permute-start | bytes 3145736 | tf_op jit(solution)/shard_map/ppermute | solution.py:955
  192.4 34.3 %collective-permute-start.14 = (bf16[1024,1024]{1,0:T(8,128)(2,1)}, bf16[1024,1024]{1,0:T(8,128)(2,1)S(1)}, u32[]{:S(2)}, u32[]{:S(2)}) collective-permute-start(bf16[1024,1024]{1,0:T(8,128)(2,1)} %fusion.12), channel_id=1, source_target_pairs={{0,1},{1,0},{2,3},{3,2},{4,5},{5,4},{6,7},{7,6},{8,9},{9,8},{10,11... | collective-permute-start | bytes 6291464 | tf_op jit(solution)/shard_map/ppermute | solution.py:955
  199.9 29.5 %collective-permute-start.13 = (bf16[2048,512]{1,0:T(8,128)(2,1)}, bf16[2048,512]{1,0:T(8,128)(2,1)}, u32[]{:S(2)}, u32[]{:S(2)}) collective-permute-start(bf16[2048,512]{1,0:T(8,128)(2,1)} %convolution_convert_fusion.1), channel_id=1, source_target_pairs={{0,1},{1,0},{2,3},{3,2},{4,5},{5,4},{6,7},{7,6},{8,9},{9,8},{10,11... | collective-permute-start | bytes 6291464 | tf_op jit(solution)/shard_map/ppermute | solution.py:955
  204.1 29.9 %all-to-all-start.5 = ((f32[8,128,256]{2,1,0:T(8,128)}), f32[8,128,256]{2,1,0:T(8,128)S(1)}, u32[]{:S(2)}, u32[]{:S(2)}) async-start(f32[8,128,256]{2,1,0:T(8,128)} %get-tuple-element.171), calls=%async_computation.5 | async-start | bytes 2097152 | tf_op jit(solution)/shard_map/all_to_all | solution.py:959
  237.2 39.4 %all-to-all-start.6 = ((f32[8,128,256]{2,1,0:T(8,128)}), f32[8,128,256]{2,1,0:T(8,128)}, u32[]{:S(2)}, u32[]{:S(2)}) async-start(f32[8,128,256]{2,1,0:T(8,128)} %chain.5), calls=%async_computation.6 | async-start | bytes 2097152 | tf_op jit(solution)/shard_map/all_to_all | solution.py:959
  243.5 55.7 %collective-permute-start.16 = (bf16[2048,256]{1,0:T(8,128)(2,1)}, bf16[2048,256]{1,0:T(8,128)(2,1)S(1)}, u32[]{:S(2)}, u32[]{:S(2)}) collective-permute-start(bf16[2048,256]{1,0:T(8,128)(2,1)} %get-tuple-element.247), channel_id=1, source_target_pairs={{0,2},{1,3},{2,0},{3,1},{4,6},{5,7},{6,4},{7,5},{8,10},{9,11},{10,... | collective-permute-start | bytes 3145736 | tf_op jit(solution)/shard_map/ppermute | solution.py:955
  308.2 37.6 %collective-permute-start.21 = (bf16[2048,256]{1,0:T(8,128)(2,1)S(1)}, bf16[2048,256]{1,0:T(8,128)(2,1)}, u32[]{:S(2)}, u32[]{:S(2)}) collective-permute-start(bf16[2048,256]{1,0:T(8,128)(2,1)S(1)} %select_convert_fusion), channel_id=1, source_target_pairs={{0,4},{4,0},{8,12},{12,8},{16,20},{20,16},{24,28},{28,24},{1,5},{5... | collective-permute-start | bytes 3145736 | tf_op jit(solution)/shard_map/ppermute | solution.py:955
  313.9 29.0 %collective-permute-start.19 = (bf16[1024,256]{1,0:T(8,128)(2,1)S(1)}, bf16[1024,256]{1,0:T(8,128)(2,1)S(1)}, u32[]{:S(2)}, u32[]{:S(2)}) collective-permute-start(bf16[1024,256]{1,0:T(8,128)(2,1)S(1)} %get-tuple-element.262), channel_id=1, source_target_pairs={{0,2},{1,3},{2,0},{3,1},{4,6},{5,7},{6,4},{7,5},{8,10},{9,11},{10,... | collective-permute-start | bytes 1572872 | tf_op jit(solution)/shard_map/ppermute | solution.py:955
  380.0 34.4 %collective-permute-start.31 = (bf16[512,256]{1,0:T(8,128)(2,1)S(1)}, bf16[512,256]{1,0:T(8,128)(2,1)S(1)}, u32[]{:S(2)}, u32[]{:S(2)}) collective-permute-start(bf16[512,256]{1,0:T(8,128)(2,1)S(1)} %add_convert_fusion.4), channel_id=1, source_target_pairs={{0,8},{4,12},{8,0},{12,4},{16,24},{20,28},{24,16},{28,20},{1,9},{5... | collective-permute-start | bytes 786440 | tf_op jit(solution)/shard_map/ppermute | solution.py:955
  388.5 27.5 %collective-permute-start.32 = (bf16[512,256]{1,0:T(8,128)(2,1)S(1)}, bf16[512,256]{1,0:T(8,128)(2,1)S(1)}, u32[]{:S(2)}, u32[]{:S(2)}) collective-permute-start(bf16[512,256]{1,0:T(8,128)(2,1)S(1)} %add_convert_fusion.4), channel_id=1, source_target_pairs={{0,16},{4,20},{8,24},{12,28},{16,0},{20,4},{24,8},{28,12},{1,17},{... | collective-permute-start | bytes 786440 | tf_op jit(solution)/shard_map/ppermute | solution.py:955
  389.5 27.3 %collective-permute-start.33 = (bf16[512,256]{1,0:T(8,128)(2,1)S(1)}, bf16[512,256]{1,0:T(8,128)(2,1)}, u32[]{:S(2)}, u32[]{:S(2)}) collective-permute-start(bf16[512,256]{1,0:T(8,128)(2,1)S(1)} %add_convert_fusion.4), channel_id=1, source_target_pairs={{0,24},{4,28},{8,16},{12,20},{16,8},{20,12},{24,0},{28,4},{1,25},{... | collective-permute-start | bytes 786440 | tf_op jit(solution)/shard_map/ppermute | solution.py:955
  391.0 30.8 %collective-permute-start.35 = (bf16[128,256]{1,0:T(8,128)(2,1)S(1)}, bf16[128,256]{1,0:T(8,128)(2,1)}, u32[]{:S(2)}, u32[]{:S(2)}) collective-permute-start(bf16[128,256]{1,0:T(8,128)(2,1)S(1)} %add_convert_fusion.6), channel_id=1, source_target_pairs={{0,8},{4,12},{8,0},{12,4},{16,24},{20,28},{24,16},{28,20},{1,9},{5... | collective-permute-start | bytes 196616 | tf_op jit(solution)/shard_map/ppermute | solution.py:955
  420.5 45.8 %collective-permute-start.34 = (bf16[2048,256]{1,0:T(8,128)(2,1)S(1)}, bf16[2048,256]{1,0:T(8,128)(2,1)}, u32[]{:S(2)}, u32[]{:S(2)}) collective-permute-start(bf16[2048,256]{1,0:T(8,128)(2,1)S(1)} %pad_maximum_fusion.3), channel_id=1, source_target_pairs={{0,4},{4,0},{8,12},{12,8},{16,20},{20,16},{24,28},{28,24},{1,5},{5... | collective-permute-start | bytes 3145736 | tf_op jit(solution)/shard_map/ppermute | solution.py:955
  424.8 36.0 %collective-permute-start.38 = (bf16[512,256]{1,0:T(8,128)(2,1)}, bf16[512,256]{1,0:T(8,128)(2,1)}, u32[]{:S(2)}, u32[]{:S(2)}) collective-permute-start(bf16[512,256]{1,0:T(8,128)(2,1)} %pad_maximum_fusion.11), channel_id=1, source_target_pairs={{0,4},{4,0},{8,12},{12,8},{16,20},{20,16},{24,28},{28,24},{1,5},{5... | collective-permute-start | bytes 786440 | tf_op jit(solution)/shard_map/ppermute | solution.py:955
  425.6 44.2 %all-to-all-start.7 = ((f32[32,8,768]{2,1,0:T(8,128)}), f32[32,8,768]{2,1,0:T(8,128)S(1)}, u32[]{:S(2)}, u32[]{:S(2)}) async-start(f32[32,8,768]{2,1,0:T(8,128)} %reshape.100), calls=%async_computation.7 | async-start | bytes 1572864 | tf_op jit(solution)/shard_map/all_to_all | solution.py:959
  431.1 30.7 %collective-permute-start.40 = (bf16[176,256]{1,0:T(8,128)(2,1)S(1)}, bf16[176,256]{1,0:T(8,128)(2,1)S(1)}, u32[]{:S(2)}, u32[]{:S(2)}) collective-permute-start(bf16[176,256]{1,0:T(8,128)(2,1)S(1)} %get-tuple-element.274), channel_id=1, source_target_pairs={{0,8},{4,12},{8,0},{12,4},{16,24},{20,28},{24,16},{28,20},{1,9},{5... | collective-permute-start | bytes 270344 | tf_op jit(solution)/shard_map/ppermute | solution.py:955
  433.0 28.8 %collective-permute-start.41 = (bf16[176,256]{1,0:T(8,128)(2,1)S(1)}, bf16[176,256]{1,0:T(8,128)(2,1)S(1)}, u32[]{:S(2)}, u32[]{:S(2)}) collective-permute-start(bf16[176,256]{1,0:T(8,128)(2,1)S(1)} %get-tuple-element.276), channel_id=1, source_target_pairs={{0,16},{4,20},{8,24},{12,28},{16,0},{20,4},{24,8},{28,12},{1,17},{... | collective-permute-start | bytes 270344 | tf_op jit(solution)/shard_map/ppermute | solution.py:955
  (103 other events, 1087.7 us)

commit v5 on v4

--- a/solution.py
+++ b/solution.py
@@ -225,7 +225,7 @@
             shape_of((EDGE, REST), bf16),
         ],
         compiler_params=cparams(),
-        cost_estimate=cost(2 * length * width * (GW + REST), 9),
+        cost_estimate=cost(4 * length * width * (GW + REST), 9),
         name="project",
     )(order, tokens, edge, gain, *pieces)
 
@@ -244,7 +244,7 @@
         ),
         out_shape=[shape_of((length, GW), bf16), shape_of((EDGE, GW), bf16)],
         compiler_params=cparams(),
-        cost_estimate=cost(2 * length * width * GW, 6),
+        cost_estimate=cost(4 * length * width * GW, 6),
         name="project_more",
     )(order, normed, edge, gain, *pieces)
 
@@ -273,7 +273,7 @@
         ),
         out_shape=shape_of((length, INNER), bf16),
         compiler_params=cparams(),
-        cost_estimate=cost(2 * length * width * INNER, 10),
+        cost_estimate=cost(4 * length * width * INNER, 10),
         name="gate_project",
     )(order, normed, *pieces)
 
@@ -354,7 +354,7 @@
         out_specs=[rows_of(BC), rows_of(128), pl.BlockSpec((HEADS, Q), lambda i: (0, i))],
         out_shape=[shape_of((length, BC)), shape_of((length, 128)), shape_of((HEADS, length))],
         compiler_params=cparams(),
-        cost_estimate=cost(10**9, 4),
+        cost_estimate=cost(5 * 10**9, 4),
         name="factors",
     )(rest, rest, rest_edge, taps_bc, bias_bc, heads)
 
@@ -945,7 +945,7 @@
         ),
         out_shape=[shape_of((length, width)), shape_of((1, width))],
         compiler_params=cparams(),
-        cost_estimate=cost(2 * length * width * (INNER + XCOLS), 26),
+        cost_estimate=cost(4 * length * width * (INNER + XCOLS), 26),
         name="input_back",
     )(order, grad_gate, grad_x0, grad_x1, tokens, cot, gain, *gate_pieces, *a_pieces, *b_pieces)
 

time: 492 us -> 495 us (level)
  transfers between devices with their start and end apart: 55 -> 55, of which waited for: 13 -> 14; matrix products, arithmetic and copies ran while one was open for 14% -> 14% of each run, Pallas kernels for 38% -> 38%
where the time goes in v5:
time: 495 us; the launch traced here: 486 us
  Pallas kernels  221 us (45%)
  starting transfers between devices  101 us (20%)
  waiting for transfers between devices  72.3 us (15%)
  local copies, waits for them, and re-layouts  33.8 us (7%)
  other arithmetic  30.7 us (6%)
  matrix products  24.8 us (5%)
    ppermute x44, starting transfers between devices, swap(): return lax.ppermute(value, axis, [(i, i ^ bit) for i in range(count)])  53.3 us
    ppermute x44, waiting for transfers between devices, swap(): return lax.ppermute(value, axis, [(i, i ^ bit) for i in range(count)])  51.8 us
    pallas_call x2, Pallas kernels, backward(): pl.pallas_call(functools.partial(back_kernel, group), grid=(chunks,), in_...  47.3 us
    all_to_all x8, starting transfers between devices, exchange(): return lax.all_to_all(value, axis, split_axis=0, concat_axis=0, tiled=True)  40.5 us
    pallas_call x2, Pallas kernels, within_back(): pl.pallas_call(functools.partial(within_back_kernel, group), grid=(length...  37.8 us
    pallas_call x1, Pallas kernels, middle(): pl.pallas_call(middle_kernel, grid_spec=pltpu.PrefetchScalarGridSpec(num_...  35.7 us
    dot_general x8, matrix products, dot_rows(): lax.dot_general(a, b, (((0,), (0,)), ((), ())), preferred_element_type=f32)  24.8 us
    pallas_call x2, Pallas kernels, within(): pl.pallas_call(functools.partial(within_kernel, group), grid=(length // Q...  22.8 us
  transfers between devices with their start and end apart: 55, of which 14 were waited for; matrix products, arithmetic and copies ran while one was open for 14% of the time, Pallas kernels for 38%

profile of v5, /device:TPU:0, one launch (start us, length us, event | category | flops | bytes accessed | tf_op | source)
XLA Modules:
  0.0 485.8 jit_solution(7753161289488201967)
XLA Ops:
  6.3 5.8 %all-to-all-start = ((f32[8,8,256]{2,1,0:T(8,128)}), f32[8,8,256]{2,1,0:T(8,128)S(1)}, u32[]{:S(2)}, u32[]{:S(2)}) async-start(f32[8,8,256]{2,1,0:T(8,128)} %broadcast_in_dim.46), calls=%async_computation | async-start | bytes 131072 | tf_op jit(solution)/shard_map/all_to_all | solution.py:959
  30.9 8.7 %project.1 = (bf16[1024,1024]{1,0:T(8,128)(2,1)}, bf16[1024,1024]{1,0:T(8,128)(2,1)}, bf16[1024,384]{1,0:T(8,128)(2,1)}, bf16[16,1024]{1,0:T(8,128)(2,1)}, bf16[16,384]{1,0:T(8,128)(2,1)}) custom-call(s32[4]{0:T(128)} %pad_add_fusion.order, bf16[1024,1024]{1,0:T(8,128)(2,1)} %bitcast.78, bf16[16,1024]{1,0:T(8,128)(2,1)} %copy-done.68, f32[1,1024]{1,0:T(1,128)} %bitcast.87, ...), custom_call_target="tpu_custom_call" | custom-call | flops 5905580032 | bytes 9437184 | tf_op jit(solution)/shard_map/project/pallas_call | solution.py:211
  39.6 5.2 %factors.1 = (f32[1024,256]{1,0:T(8,128)}, f32[1024,128]{1,0:T(8,128)}, f32[32,1024]{1,0:T(8,128)}) custom-call(bf16[1024,384]{1,0:T(8,128)(2,1)} %get-tuple-element.132.now.prior.others_0_.others_1_, bf16[1024,384]{1,0:T(8,128)(2,1)} %get-tuple-element.132.now.prior.others_0_.others_1_, bf16[16,384]{1,0:T(8,128)(2,1)} %get-tuple-element.133.edge.others_2_, ...), custom_call_target="tpu_custom_call" | custom-call | flops 5000000000 | bytes 4194304 | tf_op jit(solution)/shard_map/factors/pallas_call | solution.py:347
  45.0 10.5 %states.2 = (f32[1024,1024]{1,0:T(8,128)}, f32[4,4,128,256]{3,2,1,0:T(8,128)}, f32[8,136,128]{2,1,0:T(8,128)}) custom-call(bf16[1024,1024]{1,0:T(8,128)(2,1)} %get-tuple-element.130.now.prior, bf16[1024,1024]{1,0:T(8,128)(2,1)} %get-tuple-element.130.now.prior, bf16[16,1024]{1,0:T(8,128)(2,1)} %get-tuple-element.131.edge, f32[4,2048]{1,0:T(4,128)} %bitcast.61, ...), custom_call_target="tpu_custom_call" | custom-call | flops 10000000000 | bytes 10485760 | tf_op jit(solution)/shard_map/states/pallas_call | solution.py:365
  55.5 5.8 %all-to-all-start.2 = ((f32[8,136,128]{2,1,0:T(8,128)}), f32[8,136,128]{2,1,0:T(8,128)S(1)}, u32[]{:S(2)}, u32[]{:S(2)}) async-start(f32[8,136,128]{2,1,0:T(8,128)} %get-tuple-element.138), calls=%async_computation.2 | async-start | bytes 1114112 | tf_op jit(solution)/shard_map/all_to_all | solution.py:959
  64.9 7.2 %project_more.1 = (bf16[1024,1024]{1,0:T(8,128)(2,1)}, bf16[16,1024]{1,0:T(8,128)(2,1)}) custom-call(s32[4]{0:T(128)} %pad_add_fusion.order, bf16[1024,1024]{1,0:T(8,128)(2,1)} %get-tuple-element.148.normed, bf16[16,1024]{1,0:T(8,128)(2,1)} %copy-done.68, f32[1,1024]{1,0:T(1,128)} %bitcast.88, bf16[256,1024]{1,0:T(8,128)(2,1)} %copy-done.24, ...), custom_call_target="tpu_custom_call" | custom-call | flops 4294967296 | bytes 6291456 | tf_op jit(solution)/shard_map/project_more/pallas_call | solution.py:236
  72.1 10.6 %states.3 = (f32[1024,1024]{1,0:T(8,128)}, f32[4,4,128,256]{3,2,1,0:T(8,128)}, f32[8,136,128]{2,1,0:T(8,128)}) custom-call(bf16[1024,1024]{1,0:T(8,128)(2,1)} %get-tuple-element.142.now.prior, bf16[1024,1024]{1,0:T(8,128)(2,1)} %get-tuple-element.142.now.prior, bf16[16,1024]{1,0:T(8,128)(2,1)} %get-tuple-element.143.edge, f32[4,2048]{1,0:T(4,128)} %bitcast.62, ...), custom_call_target="tpu_custom_call" | custom-call | flops 10000000000 | bytes 10485760 | tf_op jit(solution)/shard_map/states/pallas_call | solution.py:365
  82.7 6.4 %all-to-all-start.1 = ((f32[8,136,128]{2,1,0:T(8,128)}), f32[8,136,128]{2,1,0:T(8,128)S(1)}, u32[]{:S(2)}, u32[]{:S(2)}) async-start(f32[8,136,128]{2,1,0:T(8,128)} %get-tuple-element.144), calls=%async_computation.1 | async-start | bytes 1114112 | tf_op jit(solution)/shard_map/all_to_all | solution.py:959
  89.0 11.5 %within.2.y_in0 = f32[1024,1024]{1,0:T(8,128)} custom-call(f32[1024,1024]{1,0:T(8,128)} %get-tuple-element.165.x_act, f32[1024,256]{1,0:T(8,128)} %get-tuple-element.134.bc_act, f32[1024,128]{1,0:T(8,128)} %get-tuple-element.135.aux, f32[32,1024]{1,0:T(8,128)} %get-tuple-element.146.cum_t, f32[1,2048]{1,0:T(1,128)} %broadcast_in_dim_reshape.3.skip), custom_call_target="tpu_custom_call" | custom-call | flops 10000000000 | bytes 10485760 | tf_op jit(solution)/shard_map/within/pallas_call | solution.py:471
  101.2 9.6 %gate_project.1.gate = bf16[1024,2048]{1,0:T(8,128)(2,1)} custom-call(s32[4]{0:T(128)} %pad_add_fusion.order, bf16[1024,1024]{1,0:T(8,128)(2,1)} %get-tuple-element.148.normed, bf16[256,2048]{1,0:T(8,128)(2,1)} %copy-done.15, bf16[256,2048]{1,0:T(8,128)(2,1)} %collective-permute-done.7.w1.g1, bf16[256,2048]{1,0:T(8,128)(2,1)} %collective-permute-done.8.w2.g2, ...), custom_call_target="tpu_custom_call" | custom-call | flops 8589934592 | bytes 10485760 | tf_op jit(solution)/shard_map/gate_project/pallas_call | solution.py:265
  112.8 6.0 %all-to-all-start.3 = ((f32[8,128,128]{2,1,0:T(8,128)}), f32[8,128,128]{2,1,0:T(8,128)S(1)}, u32[]{:S(2)}, u32[]{:S(2)}) async-start(f32[8,128,128]{2,1,0:T(8,128)} %chain.3), calls=%async_computation.3 | async-start | bytes 1048576 | tf_op jit(solution)/shard_map/all_to_all | solution.py:959
  124.7 8.7 %all-to-all-done.3.entering0 = f32[8,128,128]{2,1,0:T(8,128)S(1)} async-done(((f32[8,128,128]{2,1,0:T(8,128)}), f32[8,128,128]{2,1,0:T(8,128)S(1)}, u32[]{:S(2)}, u32[]{:S(2)}) %all-to-all-start.3) | async-done | bytes 524320 | tf_op jit(solution)/shard_map/all_to_all | solution.py:959
  137.0 11.3 %within.3.y_in1 = f32[1024,1024]{1,0:T(8,128)} custom-call(f32[1024,1024]{1,0:T(8,128)} %get-tuple-element.178.x_act, f32[1024,256]{1,0:T(8,128)} %get-tuple-element.134.bc_act, f32[1024,128]{1,0:T(8,128)} %get-tuple-element.135.aux, f32[32,1024]{1,0:T(8,128)} %get-tuple-element.146.cum_t, f32[1,2048]{1,0:T(1,128)} %broadcast_in_dim_reshape.3.skip), custom_call_target="tpu_custom_call" | custom-call | flops 10000000000 | bytes 10485760 | tf_op jit(solution)/shard_map/within/pallas_call | solution.py:471
  152.8 35.7 %middle.1 = (bf16[1024,2048]{1,0:T(8,128)(2,1)}, bf16[1024,1024]{1,0:T(8,128)(2,1)}, bf16[1024,2048]{1,0:T(8,128)(2,1)}, bf16[1024,2048]{1,0:T(8,128)(2,1)}, f32...) custom-call(s32[4]{0:T(128)} %pad_add_fusion.order, ...), custom_call_target="tpu_custom_call" | custom-call | flops 40000000000 | bytes 41943040 | tf_op jit(solution)/shard_map/middle/pallas_call | solution.py:697
  210.7 18.8 %within_back.2 = (bf16[1024,1024]{1,0:T(8,128)(2,1)}, bf16[1024,1024]{1,0:T(8,128)(2,1)}, f32[1024,256]{1,0:T(8,128)}, f32[1024,128]{1,0:T(8,128)}) custom-call(f32[1024,1024]{1,0:T(8,128)} %get-tuple-element.165.x_act, f32[1024,256]{1,0:T(8,128)} %get-tuple-element.134.bc_act, f32[1024,128]{1,0:T(8,128)} %get-tuple-element.135.aux, ...), custom_call_target="tpu_custom_call" | custom-call | flops 20000000000 | bytes 14680064 | tf_op jit(solution)/shard_map/within_back/pallas_call | solution.py:571
  246.8 19.1 %within_back.3 = (bf16[1024,1024]{1,0:T(8,128)(2,1)}, bf16[1024,1024]{1,0:T(8,128)(2,1)}, f32[1024,256]{1,0:T(8,128)}, f32[1024,128]{1,0:T(8,128)}) custom-call(f32[1024,1024]{1,0:T(8,128)} %get-tuple-element.178.x_act, f32[1024,256]{1,0:T(8,128)} %get-tuple-element.134.bc_act, f32[1024,128]{1,0:T(8,128)} %get-tuple-element.135.aux, ...), custom_call_target="tpu_custom_call" | custom-call | flops 20000000000 | bytes 14680064 | tf_op jit(solution)/shard_map/within_back/pallas_call | solution.py:571
  265.9 5.2 %collective-permute-done.15 = bf16[512,1024]{1,0:T(8,128)(2,1)S(1)} collective-permute-done((bf16[512,1024]{1,0:T(8,128)(2,1)}, bf16[512,1024]{1,0:T(8,128)(2,1)S(1)}, u32[]{:S(2)}, u32[]{:S(2)}) %collective-permute-start.15) | collective-permute-done | bytes 1048608 | tf_op jit(solution)/shard_map/ppermute | solution.py:955
  279.4 20.9 %backward.2 = (bf16[1024,1024]{1,0:T(8,128)(2,1)}, f32[8,1024]{1,0:T(8,128)}, f32[16,1024]{1,0:T(8,128)}, f32[8,1024]{1,0:T(8,128)}, f32[1024,128]{1,0:T(8,128)}...) custom-call(bf16[1024,1024]{1,0:T(8,128)(2,1)} %get-tuple-element.130.now.prior, bf16[16,1024]{1,0:T(8,128)(2,1)} %get-tuple-element.131.edge, ...), custom_call_target="tpu_custom_call" | custom-call | flops 20000000000 | bytes 20971520 | tf_op jit(solution)/shard_map/backward/pallas_call | solution.py:878
  318.2 26.4 %backward.3 = (bf16[1024,1408]{1,0:T(8,128)(2,1)}, f32[8,1024]{1,0:T(8,128)}, f32[16,1280]{1,0:T(8,128)}, f32[8,1280]{1,0:T(8,128)}, f32[8,256]{1,0:T(8,128)}, /*index=5*/f32[8,128]{1,0:T(8,128)}) custom-call(bf16[1024,1024]{1,0:T(8,128)(2,1)} %get-tuple-element.142.now.prior, bf16[16,1024]{1,0:T(8,128)(2,1)} %get-tuple-element.143.edge, ...), custom_call_target="tpu_custom_call" | custom-call | flops 20000000000 | bytes 20971520 | tf_op jit(solution)/shard_map/backward/pallas_call | solution.py:878
  374.6 8.0 %collective-permute-done.27 = bf16[512,256]{1,0:T(8,128)(2,1)S(1)} collective-permute-done((bf16[512,256]{1,0:T(8,128)(2,1)S(1)}, bf16[512,256]{1,0:T(8,128)(2,1)S(1)}, u32[]{:S(2)}, u32[]{:S(2)}) %collective-permute-start.27) | collective-permute-done | bytes 262176 | tf_op jit(solution)/shard_map/ppermute | solution.py:955
  382.8 8.4 %collective-permute-start.31 = (bf16[512,256]{1,0:T(8,128)(2,1)S(1)}, bf16[512,256]{1,0:T(8,128)(2,1)S(1)}, u32[]{:S(2)}, u32[]{:S(2)}) collective-permute-start(bf16[512,256]{1,0:T(8,128)(2,1)S(1)} %add_convert_fusion.4), channel_id=1, source_target_pairs={{0,8},{4,12},{8,0},{12,4},{16,24},{20,28},{24,16},{28,20},{1,9},{5... | collective-permute-start | bytes 786440 | tf_op jit(solution)/shard_map/ppermute | solution.py:955
  395.4 19.1 %input_back.1 = (f32[1024,1024]{1,0:T(8,128)}, f32[1,1024]{1,0:T(1,128)}) custom-call(s32[4]{0:T(128)} %pad_add_fusion.order, bf16[1024,2048]{1,0:T(8,128)(2,1)} %get-tuple-element.220.grad_gate, bf16[1024,1024]{1,0:T(8,128)(2,1)} %copy-done.62, bf16[1024,1408]{1,0:T(8,128)(2,1)} %copy-done.59, bf16[1024,1024]{1,0:T(8,128)(2,1)} %bitcast.80, ...), custom_call_target="tpu_custom_call" | custom-call | flops 18790481920 | bytes 27262976 | tf_op jit(solution)/shard_map/input_back/pallas_call | solution.py:935
  438.4 25.1 %collective-permute-done.38 = bf16[512,256]{1,0:T(8,128)(2,1)} collective-permute-done((bf16[512,256]{1,0:T(8,128)(2,1)}, bf16[512,256]{1,0:T(8,128)(2,1)}, u32[]{:S(2)}, u32[]{:S(2)}) %collective-permute-start.38) | collective-permute-done | bytes 262176 | tf_op jit(solution)/shard_map/ppermute | solution.py:955
  477.4 5.4 %collective-permute-done.46 = bf16[704,256]{1,0:T(8,128)(2,1)S(1)} collective-permute-done((bf16[704,256]{1,0:T(8,128)(2,1)S(1)}, bf16[704,256]{1,0:T(8,128)(2,1)S(1)}, u32[]{:S(2)}, u32[]{:S(2)}) %collective-permute-start.46) | collective-permute-done | bytes 360480 | tf_op jit(solution)/shard_map/ppermute | solution.py:955
  (349 shorter events, 184.1 us)
Async XLA Ops:
  28.6 35.5 %collective-permute-start.4 = (bf16[256,1024]{1,0:T(8,128)(2,1)S(1)}, bf16[256,1024]{1,0:T(8,128)(2,1)S(1)}, u32[]{:S(2)}, u32[]{:S(2)}) collective-permute-start(bf16[256,1024]{1,0:T(8,128)(2,1)S(1)} %copy.64.w0.b0), channel_id=1, source_target_pairs={{0,1},{1,0},{2,3},{3,2},{4,5},{5,4},{6,7},{7,6},{8,9},{9,8},{10,11... | collective-permute-start | bytes 1572872 | tf_op jit(solution)/shard_map/ppermute | solution.py:955
  28.8 35.3 %collective-permute-start.8 = (bf16[256,2048]{1,0:T(8,128)(2,1)S(1)}, bf16[256,2048]{1,0:T(8,128)(2,1)}, u32[]{:S(2)}, u32[]{:S(2)}) collective-permute-start(bf16[256,2048]{1,0:T(8,128)(2,1)S(1)} %copy.65.w0.g0), channel_id=1, source_target_pairs={{0,2},{1,3},{2,0},{3,1},{4,6},{5,7},{6,4},{7,5},{8,10},{9,11},{10,... | collective-permute-start | bytes 3145736 | tf_op jit(solution)/shard_map/ppermute | solution.py:955
  29.1 72.0 %collective-permute-start.7 = (bf16[256,2048]{1,0:T(8,128)(2,1)S(1)}, bf16[256,2048]{1,0:T(8,128)(2,1)}, u32[]{:S(2)}, u32[]{:S(2)}) collective-permute-start(bf16[256,2048]{1,0:T(8,128)(2,1)S(1)} %copy.65.w0.g0), channel_id=1, source_target_pairs={{0,1},{1,0},{2,3},{3,2},{4,5},{5,4},{6,7},{7,6},{8,9},{9,8},{10,11... | collective-permute-start | bytes 3145736 | tf_op jit(solution)/shard_map/ppermute | solution.py:955
  29.1 91.2 %collective-permute-start.11 = (bf16[512,1024]{1,0:T(8,128)(2,1)}, bf16[512,1024]{1,0:T(8,128)(2,1)}, u32[]{:S(2)}, u32[]{:S(2)}) collective-permute-start(bf16[512,1024]{1,0:T(8,128)(2,1)} %w0), channel_id=1, source_target_pairs={{0,2},{1,3},{2,0},{3,1},{4,6},{5,7},{6,4},{7,5},{8,10},{9,11},{10,... | collective-permute-start | bytes 3145736 | tf_op jit(solution)/shard_map/ppermute | solution.py:955
  64.1 37.0 %collective-permute-start.9 = (bf16[256,2048]{1,0:T(8,128)(2,1)}, bf16[256,2048]{1,0:T(8,128)(2,1)}, u32[]{:S(2)}, u32[]{:S(2)}) collective-permute-start(bf16[256,2048]{1,0:T(8,128)(2,1)} %collective-permute-done.8.w2.g2), channel_id=1, source_target_pairs={{0,1},{1,0},{2,3},{3,2},{4,5},{5,4},{6,7},{7,6},{8,9},{9,8},{10,11... | collective-permute-start | bytes 3145736 | tf_op jit(solution)/shard_map/ppermute | solution.py:955
  82.7 30.1 %all-to-all-start.1 = ((f32[8,136,128]{2,1,0:T(8,128)}), f32[8,136,128]{2,1,0:T(8,128)S(1)}, u32[]{:S(2)}, u32[]{:S(2)}) async-start(f32[8,136,128]{2,1,0:T(8,128)} %get-tuple-element.144), calls=%async_computation.1 | async-start | bytes 1114112 | tf_op jit(solution)/shard_map/all_to_all | solution.py:959
  118.8 32.9 %collective-permute-start.10 = (bf16[512,1024]{1,0:T(8,128)(2,1)}, bf16[512,1024]{1,0:T(8,128)(2,1)}, u32[]{:S(2)}, u32[]{:S(2)}) collective-permute-start(bf16[512,1024]{1,0:T(8,128)(2,1)} %w0), channel_id=1, source_target_pairs={{0,1},{1,0},{2,3},{3,2},{4,5},{5,4},{6,7},{7,6},{8,9},{9,8},{10,11... | collective-permute-start | bytes 3145736 | tf_op jit(solution)/shard_map/ppermute | solution.py:955
  120.3 31.4 %collective-permute-start.12 = (bf16[512,1024]{1,0:T(8,128)(2,1)}, bf16[512,1024]{1,0:T(8,128)(2,1)S(1)}, u32[]{:S(2)}, u32[]{:S(2)}) collective-permute-start(bf16[512,1024]{1,0:T(8,128)(2,1)} %collective-permute-done.11.w2), channel_id=1, source_target_pairs={{0,1},{1,0},{2,3},{3,2},{4,5},{5,4},{6,7},{7,6},{8,9},{9,8},{10,11... | collective-permute-start | bytes 3145736 | tf_op jit(solution)/shard_map/ppermute | solution.py:955
  195.2 34.3 %collective-permute-start.14 = (bf16[1024,1024]{1,0:T(8,128)(2,1)}, bf16[1024,1024]{1,0:T(8,128)(2,1)S(1)}, u32[]{:S(2)}, u32[]{:S(2)}) collective-permute-start(bf16[1024,1024]{1,0:T(8,128)(2,1)} %fusion.12), channel_id=1, source_target_pairs={{0,1},{1,0},{2,3},{3,2},{4,5},{5,4},{6,7},{7,6},{8,9},{9,8},{10,11... | collective-permute-start | bytes 6291464 | tf_op jit(solution)/shard_map/ppermute | solution.py:955
  202.7 29.5 %collective-permute-start.13 = (bf16[2048,512]{1,0:T(8,128)(2,1)}, bf16[2048,512]{1,0:T(8,128)(2,1)}, u32[]{:S(2)}, u32[]{:S(2)}) collective-permute-start(bf16[2048,512]{1,0:T(8,128)(2,1)} %convolution_convert_fusion.1), channel_id=1, source_target_pairs={{0,1},{1,0},{2,3},{3,2},{4,5},{5,4},{6,7},{7,6},{8,9},{9,8},{10,11... | collective-permute-start | bytes 6291464 | tf_op jit(solution)/shard_map/ppermute | solution.py:955
  206.9 29.9 %all-to-all-start.5 = ((f32[8,128,256]{2,1,0:T(8,128)}), f32[8,128,256]{2,1,0:T(8,128)S(1)}, u32[]{:S(2)}, u32[]{:S(2)}) async-start(f32[8,128,256]{2,1,0:T(8,128)} %get-tuple-element.171), calls=%async_computation.5 | async-start | bytes 2097152 | tf_op jit(solution)/shard_map/all_to_all | solution.py:959
  240.0 39.4 %all-to-all-start.6 = ((f32[8,128,256]{2,1,0:T(8,128)}), f32[8,128,256]{2,1,0:T(8,128)}, u32[]{:S(2)}, u32[]{:S(2)}) async-start(f32[8,128,256]{2,1,0:T(8,128)} %chain.5), calls=%async_computation.6 | async-start | bytes 2097152 | tf_op jit(solution)/shard_map/all_to_all | solution.py:959
  246.3 55.7 %collective-permute-start.16 = (bf16[2048,256]{1,0:T(8,128)(2,1)}, bf16[2048,256]{1,0:T(8,128)(2,1)S(1)}, u32[]{:S(2)}, u32[]{:S(2)}) collective-permute-start(bf16[2048,256]{1,0:T(8,128)(2,1)} %get-tuple-element.247), channel_id=1, source_target_pairs={{0,2},{1,3},{2,0},{3,1},{4,6},{5,7},{6,4},{7,5},{8,10},{9,11},{10,... | collective-permute-start | bytes 3145736 | tf_op jit(solution)/shard_map/ppermute | solution.py:955
  310.9 37.6 %collective-permute-start.21 = (bf16[2048,256]{1,0:T(8,128)(2,1)S(1)}, bf16[2048,256]{1,0:T(8,128)(2,1)}, u32[]{:S(2)}, u32[]{:S(2)}) collective-permute-start(bf16[2048,256]{1,0:T(8,128)(2,1)S(1)} %select_convert_fusion), channel_id=1, source_target_pairs={{0,4},{4,0},{8,12},{12,8},{16,20},{20,16},{24,28},{28,24},{1,5},{5... | collective-permute-start | bytes 3145736 | tf_op jit(solution)/shard_map/ppermute | solution.py:955
  316.6 29.0 %collective-permute-start.19 = (bf16[1024,256]{1,0:T(8,128)(2,1)S(1)}, bf16[1024,256]{1,0:T(8,128)(2,1)S(1)}, u32[]{:S(2)}, u32[]{:S(2)}) collective-permute-start(bf16[1024,256]{1,0:T(8,128)(2,1)S(1)} %get-tuple-element.262), channel_id=1, source_target_pairs={{0,2},{1,3},{2,0},{3,1},{4,6},{5,7},{6,4},{7,5},{8,10},{9,11},{10,... | collective-permute-start | bytes 1572872 | tf_op jit(solution)/shard_map/ppermute | solution.py:955
  382.8 34.4 %collective-permute-start.31 = (bf16[512,256]{1,0:T(8,128)(2,1)S(1)}, bf16[512,256]{1,0:T(8,128)(2,1)S(1)}, u32[]{:S(2)}, u32[]{:S(2)}) collective-permute-start(bf16[512,256]{1,0:T(8,128)(2,1)S(1)} %add_convert_fusion.4), channel_id=1, source_target_pairs={{0,8},{4,12},{8,0},{12,4},{16,24},{20,28},{24,16},{28,20},{1,9},{5... | collective-permute-start | bytes 786440 | tf_op jit(solution)/shard_map/ppermute | solution.py:955
  391.3 27.5 %collective-permute-start.32 = (bf16[512,256]{1,0:T(8,128)(2,1)S(1)}, bf16[512,256]{1,0:T(8,128)(2,1)S(1)}, u32[]{:S(2)}, u32[]{:S(2)}) collective-permute-start(bf16[512,256]{1,0:T(8,128)(2,1)S(1)} %add_convert_fusion.4), channel_id=1, source_target_pairs={{0,16},{4,20},{8,24},{12,28},{16,0},{20,4},{24,8},{28,12},{1,17},{... | collective-permute-start | bytes 786440 | tf_op jit(solution)/shard_map/ppermute | solution.py:955
  392.2 27.3 %collective-permute-start.33 = (bf16[512,256]{1,0:T(8,128)(2,1)S(1)}, bf16[512,256]{1,0:T(8,128)(2,1)}, u32[]{:S(2)}, u32[]{:S(2)}) collective-permute-start(bf16[512,256]{1,0:T(8,128)(2,1)S(1)} %add_convert_fusion.4), channel_id=1, source_target_pairs={{0,24},{4,28},{8,16},{12,20},{16,8},{20,12},{24,0},{28,4},{1,25},{... | collective-permute-start | bytes 786440 | tf_op jit(solution)/shard_map/ppermute | solution.py:955
  393.8 30.8 %collective-permute-start.35 = (bf16[128,256]{1,0:T(8,128)(2,1)S(1)}, bf16[128,256]{1,0:T(8,128)(2,1)}, u32[]{:S(2)}, u32[]{:S(2)}) collective-permute-start(bf16[128,256]{1,0:T(8,128)(2,1)S(1)} %add_convert_fusion.6), channel_id=1, source_target_pairs={{0,8},{4,12},{8,0},{12,4},{16,24},{20,28},{24,16},{28,20},{1,9},{5... | collective-permute-start | bytes 196616 | tf_op jit(solution)/shard_map/ppermute | solution.py:955
  423.3 45.8 %collective-permute-start.34 = (bf16[2048,256]{1,0:T(8,128)(2,1)S(1)}, bf16[2048,256]{1,0:T(8,128)(2,1)}, u32[]{:S(2)}, u32[]{:S(2)}) collective-permute-start(bf16[2048,256]{1,0:T(8,128)(2,1)S(1)} %pad_maximum_fusion.3), channel_id=1, source_target_pairs={{0,4},{4,0},{8,12},{12,8},{16,20},{20,16},{24,28},{28,24},{1,5},{5... | collective-permute-start | bytes 3145736 | tf_op jit(solution)/shard_map/ppermute | solution.py:955
  427.5 36.0 %collective-permute-start.38 = (bf16[512,256]{1,0:T(8,128)(2,1)}, bf16[512,256]{1,0:T(8,128)(2,1)}, u32[]{:S(2)}, u32[]{:S(2)}) collective-permute-start(bf16[512,256]{1,0:T(8,128)(2,1)} %pad_maximum_fusion.11), channel_id=1, source_target_pairs={{0,4},{4,0},{8,12},{12,8},{16,20},{20,16},{24,28},{28,24},{1,5},{5... | collective-permute-start | bytes 786440 | tf_op jit(solution)/shard_map/ppermute | solution.py:955
  428.4 44.2 %all-to-all-start.7 = ((f32[32,8,768]{2,1,0:T(8,128)}), f32[32,8,768]{2,1,0:T(8,128)S(1)}, u32[]{:S(2)}, u32[]{:S(2)}) async-start(f32[32,8,768]{2,1,0:T(8,128)} %reshape.100), calls=%async_computation.7 | async-start | bytes 1572864 | tf_op jit(solution)/shard_map/all_to_all | solution.py:959
  433.9 30.7 %collective-permute-start.40 = (bf16[176,256]{1,0:T(8,128)(2,1)S(1)}, bf16[176,256]{1,0:T(8,128)(2,1)S(1)}, u32[]{:S(2)}, u32[]{:S(2)}) collective-permute-start(bf16[176,256]{1,0:T(8,128)(2,1)S(1)} %get-tuple-element.274), channel_id=1, source_target_pairs={{0,8},{4,12},{8,0},{12,4},{16,24},{20,28},{24,16},{28,20},{1,9},{5... | collective-permute-start | bytes 270344 | tf_op jit(solution)/shard_map/ppermute | solution.py:955
  435.8 28.8 %collective-permute-start.41 = (bf16[176,256]{1,0:T(8,128)(2,1)S(1)}, bf16[176,256]{1,0:T(8,128)(2,1)S(1)}, u32[]{:S(2)}, u32[]{:S(2)}) collective-permute-start(bf16[176,256]{1,0:T(8,128)(2,1)S(1)} %get-tuple-element.276), channel_id=1, source_target_pairs={{0,16},{4,20},{8,24},{12,28},{16,0},{20,4},{24,8},{28,12},{1,17},{... | collective-permute-start | bytes 270344 | tf_op jit(solution)/shard_map/ppermute | solution.py:955
  (103 other events, 1090.3 us)
